TPU v7x, 32 devices: a whole 2x2x4 slice. The times are simulated.
32 devices in a mesh: clips: 2 (over y), tm: 4 (over z), rows: 2 (over x), cols: 2 (over core).
Axes of the slice: x: 2, y: 2, z: 4, core: 2. Of those that a mesh axis runs over, the one named last changes fastest.
Arguments:
- latent: bfloat16 [16, 4, 64, 384], P(('clips', 'tm'), 'rows', 'cols'), parts along dimension 0, may hold values from -400 to 400, as said below
- norm_gain: float32 [384], replicated, may hold values from 0.1 to 1.9
- time_weight: bfloat16 [3, 384, 768], replicated, may hold values from -0.1875 to 0.1875
- time_bias: float32 [768], replicated, may hold values from -3 to 3
- space_weight: bfloat16 [3, 3, 384, 192], replicated, may hold values from -0.109375 to 0.109375
- space_bias: float32 [192], replicated, may hold values from -3 to 3
Outputs:
- decoded: bfloat16 [32, 8, 128, 192], P(('clips', 'tm'), 'rows', 'cols'), parts along dimension 0
There are 2 independent parts, one for each index of `clips`. A program takes and returns all parts, laid end to end along the dimension named above; an argument that names none is the same for every part. Nothing has to cross between parts.
Inputs may be any that keep to these rules, and one draw needn't show every extreme that they name: `latent`: real-valued activations.
All inputs are finite; a program needn't handle non-finite values.
Results may differ from a plain program's by a relative error of at most 0.0051.
Values may be sent and summed in bfloat16 or wider, within the bound.
No kernel may reach another device: no remote copies, remote signals or barrier semaphores. Data moves between devices by JAX's collectives and lax.ppermute only.
A program may use at most 64 MiB of HBM per device.

v0:
```python
import jax
import jax.numpy as jnp
from jax import lax
from jax.sharding import PartitionSpec as P


def passed_along(block, axis, distance):
    devices = range(lax.axis_size(axis))
    route = [(i - distance, i) for i in devices if i - distance in devices]
    return lax.ppermute(block, axis, route)


def with_halo(cells, sides, width):
    for axis, dim in sides:
        count = lax.axis_size(axis)
        ends = count - 1
        head = lax.slice_in_dim(cells, 0, width, axis=dim)
        tail = lax.slice_in_dim(cells, cells.shape[dim] - width, cells.shape[dim], axis=dim)
        cells = jnp.concatenate(
            [
                lax.ppermute(tail, axis, [(i, (i + 1) % count) for i in range(ends)]),
                cells,
                lax.ppermute(head, axis, [((i + 1) % count, i) for i in range(ends)]),
            ],
            axis=dim,
        )
    return cells


def pre_activate(latent, norm_gain):
    values = latent.astype(jnp.float32)
    mean_square = jnp.mean(values * values, axis=-1, keepdims=True)
    scaled = values * lax.rsqrt(mean_square + 1e-06) * norm_gain
    return jax.nn.silu(scaled).astype(jnp.bfloat16)


def time_conv(extended, time_weight, time_bias):
    frames = extended.shape[0] - 2
    height_in = extended.shape[1]
    width_in = extended.shape[2]
    channels = extended.shape[3]
    summed = jnp.zeros((frames * height_in * width_in, time_weight.shape[2]), jnp.float32)
    for offset in range(3):
        window = extended[offset : offset + frames].reshape(-1, channels)
        summed = summed + jnp.dot(window, time_weight[offset], preferred_element_type=jnp.float32)
    summed = summed + time_bias
    return summed.astype(jnp.bfloat16).reshape(frames, height_in, width_in, time_weight.shape[2])


def split_frames(stacked):
    frames, height_in, width_in, doubled = stacked.shape
    channels = doubled // 2
    parted = stacked.reshape(frames, height_in, width_in, 2, channels)
    return jnp.moveaxis(parted, 3, 1).reshape(2 * frames, height_in, width_in, channels)


def space_conv(margined, space_weight, space_bias):
    enlarged = jnp.repeat(jnp.repeat(margined, 2, axis=1), 2, axis=2)[:, 1:-1, 1:-1]
    frames = enlarged.shape[0]
    out_rows = enlarged.shape[1] - 2
    out_cols = enlarged.shape[2] - 2
    channels = enlarged.shape[3]
    summed = jnp.zeros((frames * out_rows * out_cols, space_weight.shape[3]), jnp.float32)
    for row_tap in range(3):
        patches = jnp.concatenate(
            [
                enlarged[:, row_tap : row_tap + out_rows, col_tap : col_tap + out_cols]
                for col_tap in range(3)
            ],
            axis=-1,
        )
        summed = summed + jnp.dot(
            patches.reshape(-1, 3 * channels),
            space_weight[row_tap].reshape(3 * channels, -1),
            preferred_element_type=jnp.float32,
        )
    summed = summed + space_bias
    return summed.astype(jnp.bfloat16).reshape(frames, out_rows, out_cols, space_weight.shape[3])


def local(latent, norm_gain, time_weight, time_bias, space_weight, space_bias):
    activated = pre_activate(latent, norm_gain)
    cached = passed_along(activated, "tm", 1)
    extended = jnp.concatenate([cached, activated], axis=0)
    stacked = time_conv(extended, time_weight, time_bias)
    margined = with_halo(split_frames(stacked), (("rows", 1), ("cols", 2)), 1)
    return space_conv(margined, space_weight, space_bias)


def solution(mesh):
    in_specs = (P(("clips", "tm"), "rows", "cols", None), P(), P(), P(), P(), P())
    out_specs = P(("clips", "tm"), "rows", "cols", None)
    return jax.shard_map(local, mesh=mesh, in_specs=in_specs, out_specs=out_specs, check_vma=False)
```

profile of v0, /device:TPU:0, one launch (start us, length us, event | category | flops | bytes accessed | tf_op | source)
XLA Modules:
  0.0 40.4 jit_solution(18434042265576714465)
XLA Ops:
  0.0 0.0 copy-start.1
  0.0 1.0 %fusion.13 = f32[2,2,32]{2,1,0:T(2,128)S(1)} fusion(bf16[2,2,32,384]{3,2,1,0:T(8,128)(2,1)} %param.6), kind=kLoop, calls=%fused_computation.22 | loop fusion | flops 147328 | bytes 98816 | tf_op jit(solution)/shard_map/reduce_sum | solution.py:32
  1.0 1.0 %fusion.20 = bf16[2,2,32,384]{3,2,1,0:T(8,128)(2,1)S(1)} fusion(bf16[2,2,32,384]{3,2,1,0:T(8,128)(2,1)} %param.6, f32[384]{0:T(512)} %param.7, f32[2,2,32]{2,1,0:T(2,128)S(1)} %add_rsqrt_fusion), kind=kLoop, calls=%fused_computation.29 | loop fusion | flops 393216 | bytes 198656 | tf_op jit(solution)/shard_map/convert_element_type | solution.py:34
  2.1 4.9 %collective-permute-start = (bf16[2,2,32,384]{3,2,1,0:T(8,128)(2,1)S(1)}, bf16[2,2,32,384]{3,2,1,0:T(8,128)(2,1)S(1)}, u32[]{:S(2)}, u32[]{:S(2)}) collective-permute-start(bf16[2,2,32,384]{3,2,1,0:T(8,128)(2,1)S(1)} %fusion.20), channel_id=1, source_target_pairs={{0,4},{4,8},{8,12},{1,5},{5,9},{9,13},{2,6},{6,10},{10,14},{3,7},{... | collective-permute-start | bytes 294920 | tf_op jit(solution)/shard_map/ppermute | solution.py:10
  7.0 1.3 %fusion.5 = f32[128,768]{1,0:T(8,128)S(1)} fusion(bf16[128,384]{1,0:T(8,128)(2,1)S(1)} %bitcast.59, bf16[3,384,768]{2,1,0:T(8,128)(2,1)} %param.8), kind=kOutput, calls=%fused_computation.11 | convolution fusion | flops 75497472 | bytes 1081344 | tf_op jit(solution)/shard_map/dot_general | solution.py:45
  8.3 0.0 copy-start
  8.3 0.8 %collective-permute-done = bf16[2,2,32,384]{3,2,1,0:T(8,128)(2,1)S(1)} collective-permute-done((bf16[2,2,32,384]{3,2,1,0:T(8,128)(2,1)S(1)}, bf16[2,2,32,384]{3,2,1,0:T(8,128)(2,1)S(1)}, u32[]{:S(2)}, u32[]{:S(2)}) %collective-permute-start) | collective-permute-done | bytes 98336 | tf_op jit(solution)/shard_map/ppermute | solution.py:10
  9.2 1.3 %fusion.7 = f32[128,768]{1,0:T(8,128)S(1)} fusion(bf16[128,384]{1,0:T(8,128)(2,1)S(1)} %bitcast.61, bf16[3,384,768]{2,1,0:T(8,128)(2,1)} %param.8), kind=kOutput, calls=%fused_computation.13 | convolution fusion | flops 75497472 | bytes 1081344 | tf_op jit(solution)/shard_map/dot_general | solution.py:45
  10.5 0.0 copy-done.1
  10.5 1.3 %fusion.4 = bf16[128,768]{1,0:T(8,128)(2,1)S(1)} fusion(f32[128,768]{1,0:T(8,128)S(1)} %fusion.5, f32[128,768]{1,0:T(8,128)S(1)} %fusion.7, bf16[128,384]{1,0:T(8,128)(2,1)S(1)} %bitcast.60, bf16[3,384,768]{2,1,0:T(8,128)(2,1)} %param.8, f32[768]{0:T(1024)S(1)} %copy-done.1), kind=kOutput, calls=%fused_computation.10 | convolution fusion | flops 75890688 | bytes 1674240 | tf_op jit(solution)/shard_map/dot_general | solution.py:45
  11.9 0.1 reshape_reshape.3
  12.0 3.4 %collective-permute-start.1 = (bf16[4,1,32,384]{3,2,1,0:T(8,128)(2,1)S(1)}, bf16[4,1,32,384]{3,2,1,0:T(8,128)(2,1)S(1)}, u32[]{:S(2)}, u32[]{:S(2)}) collective-permute-start(bf16[4,1,32,384]{3,2,1,0:T(8,128)(2,1)S(1)} %get-tuple-element.19), channel_id=1, source_target_pairs={{0,2},{1,3},{4,6},{5,7},{8,10},{9,11},{12,14},{13,15},{16,18},{17,... | collective-permute-start | bytes 294920 | tf_op jit(solution)/shard_map/ppermute | solution.py:21
  15.4 1.3 %collective-permute-start.2 = (bf16[4,1,32,384]{3,2,1,0:T(8,128)(2,1)S(1)}, bf16[4,1,32,384]{3,2,1,0:T(8,128)(2,1)S(1)}, u32[]{:S(2)}, u32[]{:S(2)}) collective-permute-start(bf16[4,1,32,384]{3,2,1,0:T(8,128)(2,1)S(1)} %get-tuple-element.20), channel_id=1, source_target_pairs={{2,0},{3,1},{6,4},{7,5},{10,8},{11,9},{14,12},{15,13},{18,16},{19,... | collective-permute-start | bytes 294920 | tf_op jit(solution)/shard_map/ppermute | solution.py:23
  16.7 0.9 %collective-permute-done.1 = bf16[4,1,32,384]{3,2,1,0:T(8,128)(2,1)S(1)} collective-permute-done((bf16[4,1,32,384]{3,2,1,0:T(8,128)(2,1)S(1)}, bf16[4,1,32,384]{3,2,1,0:T(8,128)(2,1)S(1)}, u32[]{:S(2)}, u32[]{:S(2)}) %collective-permute-start.1) | collective-permute-done | bytes 98336 | tf_op jit(solution)/shard_map/ppermute | solution.py:21
  17.6 4.3 %collective-permute-done.2 = bf16[4,1,32,384]{3,2,1,0:T(8,128)(2,1)S(1)} collective-permute-done((bf16[4,1,32,384]{3,2,1,0:T(8,128)(2,1)S(1)}, bf16[4,1,32,384]{3,2,1,0:T(8,128)(2,1)S(1)}, u32[]{:S(2)}, u32[]{:S(2)}) %collective-permute-start.2) | collective-permute-done | bytes 98336 | tf_op jit(solution)/shard_map/ppermute | solution.py:23
  22.0 1.3 %collective-permute-start.3 = (bf16[4,4,1,384]{3,2,1,0:T(2,128)(2,1)S(1)}, bf16[4,4,1,384]{3,2,1,0:T(2,128)(2,1)S(1)}, u32[]{:S(2)}, u32[]{:S(2)}) collective-permute-start(bf16[4,4,1,384]{3,2,1,0:T(2,128)(2,1)S(1)} %get-tuple-element.17), channel_id=1, source_target_pairs={{0,1},{2,3},{4,5},{6,7},{8,9},{10,11},{12,13},{14,15},{16,17},{18,... | collective-permute-start | bytes 36872 | tf_op jit(solution)/shard_map/ppermute | solution.py:21
  23.3 1.3 %collective-permute-start.4 = (bf16[4,4,1,384]{3,2,1,0:T(2,128)(2,1)S(1)}, bf16[4,4,1,384]{3,2,1,0:T(2,128)(2,1)S(1)}, u32[]{:S(2)}, u32[]{:S(2)}) collective-permute-start(bf16[4,4,1,384]{3,2,1,0:T(2,128)(2,1)S(1)} %get-tuple-element.18), channel_id=1, source_target_pairs={{1,0},{3,2},{5,4},{7,6},{9,8},{11,10},{13,12},{15,14},{17,16},{19,... | collective-permute-start | bytes 36872 | tf_op jit(solution)/shard_map/ppermute | solution.py:23
  24.6 0.0 copy-done
  24.6 0.1 fusion.22
  24.7 0.4 copy.17
  25.1 0.1 copy.23
  25.2 0.4 copy.19
  25.6 0.1 copy.24
  25.6 0.4 copy.21
  26.0 0.1 copy.25
  26.1 0.0 collective-permute-done.3
  26.1 0.3 collective-permute-done.4
  26.4 0.2 pad_maximum_fusion.3
  26.6 0.2 copy.15
  26.8 0.6 %broadcast_in_dim.4 = bf16[4,4,2,34,384]{4,2,1,3,0:T(2,128)(2,1)S(1)} broadcast(bf16[4,4,34,384]{3,1,2,0:T(4,128)(2,1)S(1)} %copy.15), dimensions={0,1,3,4} | broadcast | bytes 1253376 | tf_op jit(solution)/shard_map/broadcast_in_dim | solution.py:58
  27.3 0.3 reshape.45
  27.7 0.1 broadcast_in_dim.5
  27.8 4.3 %fusion.21 = (bf16[4,4,64,384]{3,1,2,0:T(4,128)(2,1)S(1)}, bf16[4,4,64,384]{3,1,2,0:T(4,128)(2,1)S(1)}, bf16[4,4,64,384]{3,1,2,0:T(4,128)(2,1)S(1)}, bf16[4,4,64...) fusion(bf16[4,8,68,384]{3,1,2,0:T(8,128)(2,1)S(1)} %bitcast.46), kind=kLoop, calls=%fused_computation.35 | loop fusion | bytes 14155776 | tf_op jit(solution)/shard_map/slice | solution.py:67
  32.1 1.1 %pad_maximum_fusion.2 = bf16[4,4,64,1152]{3,1,2,0:T(4,128)(2,1)S(1)} fusion(bf16[4,4,64,384]{3,1,2,0:T(4,128)(2,1)S(1)} %get-tuple-element.6, bf16[4,4,64,384]{3,1,2,0:T(4,128)(2,1)S(1)} %get-tuple-element.7, bf16[4,4,64,384]{3,1,2,0:T(4,128)(2,1)S(1)} %get-tuple-element.5), kind=kLoop, calls=%fused_computation.2 | loop fusion | flops 7077888 | bytes 4718592 | tf_op jit(solution)/shard_map/concatenate | solution.py:65
  33.2 0.4 copy.20
  33.6 2.1 %pad_maximum_fusion = (bf16[4,4,64,1152]{3,1,2,0:T(4,128)(2,1)S(1)}, bf16[4,4,64,1152]{3,1,2,0:T(4,128)(2,1)S(1)}) fusion(bf16[4,4,64,384]{3,1,2,0:T(4,128)(2,1)S(1)} %get-tuple-element.11, bf16[4,4,64,384]{3,1,2,0:T(4,128)(2,1)S(1)} %get-tuple-element.12, bf16[4,4,64,384]{3,1,2,0:T(4,128)(2,1)S(1)} %get-tuple-element.13, ...), kind=kLoop, calls=%fused_computation | loop fusion | flops 14155776 | bytes 9437184 | tf_op jit(solution)/shard_map/concatenate | solution.py:65
  35.7 0.4 copy.16
  36.1 0.4 copy.18
  36.5 0.9 %fusion.24 = f32[1024,192]{0,1:T(8,128)S(1)} fusion(bf16[1024,1152]{1,0:T(8,128)(2,1)S(1)} %bitcast.49, bf16[1152,192]{0,1:T(8,128)(2,1)S(1)} %bitcast.57), kind=kOutput, calls=%fused_computation.38 | convolution fusion | flops 452984832 | bytes 3588096 | tf_op jit(solution)/shard_map/dot_general | solution.py:72
  37.5 0.0 copy-start.2
  37.5 0.9 %convolution_add_fusion.1 = f32[1024,192]{0,1:T(8,128)S(1)} fusion(f32[1024,192]{0,1:T(8,128)S(1)} %fusion.24, bf16[1024,1152]{1,0:T(8,128)(2,1)S(1)} %bitcast.47, bf16[1152,192]{0,1:T(8,128)(2,1)S(1)} %bitcast.56), kind=kOutput, calls=%fused_computation.4 | convolution fusion | flops 453181440 | bytes 4374528 | tf_op jit(solution)/shard_map/dot_general | solution.py:72
  38.4 0.0 copy-done.2
  38.4 0.9 %fusion.1 = bf16[1024,192]{0,1:T(8,128)(2,1)S(1)} fusion(f32[1024,192]{0,1:T(8,128)S(1)} %convolution_add_fusion.1, bf16[1024,1152]{1,0:T(8,128)(2,1)S(1)} %bitcast.48, bf16[1152,192]{0,1:T(8,128)(2,1)S(1)} %bitcast.58, f32[192]{0:T(256)S(1)} %copy-done.2), kind=kOutput, calls=%fused_computation.6 | convolution fusion | flops 453574656 | bytes 3982080 | tf_op jit(solution)/shard_map/dot_general | solution.py:72
  39.4 1.0 %copy.22 = bf16[1024,192]{1,0:T(8,128)(2,1)} copy(bf16[1024,192]{0,1:T(8,128)(2,1)S(1)} %fusion.1) | data formatting | bytes 786432 | tf_op jit(solution)/shard_map/convert_element_type | solution.py:78
  (5 shorter events, 0.1 us)
Async XLA Ops:
  0.0 10.5 %copy-start.1 = (f32[768]{0:T(1024)S(1)}, f32[768]{0:T(1024)}, u32[]{:S(2)}) copy-start(f32[768]{0:T(1024)} %param.9) | copy-start | bytes 9220
  2.1 7.1 %collective-permute-start = (bf16[2,2,32,384]{3,2,1,0:T(8,128)(2,1)S(1)}, bf16[2,2,32,384]{3,2,1,0:T(8,128)(2,1)S(1)}, u32[]{:S(2)}, u32[]{:S(2)}) collective-permute-start(bf16[2,2,32,384]{3,2,1,0:T(8,128)(2,1)S(1)} %fusion.20), channel_id=1, source_target_pairs={{0,4},{4,8},{8,12},{1,5},{5,9},{9,13},{2,6},{6,10},{10,14},{3,7},{... | collective-permute-start | bytes 294920 | tf_op jit(solution)/shard_map/ppermute | solution.py:10
  8.3 16.2 %copy-start = (bf16[3,3,384,192]{2,3,1,0:T(8,128)(2,1)S(1)}, bf16[3,3,384,192]{2,3,1,0:T(8,128)(2,1)}, u32[]{:S(2)}) copy-start(bf16[3,3,384,192]{2,3,1,0:T(8,128)(2,1)} %param.10) | copy-start | bytes 3981316
  12.0 5.6 %collective-permute-start.1 = (bf16[4,1,32,384]{3,2,1,0:T(8,128)(2,1)S(1)}, bf16[4,1,32,384]{3,2,1,0:T(8,128)(2,1)S(1)}, u32[]{:S(2)}, u32[]{:S(2)}) collective-permute-start(bf16[4,1,32,384]{3,2,1,0:T(8,128)(2,1)S(1)} %get-tuple-element.19), channel_id=1, source_target_pairs={{0,2},{1,3},{4,6},{5,7},{8,10},{9,11},{12,14},{13,15},{16,18},{17,... | collective-permute-start | bytes 294920 | tf_op jit(solution)/shard_map/ppermute | solution.py:21
  15.4 6.5 %collective-permute-start.2 = (bf16[4,1,32,384]{3,2,1,0:T(8,128)(2,1)S(1)}, bf16[4,1,32,384]{3,2,1,0:T(8,128)(2,1)S(1)}, u32[]{:S(2)}, u32[]{:S(2)}) collective-permute-start(bf16[4,1,32,384]{3,2,1,0:T(8,128)(2,1)S(1)} %get-tuple-element.20), channel_id=1, source_target_pairs={{2,0},{3,1},{6,4},{7,5},{10,8},{11,9},{14,12},{15,13},{18,16},{19,... | collective-permute-start | bytes 294920 | tf_op jit(solution)/shard_map/ppermute | solution.py:23
  22.0 4.1 %collective-permute-start.3 = (bf16[4,4,1,384]{3,2,1,0:T(2,128)(2,1)S(1)}, bf16[4,4,1,384]{3,2,1,0:T(2,128)(2,1)S(1)}, u32[]{:S(2)}, u32[]{:S(2)}) collective-permute-start(bf16[4,4,1,384]{3,2,1,0:T(2,128)(2,1)S(1)} %get-tuple-element.17), channel_id=1, source_target_pairs={{0,1},{2,3},{4,5},{6,7},{8,9},{10,11},{12,13},{14,15},{16,17},{18,... | collective-permute-start | bytes 36872 | tf_op jit(solution)/shard_map/ppermute | solution.py:21
  23.3 3.1 %collective-permute-start.4 = (bf16[4,4,1,384]{3,2,1,0:T(2,128)(2,1)S(1)}, bf16[4,4,1,384]{3,2,1,0:T(2,128)(2,1)S(1)}, u32[]{:S(2)}, u32[]{:S(2)}) collective-permute-start(bf16[4,4,1,384]{3,2,1,0:T(2,128)(2,1)S(1)} %get-tuple-element.18), channel_id=1, source_target_pairs={{1,0},{3,2},{5,4},{7,6},{9,8},{11,10},{13,12},{15,14},{17,16},{19,... | collective-permute-start | bytes 36872 | tf_op jit(solution)/shard_map/ppermute | solution.py:23
  37.5 1.0 %copy-start.2 = (f32[192]{0:T(256)S(1)}, f32[192]{0:T(256)}, u32[]{:S(2)}) copy-start(f32[192]{0:T(256)} %param.11) | copy-start | bytes 2308
where the time goes:
time: 41.2 us; the launch traced here: 40.4 us
  starting transfers between devices  12.2 us (30%)
  local copies, waits for them, and re-layouts  9.24 us (22%)
  matrix products  6.81 us (17%)
  waiting for transfers between devices  6.31 us (15%)
  other arithmetic  5.52 us (13%)
    ppermute x1, starting transfers between devices, passed_along(): return lax.ppermute(block, axis, route)  4.93 us
    ppermute x2, starting transfers between devices, with_halo(): lax.ppermute(tail, axis, [(i, (i + 1) % count) for i in range(ends)])  4.69 us
    ppermute x2, waiting for transfers between devices, with_halo(): lax.ppermute(head, axis, [((i + 1) % count, i) for i in range(ends)])  4.57 us
    slice x1, local copies, waits for them, and re-layouts, space_conv(): enlarged[:, row_tap:row_tap + out_rows, col_tap:col_tap + out_cols]  4.29 us
    dot_general x3, matrix products, time_conv(): jnp.dot(window, time_weight[offset], preferred_element_type=jnp.float32)  3.99 us
    concatenate x2, other arithmetic, space_conv(): jnp.concatenate([enlarged[:, row_tap:row_tap + out_rows, col_tap:col_tap...  3.2 us
    dot_general x3, matrix products, space_conv(): jnp.dot(patches.reshape(-1, 3 * channels), space_weight[row_tap].reshape(...  2.82 us
    ppermute x2, starting transfers between devices, with_halo(): lax.ppermute(head, axis, [((i + 1) % count, i) for i in range(ends)])  2.58 us
  transfers between devices with their start and end apart: 5, of which 4 were waited for; matrix products, arithmetic and copies ran while one was open for 7% of the time, Pallas kernels for 0%

commit v1 on v0

v1 whole, which is shorter than its diff:
```python
import functools

import jax
import jax.numpy as jnp
from jax import lax
from jax.experimental import pallas as pl
from jax.experimental.pallas import tpu as pltpu
from jax.sharding import PartitionSpec as P

LANES = 128


def activate(values, gain):
    mean_square = jnp.mean(values * values, axis=-1, keepdims=True)
    scaled = values * lax.rsqrt(mean_square + 1e-06) * gain
    return scaled / (1.0 + jnp.exp(-scaled))


def dot_nt(x, w):
    return lax.dot_general(x, w, (((1,), (1,)), ((), ())), preferred_element_type=jnp.float32)


def block_kernel(sides, *refs):
    n = len(sides)
    own, before = refs[0], refs[1]
    halo_own, halo_before = refs[2 : 2 + n], refs[2 + n : 2 + 2 * n]
    edge, gain_ref, tw, tb, sw, sb, out = refs[2 + 2 * n : 9 + 2 * n]
    acts, ups, side, taps, reach, rim, shift, wide = refs[9 + 2 * n :]
    frames, rows, cols, chans = own.shape
    ups_frames = 2 * frames
    c_out = sb.shape[1]
    body = rows * cols
    span = body + n * cols
    padded = acts.shape[1]

    shard = lax.axis_index("tm")
    row = lax.axis_index("rows")
    col = lax.axis_index("cols")
    last_row = lax.axis_size("rows") - 1
    not_first = (shard > 0).astype(jnp.float32)
    has_above = (row > 0).astype(jnp.float32)
    has_below = (row < last_row).astype(jnp.float32)

    gain = gain_ref[...]

    def put(f, first, values):
        acts[f, first : first + values.shape[0]] = values.astype(jnp.bfloat16)

    for f in range(2 * frames):
        if f < frames:
            source, halo, keep, g = before, halo_before, not_first, f
        else:
            source, halo, keep, g = own, halo_own, None, f - frames
        parts = [source[g, i] for i in range(rows)] + [h[g] for h in halo]
        parts.append(jnp.concatenate([edge[f], jnp.zeros_like(edge[f])], axis=0))
        first = 0
        for part in parts:
            values = activate(part.astype(jnp.float32), gain)
            if keep is not None:
                values = values * keep
            put(f, first, values)
            first += part.shape[0]

    window = jnp.concatenate(
        [acts[k : k + frames].reshape(frames * padded, chans) for k in range(3)], axis=1
    )
    summed = jnp.dot(window, tw[...].reshape(3 * chans, 2 * chans), preferred_element_type=jnp.float32)
    stacked = (summed + tb[...]).astype(jnp.bfloat16)
    for t in range(frames):
        for s in range(2):
            u = 2 * t + s
            lanes = slice(s * chans, (s + 1) * chans)
            ups[u] = stacked[t * padded : t * padded + span, lanes]
            beside = stacked[t * padded + span : (t + 1) * padded, lanes].astype(jnp.float32)
            for i in range(rows + n):
                side[8 * i + u : 8 * i + u + 1] = beside[i : i + 1]

    for a in range(3):
        for b in range(3):
            taps[a, b, :, :, :, :c_out] = dot_nt(
                ups[:, :body].reshape(ups_frames * body, chans), sw[a, b]
            ).reshape(ups_frames, rows, cols, c_out)

    for h, where in enumerate(sides):
        x = ups[:, body + h * cols : body + (h + 1) * cols].reshape(ups_frames * cols, chans)
        for b in range(3):
            tap = {"either": jnp.where(row == 0, 2, 0), "above": 0, "below": 2}[where]
            reach[h, b, :, :, :c_out] = dot_nt(x, sw[tap, b]).reshape(ups_frames, cols, c_out)

    tap = jnp.where(col == 0, 2, 0)
    x = side[...].astype(jnp.bfloat16)
    beside = [dot_nt(x, sw[a, tap]) for a in range(3)]

    def of_row(a, i):
        return beside[a][8 * i : 8 * i + 8]

    for p in range(2):
        for i in range(rows):
            if p == 0:
                total = of_row(1, i) + of_row(2, i)
                if i > 0:
                    total = total + of_row(0, i - 1)
                else:
                    for h, where in enumerate(sides):
                        if where != "below":
                            total = total + of_row(0, rows + h) * has_above
            else:
                total = of_row(0, i) + of_row(1, i)
                if i < rows - 1:
                    total = total + of_row(2, i + 1)
                else:
                    for h, where in enumerate(sides):
                        if where != "above":
                            total = total + of_row(2, rows + h) * has_below
            rim[p, i, :, :c_out] = total
    shift[:, :c_out] = sb[...]
    from_left = (col > 0).astype(jnp.float32)
    from_right = (col < lax.axis_size("cols") - 1).astype(jnp.float32)
    above = [h for h, where in enumerate(sides) if where != "below"][0]
    below = [h for h, where in enumerate(sides) if where != "above"][0]

    place = lax.broadcasted_iota(jnp.int32, (cols, LANES), 0)
    for half in range(2):
        lanes = slice(half * LANES, (half + 1) * LANES)
        bias = shift[:, lanes]
        for u in range(ups_frames):
            for i in range(rows):
                for p in range(2):
                    parts = []
                    for b in range(3):
                        if p == 0:
                            near = taps[1, b, u, i, :, lanes] + taps[2, b, u, i, :, lanes]
                            if i > 0:
                                far = taps[0, b, u, i - 1, :, lanes]
                            else:
                                far = reach[above, b, u, :, lanes] * has_above
                        else:
                            near = taps[0, b, u, i, :, lanes] + taps[1, b, u, i, :, lanes]
                            if i < rows - 1:
                                far = taps[2, b, u, i + 1, :, lanes]
                            else:
                                far = reach[below, b, u, :, lanes] * has_below
                        parts.append(near + far)
                    border = rim[p, i, u : u + 1, lanes]
                    left = jnp.where(place == 0, border * from_left, pltpu.roll(parts[0], 1, 0))
                    right = jnp.where(place == cols - 1, border * from_right, pltpu.roll(parts[2], cols - 1, 0))
                    middle = parts[1] + bias
                    wide[half, u, 2 * i + p, pl.ds(0, cols, 2)] = middle + parts[2] + left
                    wide[half, u, 2 * i + p, pl.ds(1, cols, 2)] = middle + parts[0] + right
    out[:, :, :, :LANES] = wide[0].astype(out.dtype)
    out[:, :, :, LANES:] = wide[1, :, :, :, : c_out - LANES].astype(out.dtype)


def block(sides, own, before, halo_own, halo_before, edge, norm_gain, time_weight, time_bias, space_weight, space_bias):
    frames, rows, cols, chans = own.shape
    c_out = space_bias.shape[0]
    n = len(sides)
    span = (rows + n) * cols
    vmem = pl.BlockSpec(memory_space=pltpu.VMEM)
    operands = (
        own,
        before,
        *halo_own,
        *halo_before,
        edge,
        norm_gain.reshape(1, chans),
        time_weight,
        time_bias.reshape(1, -1),
        jnp.swapaxes(space_weight, 2, 3),
        space_bias.reshape(1, c_out),
    )
    return pl.pallas_call(
        functools.partial(block_kernel, sides),
        out_shape=jax.ShapeDtypeStruct((2 * frames, 2 * rows, 2 * cols, c_out), jnp.bfloat16),
        in_specs=[vmem] * len(operands),
        out_specs=vmem,
        scratch_shapes=[
            pltpu.VMEM((2 * frames, span + 16, chans), jnp.bfloat16),
            pltpu.VMEM((2 * frames, span, chans), jnp.bfloat16),
            pltpu.VMEM((8 * (rows + n), chans), jnp.float32),
            pltpu.VMEM((3, 3, 2 * frames, rows, cols, 2 * LANES), jnp.float32),
            pltpu.VMEM((n, 3, 2 * frames, cols, 2 * LANES), jnp.float32),
            pltpu.VMEM((2, rows, 8, 2 * LANES), jnp.float32),
            pltpu.VMEM((1, 2 * LANES), jnp.float32),
            pltpu.VMEM((2, 2 * frames, 2 * rows, 2 * cols, LANES), jnp.float32),
        ],
        compiler_params=pltpu.CompilerParams(vmem_limit_bytes=24 * 1024 * 1024),
    )(*operands)


def local(latent, norm_gain, time_weight, time_bias, space_weight, space_bias):
    frames, rows, cols, chans = latent.shape
    shards, n_rows, n_cols = (lax.axis_size(a) for a in ("tm", "rows", "cols"))
    row = lax.axis_index("rows")
    col = lax.axis_index("cols")
    axes = ("tm", "rows", "cols")

    def moved(x, route):
        pairs = []
        for t in range(shards):
            for r in range(n_rows):
                for c in range(n_cols):
                    t2, r2, c2 = route(t, r, c)
                    pairs.append(((t * n_rows + r) * n_cols + c, (t2 * n_rows + r2) * n_cols + c2))
        return lax.ppermute(x, axes, pairs)

    def later(t):
        return (t + 1) % shards

    before = moved(latent, lambda t, r, c: (later(t), r, c))
    if n_rows == 2:
        sides = ("either",)
        near = jnp.where(row == 0, latent[:, rows - 1], latent[:, 0])
        halo_before = (moved(near, lambda t, r, c: (later(t), 1 - r, c)),)
        halo_own = (moved(near, lambda t, r, c: (t, 1 - r, c)),)
    else:
        sides = ("above", "below")

        def both(x):
            return (
                moved(x[:, rows - 1], lambda t, r, c: (t, (r + 1) % n_rows, c)),
                moved(x[:, 0], lambda t, r, c: (t, (r - 1) % n_rows, c)),
            )

        halo_own = both(latent)
        halo_before = both(before)

    def side(x):
        return jnp.where(col == 0, x[..., cols - 1, :], x[..., 0, :])

    levels = []
    for block_rows, halos in ((before, halo_before), (latent, halo_own)):
        levels.append(jnp.concatenate([side(block_rows)] + [side(h)[:, None] for h in halos], axis=1))
    edge = jnp.concatenate(levels, axis=0)
    edge = jnp.pad(edge, ((0, 0), (0, 8 - edge.shape[1]), (0, 0)))
    edge = moved(edge, lambda t, r, c: (t, r, 1 - c))
    return block(
        sides, latent, before, halo_own, halo_before, edge, norm_gain, time_weight, time_bias, space_weight, space_bias
    )


def solution(mesh):
    in_specs = (P(("clips", "tm"), "rows", "cols", None), P(), P(), P(), P(), P())
    out_specs = P(("clips", "tm"), "rows", "cols", None)
    return jax.shard_map(local, mesh=mesh, in_specs=in_specs, out_specs=out_specs, check_vma=False)
```

time: 41.2 us -> 22 us (0.53); the launches traced: 40.4 us -> 21.6 us
  matrix products: 6.81 us -> 0 us
  starting transfers between devices: 12.2 us -> 6.23 us
  other arithmetic: 5.52 us -> 0.9 us
  Pallas kernels: 0 us -> 2.94 us
  local copies, waits for them, and re-layouts: 9.24 us -> 6.72 us
  waiting for transfers between devices: 6.31 us -> 4.8 us
    dot_general x6 -> x0, matrix products: 6.81 us -> none  [the longest x3 3.99 us: time_conv(): jnp.dot(window, time_weight[offset], preferred_element_type=jnp.float32)]
    ppermute x5 -> x4, starting transfers between devices: 12.2 us -> 6.23 us  [moved(): return lax.ppermute(x, axes, pairs)]
    slice x6 -> x0, local copies, waits for them, and re-layouts: 5.59 us -> none  [the longest x1 4.29 us: space_conv(): enlarged[:, row_tap:row_tap + out_rows, col_tap:col_tap + out_cols]]
    unnamed x9, local copies, waits for them, and re-layouts: 0.2 us -> 5.33 us
    concatenate x4 -> x1, other arithmetic: 3.44 us -> 0.03 us  [local(): edge = jnp.concatenate(levels, axis=0)]
    pallas_call x0 -> x1, Pallas kernels: none -> 2.94 us  [block(): pl.pallas_call(functools.partial(block_kernel, sides), out_shape=jax.Shap...]
    ppermute x5 -> x4, waiting for transfers between devices: 6.31 us -> 4.8 us  [moved(): return lax.ppermute(x, axes, pairs)]
    concatenate x4 -> x0, local copies, waits for them, and re-layouts: 1.34 us -> none  [the longest x3 1.18 us: space_conv(): jnp.concatenate([enlarged[:, row_tap:row_tap + out_rows, col_tap:col_tap...]
  transfers between devices with their start and end apart: 5 -> 4, of which waited for: 4 -> 3; matrix products, arithmetic and copies ran while one was open for 7% -> 11% of each run, Pallas kernels for 0% -> 0%
where the time goes in v1:
time: 22 us; the launch traced here: 21.6 us
  local copies, waits for them, and re-layouts  6.72 us (31%)
  starting transfers between devices  6.23 us (28%)
  waiting for transfers between devices  4.8 us (22%)
  Pallas kernels  2.94 us (13%)
  other arithmetic  0.9 us (4%)
    ppermute x4, starting transfers between devices, moved(): return lax.ppermute(x, axes, pairs)  6.23 us
    unnamed x9, local copies, waits for them, and re-layouts  5.33 us
    ppermute x4, waiting for transfers between devices, moved(): return lax.ppermute(x, axes, pairs)  4.8 us
    pallas_call x1, Pallas kernels, block(): pl.pallas_call(functools.partial(block_kernel, sides), out_shape=jax.Shap...  2.94 us
    select_n x1, other arithmetic, local(): near = jnp.where(row == 0, latent[:, rows - 1], latent[:, 0])  0.83 us
    reshape x1, local copies, waits for them, and re-layouts, block(): time_bias.reshape(1, -1)  0.69 us
    reshape x1, local copies, waits for them, and re-layouts, block(): norm_gain.reshape(1, chans)  0.69 us
  transfers between devices with their start and end apart: 4, of which 3 were waited for; matrix products, arithmetic and copies ran while one was open for 11% of the time, Pallas kernels for 0%

profile of v1, /device:TPU:0, one launch (start us, length us, event | category | flops | bytes accessed | tf_op | source)
XLA Modules:
  0.0 21.6 jit_solution(15490690773679529804)
XLA Ops:
  0.0 0.8 %fusion.4 = bf16[2,32,384]{2,1,0:T(8,128)(2,1)S(1)} fusion(bf16[2,2,32,384]{3,2,1,0:T(8,128)(2,1)} %refs_0_.1, pred[]{:T(512)S(6)} %eq.4), kind=kLoop, calls=%fused_computation.6 | loop fusion | flops 24576 | bytes 147457 | tf_op jit(solution)/shard_map/jit(_where)/select_n | solution.py:213
  0.8 4.0 %collective-permute-start.2 = (bf16[2,32,384]{2,1,0:T(8,128)(2,1)S(1)}, bf16[2,32,384]{2,1,0:T(8,128)(2,1)S(1)}, u32[]{:S(2)}, u32[]{:S(2)}) collective-permute-start(bf16[2,32,384]{2,1,0:T(8,128)(2,1)S(1)} %fusion.4), channel_id=1, source_target_pairs={{0,6},{1,7},{2,4},{3,5},{4,10},{5,11},{6,8},{7,9},{8,14},{9,15},{1... | collective-permute-start | bytes 147464 | tf_op jit(solution)/shard_map/ppermute | solution.py:205
  4.8 0.5 %collective-permute-start.1 = (bf16[2,32,384]{2,1,0:T(8,128)(2,1)S(1)}, bf16[2,32,384]{2,1,0:T(8,128)(2,1)S(1)}, u32[]{:S(2)}, u32[]{:S(2)}) collective-permute-start(bf16[2,32,384]{2,1,0:T(8,128)(2,1)S(1)} %fusion.4), channel_id=1, source_target_pairs={{0,2},{1,3},{2,0},{3,1},{4,6},{5,7},{6,4},{7,5},{8,10},{9,11},{10,... | collective-permute-start | bytes 147464 | tf_op jit(solution)/shard_map/ppermute | solution.py:205
  5.4 1.0 %copy.7 = bf16[2,2,32,384]{3,1,0,2:T(2,128)(2,1)S(1)} copy(bf16[2,2,32,384]{3,2,1,0:T(8,128)(2,1)} %refs_0_.1) | data formatting | bytes 196608 | tf_op args[0]
  6.3 1.6 %collective-permute-start = (bf16[2,2,32,384]{3,1,0,2:T(2,128)(2,1)S(1)}, bf16[2,2,32,384]{3,1,0,2:T(2,128)(2,1)S(1)}, u32[]{:S(2)}, u32[]{:S(2)}) collective-permute-start(bf16[2,2,32,384]{3,1,0,2:T(2,128)(2,1)S(1)} %copy.7), channel_id=1, source_target_pairs={{0,4},{1,5},{2,6},{3,7},{4,8},{5,9},{6,10},{7,11},{8,12},{9,13},{1... | collective-permute-start | bytes 294920 | tf_op jit(solution)/shard_map/ppermute | solution.py:205
  8.0 1.1 %collective-permute-done.2.refs_3_ = bf16[2,32,384]{2,1,0:T(8,128)(2,1)S(1)} collective-permute-done((bf16[2,32,384]{2,1,0:T(8,128)(2,1)S(1)}, bf16[2,32,384]{2,1,0:T(8,128)(2,1)S(1)}, u32[]{:S(2)}, u32[]{:S(2)}) %collective-permute-start.2) | collective-permute-done | bytes 49184 | tf_op jit(solution)/shard_map/ppermute | solution.py:205
  9.0 0.4 %collective-permute-done.1.refs_2_ = bf16[2,32,384]{2,1,0:T(8,128)(2,1)S(1)} collective-permute-done((bf16[2,32,384]{2,1,0:T(8,128)(2,1)S(1)}, bf16[2,32,384]{2,1,0:T(8,128)(2,1)S(1)}, u32[]{:S(2)}, u32[]{:S(2)}) %collective-permute-start.1) | collective-permute-done | bytes 49184 | tf_op jit(solution)/shard_map/ppermute | solution.py:205
  9.5 3.3 %collective-permute-done = bf16[2,2,32,384]{3,1,0,2:T(2,128)(2,1)S(1)} collective-permute-done((bf16[2,2,32,384]{3,1,0,2:T(2,128)(2,1)S(1)}, bf16[2,2,32,384]{3,1,0,2:T(2,128)(2,1)S(1)}, u32[]{:S(2)}, u32[]{:S(2)}) %collective-permute-start) | collective-permute-done | bytes 98336 | tf_op jit(solution)/shard_map/ppermute | solution.py:205
  12.9 0.1 collective-permute-start.3
  12.9 0.7 %reshape.15.refs_5_ = f32[1,384]{1,0:T(1,128)S(1)} reshape(f32[384]{0:T(512)} %param.7) | data formatting | bytes 3072 | tf_op jit(solution)/shard_map/reshape | solution.py:166
  13.6 0.7 %reshape.16.refs_7_ = f32[1,768]{1,0:T(1,128)S(1)} reshape(f32[768]{0:T(1024)} %param.9) | data formatting | bytes 6144 | tf_op jit(solution)/shard_map/reshape | solution.py:168
  14.3 0.0 collective-permute-done.3.refs_4_
  14.3 0.0 copy-start
  14.3 1.5 %copy-done = bf16[3,384,768]{2,1,0:T(8,128)(2,1)S(1)} copy-done((bf16[3,384,768]{2,1,0:T(8,128)(2,1)S(1)}, bf16[3,384,768]{2,1,0:T(8,128)(2,1)}, u32[]{:S(2)}) %copy-start) | copy-done | bytes 1769496
  15.8 0.0 copy-start.1
  15.8 1.3 %copy-done.1 = bf16[3,3,384,192]{2,3,1,0:T(8,128)(2,1)S(1)} copy-done((bf16[3,3,384,192]{2,3,1,0:T(8,128)(2,1)S(1)}, bf16[3,3,384,192]{2,3,1,0:T(8,128)(2,1)}, u32[]{:S(2)}) %copy-start.1) | copy-done | bytes 1327128
  17.1 0.0 copy-start.2
  17.1 0.9 %copy-done.2 = bf16[2,2,32,384]{3,2,1,0:T(8,128)(2,1)S(1)} copy-done((bf16[2,2,32,384]{3,2,1,0:T(8,128)(2,1)S(1)}, bf16[2,2,32,384]{3,2,1,0:T(8,128)(2,1)}, u32[]{:S(2)}) %copy-start.2) | copy-done | bytes 98328
  18.0 0.0 copy-start.3
  18.0 0.7 %copy-done.3 = f32[192]{0:T(256)S(1)} copy-done((f32[192]{0:T(256)S(1)}, f32[192]{0:T(256)}, u32[]{:S(2)}) %copy-start.3) | copy-done | bytes 792
  18.7 2.9 %shard_map.64 = bf16[4,4,64,192]{3,2,1,0:T(8,128)(2,1)} custom-call(bf16[2,2,32,384]{3,2,1,0:T(8,128)(2,1)S(1)} %copy-done.2, bf16[2,2,32,384]{3,2,1,0:T(8,128)(2,1)S(1)} %copy.12.refs_1_, bf16[2,32,384]{2,1,0:T(8,128)(2,1)S(1)} %collective-permute-done.1.refs_2_, bf16[2,32,384]{2,1,0:T(8,128)(2,1)S(1)} %collective-permute-done.2.refs_3_, ...), custom_call_target="tpu_custom_call" | custom-call | tf_op jit(solution)/shard_map/pallas_call | solution.py:172
  (6 shorter events, 0.1 us)
Async XLA Ops:
  0.8 8.2 %collective-permute-start.2 = (bf16[2,32,384]{2,1,0:T(8,128)(2,1)S(1)}, bf16[2,32,384]{2,1,0:T(8,128)(2,1)S(1)}, u32[]{:S(2)}, u32[]{:S(2)}) collective-permute-start(bf16[2,32,384]{2,1,0:T(8,128)(2,1)S(1)} %fusion.4), channel_id=1, source_target_pairs={{0,6},{1,7},{2,4},{3,5},{4,10},{5,11},{6,8},{7,9},{8,14},{9,15},{1... | collective-permute-start | bytes 147464 | tf_op jit(solution)/shard_map/ppermute | solution.py:205
  4.8 4.6 %collective-permute-start.1 = (bf16[2,32,384]{2,1,0:T(8,128)(2,1)S(1)}, bf16[2,32,384]{2,1,0:T(8,128)(2,1)S(1)}, u32[]{:S(2)}, u32[]{:S(2)}) collective-permute-start(bf16[2,32,384]{2,1,0:T(8,128)(2,1)S(1)} %fusion.4), channel_id=1, source_target_pairs={{0,2},{1,3},{2,0},{3,1},{4,6},{5,7},{6,4},{7,5},{8,10},{9,11},{10,... | collective-permute-start | bytes 147464 | tf_op jit(solution)/shard_map/ppermute | solution.py:205
  6.3 6.5 %collective-permute-start = (bf16[2,2,32,384]{3,1,0,2:T(2,128)(2,1)S(1)}, bf16[2,2,32,384]{3,1,0,2:T(2,128)(2,1)S(1)}, u32[]{:S(2)}, u32[]{:S(2)}) collective-permute-start(bf16[2,2,32,384]{3,1,0,2:T(2,128)(2,1)S(1)} %copy.7), channel_id=1, source_target_pairs={{0,4},{1,5},{2,6},{3,7},{4,8},{5,9},{6,10},{7,11},{8,12},{9,13},{1... | collective-permute-start | bytes 294920 | tf_op jit(solution)/shard_map/ppermute | solution.py:205
  12.9 1.5 %collective-permute-start.3 = (bf16[4,8,384]{2,1,0:T(8,128)(2,1)S(1)}, bf16[4,8,384]{2,1,0:T(8,128)(2,1)S(1)}, u32[]{:S(2)}, u32[]{:S(2)}) collective-permute-start(bf16[4,8,384]{2,1,0:T(8,128)(2,1)S(1)} %fusion.6), channel_id=1, source_target_pairs={{0,1},{1,0},{2,3},{3,2},{4,5},{5,4},{6,7},{7,6},{8,9},{9,8},{10,11... | collective-permute-start | bytes 73736 | tf_op jit(solution)/shard_map/ppermute | solution.py:205
  14.3 1.5 %copy-start = (bf16[3,384,768]{2,1,0:T(8,128)(2,1)S(1)}, bf16[3,384,768]{2,1,0:T(8,128)(2,1)}, u32[]{:S(2)}) copy-start(bf16[3,384,768]{2,1,0:T(8,128)(2,1)} %refs_6_.1) | copy-start | bytes 5308420
  15.8 1.3 %copy-start.1 = (bf16[3,3,384,192]{2,3,1,0:T(8,128)(2,1)S(1)}, bf16[3,3,384,192]{2,3,1,0:T(8,128)(2,1)}, u32[]{:S(2)}) copy-start(bf16[3,3,384,192]{2,3,1,0:T(8,128)(2,1)} %param.10) | copy-start | bytes 3981316
  17.1 0.9 %copy-start.2 = (bf16[2,2,32,384]{3,2,1,0:T(8,128)(2,1)S(1)}, bf16[2,2,32,384]{3,2,1,0:T(8,128)(2,1)}, u32[]{:S(2)}) copy-start(bf16[2,2,32,384]{3,2,1,0:T(8,128)(2,1)} %refs_0_.1) | copy-start | bytes 294916
  18.0 0.7 %copy-start.3 = (f32[192]{0:T(256)S(1)}, f32[192]{0:T(256)}, u32[]{:S(2)}) copy-start(f32[192]{0:T(256)} %param.11) | copy-start | bytes 2308

commit v2 on v1

v2 whole, which is shorter than its diff:
```python
import functools

import jax
import jax.numpy as jnp
from jax import lax
from jax.experimental import pallas as pl
from jax.experimental.pallas import tpu as pltpu
from jax.sharding import PartitionSpec as P

LANES = 128
SMALL = pltpu.CompilerParams(vmem_limit_bytes=4 * 1024 * 1024)
VMEM = pl.BlockSpec(memory_space=pltpu.VMEM)


def activate(values, gain):
    values = values.astype(jnp.float32)
    mean_square = jnp.mean(values * values, axis=-1, keepdims=True)
    scaled = values * lax.rsqrt(mean_square + 1e-06) * gain
    return scaled / (1.0 + jnp.exp(-scaled))


def dot_nt(x, w):
    return lax.dot_general(x, w, (((1,), (1,)), ((), ())), preferred_element_type=jnp.float32)


def time_conv(acts, tw, tb):
    frames, positions, chans = acts.shape[0] - 2, acts.shape[1], acts.shape[2]
    window = jnp.concatenate(
        [acts[k : k + frames].reshape(frames * positions, chans) for k in range(3)], axis=1
    )
    summed = jnp.dot(window, tw[...].reshape(3 * chans, 2 * chans), preferred_element_type=jnp.float32)
    return (summed + tb[...].reshape(1, -1)).astype(jnp.bfloat16)


def put_column(x, out):
    frames, rows, cols, _ = x.shape
    col = lax.axis_index("cols")
    for i in range(rows):
        for f in range(frames):
            first = x[f, i, 0:8].astype(jnp.float32)[0:1]
            last = x[f, i, cols - 8 :].astype(jnp.float32)[7:8]
            out[i * frames + f : i * frames + f + 1] = jnp.where(col == 0, last, first)


def column_kernel(x, out, rows_f32):
    put_column(x, rows_f32)
    out[...] = rows_f32[...].astype(out.dtype)


def column_of(x):
    shape = (8, x.shape[-1])
    return pl.pallas_call(
        column_kernel,
        out_shape=jax.ShapeDtypeStruct(shape, x.dtype),
        in_specs=[VMEM],
        out_specs=VMEM,
        scratch_shapes=[pltpu.VMEM(shape, jnp.float32)],
        compiler_params=SMALL,
    )(x)


def split_kernel(latent, column, near, rows_f32):
    frames, rows, cols, _ = latent.shape
    put_column(latent, rows_f32)
    column[...] = rows_f32[...].astype(column.dtype)
    row = lax.axis_index("rows")
    for f in range(frames):
        near[f * cols : (f + 1) * cols] = jnp.where(row == 0, latent[f, rows - 1], latent[f, 0])


def split(latent):
    frames, _, cols, chans = latent.shape
    return pl.pallas_call(
        split_kernel,
        out_shape=[
            jax.ShapeDtypeStruct((8, chans), latent.dtype),
            jax.ShapeDtypeStruct((frames * cols, chans), latent.dtype),
        ],
        in_specs=[VMEM],
        out_specs=[VMEM] * 2,
        scratch_shapes=[pltpu.VMEM((8, chans), jnp.float32)],
        cost_estimate=pl.CostEstimate(flops=8 * 10**9, bytes_accessed=10**5, transcendentals=0),
        compiler_params=SMALL,
    )(latent)


def mid_kernel(before, own, gain_v, tw, tb, sw, taps, acts, ups):
    frames, rows, cols, chans = before.shape
    body = rows * cols
    c_out = sw.shape[2]
    keep = (lax.axis_index("tm") > 0).astype(jnp.float32)
    g = gain_v[...].reshape(1, -1)
    for f in range(frames):
        for i in range(rows):
            at = slice(i * cols, (i + 1) * cols)
            acts[f, at] = (activate(before[f, i], g) * keep).astype(jnp.bfloat16)
            acts[frames + f, at] = activate(own[f, i], g).astype(jnp.bfloat16)
    stacked = time_conv(acts, tw, tb)
    for t in range(frames):
        for s in range(2):
            ups[2 * t + s] = stacked[t * body : (t + 1) * body, s * chans : (s + 1) * chans]
    for a in range(3):
        for b in range(3):
            product = dot_nt(ups[...].reshape(2 * frames * body, chans), sw[a, b])
            taps[a, b, :, :, :, :c_out] = product.reshape(2 * frames, rows, cols, c_out)


def mid(before, own, gain, tw, tb, sw):
    frames, rows, cols, chans = before.shape
    return pl.pallas_call(
        mid_kernel,
        out_shape=jax.ShapeDtypeStruct((3, 3, 2 * frames, rows, cols, 2 * LANES), jnp.float32),
        in_specs=[VMEM] * 6,
        out_specs=VMEM,
        scratch_shapes=[
            pltpu.VMEM((2 * frames, rows * cols, chans), jnp.bfloat16),
            pltpu.VMEM((2 * frames, rows * cols, chans), jnp.bfloat16),
        ],
        cost_estimate=pl.CostEstimate(flops=6 * 10**8, bytes_accessed=6 * 10**6, transcendentals=0),
        compiler_params=pltpu.CompilerParams(vmem_limit_bytes=16 * 1024 * 1024),
    )(before, own, gain, tw, tb, sw)


def post_kernel(sides, *refs):
    n = len(sides)
    halo_own, halo_before = refs[:n], refs[n : 2 * n]
    edge_own, edge_before, taps, gain_v, tw, tb, sw, sb, out = refs[2 * n : 9 + 2 * n]
    edges, acts, ups, side, reach, rim, shift, wide = refs[9 + 2 * n :]
    ups_frames, rows, cols = taps.shape[2:5]
    frames = ups_frames // 2
    chans, c_out = sw.shape[3], sw.shape[2]
    span = n * cols
    padded = span + 16

    row = lax.axis_index("rows")
    col = lax.axis_index("cols")
    last_row = lax.axis_size("rows") - 1
    not_first = (lax.axis_index("tm") > 0).astype(jnp.float32)
    has_above = (row > 0).astype(jnp.float32)
    has_below = (row < last_row).astype(jnp.float32)

    gain = gain_v[...].reshape(1, -1)
    for f in range(2 * frames):
        halo, edge, g = (halo_before, edge_before, f) if f < frames else (halo_own, edge_own, f - frames)
        for i in range(rows):
            edges[f, i : i + 1] = edge[...].astype(jnp.float32)[i * frames + g : i * frames + g + 1]
        for h in range(n):
            corners = halo[h][frames * cols : frames * cols + 8].astype(jnp.float32)
            edges[f, rows + h : rows + h + 1] = corners[g : g + 1]
        parts = [halo[h][g * cols : (g + 1) * cols] for h in range(n)]
        parts.append(edges[f])
        first = 0
        for part in parts:
            values = activate(part, gain)
            if f < frames:
                values = values * not_first
            acts[f, first : first + part.shape[0]] = values.astype(jnp.bfloat16)
            first += part.shape[0]
    stacked = time_conv(acts, tw, tb)
    for t in range(frames):
        for s in range(2):
            u = 2 * t + s
            lanes = slice(s * chans, (s + 1) * chans)
            ups[u] = stacked[t * padded : t * padded + span, lanes]
            beside = stacked[t * padded + span : (t + 1) * padded, lanes].astype(jnp.float32)
            for i in range(rows + n):
                side[8 * i + u : 8 * i + u + 1] = beside[i : i + 1]

    for h, where in enumerate(sides):
        x = ups[:, h * cols : (h + 1) * cols].reshape(ups_frames * cols, chans)
        for b in range(3):
            tap = {"either": jnp.where(row == 0, 2, 0), "above": 0, "below": 2}[where]
            reach[h, b, :, :, :c_out] = dot_nt(x, sw[tap, b]).reshape(ups_frames, cols, c_out)

    tap = jnp.where(col == 0, 2, 0)
    x = side[...].astype(jnp.bfloat16)
    beside = [dot_nt(x, sw[a, tap]) for a in range(3)]

    def of_row(a, i):
        return beside[a][8 * i : 8 * i + 8]

    for p in range(2):
        for i in range(rows):
            if p == 0:
                total = of_row(1, i) + of_row(2, i)
                if i > 0:
                    total = total + of_row(0, i - 1)
                else:
                    for h, where in enumerate(sides):
                        if where != "below":
                            total = total + of_row(0, rows + h) * has_above
            else:
                total = of_row(0, i) + of_row(1, i)
                if i < rows - 1:
                    total = total + of_row(2, i + 1)
                else:
                    for h, where in enumerate(sides):
                        if where != "above":
                            total = total + of_row(2, rows + h) * has_below
            rim[p, i, :, :c_out] = total
    shift[:, :c_out] = sb[...].reshape(1, c_out)
    from_left = (col > 0).astype(jnp.float32)
    from_right = (col < lax.axis_size("cols") - 1).astype(jnp.float32)
    above = [h for h, where in enumerate(sides) if where != "below"][0]
    below = [h for h, where in enumerate(sides) if where != "above"][0]

    place = lax.broadcasted_iota(jnp.int32, (cols, LANES), 0)
    for half in range(2):
        lanes = slice(half * LANES, (half + 1) * LANES)
        bias = shift[:, lanes]
        for u in range(ups_frames):
            for i in range(rows):
                for p in range(2):
                    parts = []
                    for b in range(3):
                        if p == 0:
                            near = taps[1, b, u, i, :, lanes] + taps[2, b, u, i, :, lanes]
                            if i > 0:
                                far = taps[0, b, u, i - 1, :, lanes]
                            else:
                                far = reach[above, b, u, :, lanes] * has_above
                        else:
                            near = taps[0, b, u, i, :, lanes] + taps[1, b, u, i, :, lanes]
                            if i < rows - 1:
                                far = taps[2, b, u, i + 1, :, lanes]
                            else:
                                far = reach[below, b, u, :, lanes] * has_below
                        parts.append(near + far)
                    border = rim[p, i, u : u + 1, lanes]
                    left = jnp.where(place == 0, border * from_left, pltpu.roll(parts[0], 1, 0))
                    right = jnp.where(place == cols - 1, border * from_right, pltpu.roll(parts[2], cols - 1, 0))
                    middle = parts[1] + bias
                    wide[half, u, 2 * i + p, pl.ds(0, cols, 2)] = middle + parts[2] + left
                    wide[half, u, 2 * i + p, pl.ds(1, cols, 2)] = middle + parts[0] + right
    out[:, :, :, :LANES] = wide[0].astype(out.dtype)
    out[:, :, :, LANES:] = wide[1, :, :, :, : c_out - LANES].astype(out.dtype)


def post(sides, halo_own, halo_before, edge_own, edge_before, taps, gain, tw, tb, sw, sb):
    frames = taps.shape[2] // 2
    rows, cols = taps.shape[3:5]
    chans, c_out = sw.shape[3], sw.shape[2]
    n = len(sides)
    operands = (*halo_own, *halo_before, edge_own, edge_before, taps, gain, tw, tb, sw, sb)
    return pl.pallas_call(
        functools.partial(post_kernel, sides),
        out_shape=jax.ShapeDtypeStruct((2 * frames, 2 * rows, 2 * cols, c_out), jnp.bfloat16),
        in_specs=[VMEM] * len(operands),
        out_specs=VMEM,
        scratch_shapes=[
            pltpu.VMEM((2 * frames, 16, chans), jnp.float32),
            pltpu.VMEM((2 * frames, n * cols + 16, chans), jnp.bfloat16),
            pltpu.VMEM((2 * frames, n * cols, chans), jnp.bfloat16),
            pltpu.VMEM((8 * (rows + n), chans), jnp.float32),
            pltpu.VMEM((n, 3, 2 * frames, cols, 2 * LANES), jnp.float32),
            pltpu.VMEM((2, rows, 8, 2 * LANES), jnp.float32),
            pltpu.VMEM((1, 2 * LANES), jnp.float32),
            pltpu.VMEM((2, 2 * frames, 2 * rows, 2 * cols, LANES), jnp.float32),
        ],
        compiler_params=pltpu.CompilerParams(vmem_limit_bytes=24 * 1024 * 1024),
    )(*operands)


def local(latent, norm_gain, time_weight, time_bias, space_weight, space_bias):
    frames, rows, cols, chans = latent.shape
    shards, n_rows, n_cols = (lax.axis_size(a) for a in ("tm", "rows", "cols"))
    row = lax.axis_index("rows")
    axes = ("tm", "rows", "cols")

    def moved(x, route):
        pairs = []
        for t in range(shards):
            for r in range(n_rows):
                for c in range(n_cols):
                    t2, r2, c2 = route(t, r, c)
                    pairs.append(((t * n_rows + r) * n_cols + c, (t2 * n_rows + r2) * n_cols + c2))
        return lax.ppermute(x, axes, pairs)

    def later(t):
        return (t + 1) % shards

    def column(x):
        return moved(x, lambda t, r, c: (t, r, 1 - c))

    def and_corner(x, column, i):
        corner = lax.dynamic_slice_in_dim(column, i * frames, frames, 0)
        return jnp.concatenate([x, corner, jnp.zeros((8 - frames, chans), x.dtype)], axis=0)

    edge, near = split(latent)
    edge_own = column(edge)
    before = moved(latent, lambda t, r, c: (later(t), r, c))
    edge_before = column(column_of(before))
    if n_rows == 2:
        sides = ("either",)
        near = and_corner(near, edge_own, (rows - 1) * (1 - row))
        halo_before = (moved(near, lambda t, r, c: (later(t), 1 - r, c)),)
        halo_own = (moved(near, lambda t, r, c: (t, 1 - r, c)),)
    else:
        sides = ("above", "below")

        def both(x, edge):
            last = and_corner(x[:, rows - 1].reshape(frames * cols, chans), edge, rows - 1)
            first = and_corner(x[:, 0].reshape(frames * cols, chans), edge, 0)
            return (
                moved(last, lambda t, r, c: (t, (r + 1) % n_rows, c)),
                moved(first, lambda t, r, c: (t, (r - 1) % n_rows, c)),
            )

        halo_own = both(latent, edge_own)
        halo_before = both(before, edge_before)

    gain, tw, tb, sb = norm_gain, time_weight, time_bias, space_bias
    sw = jnp.swapaxes(space_weight, 2, 3)
    taps = mid(before, latent, gain, tw, tb, sw)
    return post(sides, halo_own, halo_before, edge_own, edge_before, taps, gain, tw, tb, sw, sb)


def solution(mesh):
    in_specs = (P(("clips", "tm"), "rows", "cols", None), P(), P(), P(), P(), P())
    out_specs = P(("clips", "tm"), "rows", "cols", None)
    return jax.shard_map(local, mesh=mesh, in_specs=in_specs, out_specs=out_specs, check_vma=False)
```

time: 22 us -> 14.6 us (0.66); the launches traced: 21.6 us -> 14.5 us
  local copies, waits for them, and re-layouts: 6.72 us -> 0.11 us
  Pallas kernels: 2.94 us -> 5.49 us
  waiting for transfers between devices: 4.8 us -> 2.37 us
  other arithmetic: 0.9 us -> 0.08 us
    unnamed x9 -> x10, local copies, waits for them, and re-layouts: 5.33 us -> 0.02 us
    pallas_call x1 -> x4, Pallas kernels: 2.94 us -> 5.49 us  [the longest x1 2.24 us: mid(): pl.pallas_call(mid_kernel, out_shape=jax.ShapeDtypeStruct((3, 3, 2 * fram...]
    ppermute x4 -> x5, waiting for transfers between devices: 4.8 us -> 2.37 us  [moved(): return lax.ppermute(x, axes, pairs)]
    reshape x2 -> x0, local copies, waits for them, and re-layouts: 1.37 us -> none  [the longest x1 0.69 us: block(): time_bias.reshape(1, -1)]
    select_n x5 -> x0, other arithmetic: 0.87 us -> none  [the longest x1 0.83 us: local(): near = jnp.where(row == 0, latent[:, rows - 1], latent[:, 0])]
    ppermute x4 -> x5, starting transfers between devices: 6.23 us -> 6.33 us  [moved(): return lax.ppermute(x, axes, pairs)]
  transfers between devices with their start and end apart: 4 -> 5, of which waited for: 3 -> 1; matrix products, arithmetic and copies ran while one was open for 11% -> 1% of each run, Pallas kernels for 0% -> 16%
where the time goes in v2:
time: 14.6 us; the launch traced here: 14.5 us
  starting transfers between devices  6.33 us (43%)
  Pallas kernels  5.49 us (38%)
  waiting for transfers between devices  2.37 us (16%)
    ppermute x5, starting transfers between devices, moved(): return lax.ppermute(x, axes, pairs)  6.33 us
    ppermute x5, waiting for transfers between devices, moved(): return lax.ppermute(x, axes, pairs)  2.37 us
    pallas_call x1, Pallas kernels, mid(): pl.pallas_call(mid_kernel, out_shape=jax.ShapeDtypeStruct((3, 3, 2 * fram...  2.24 us
    pallas_call x1, Pallas kernels, post(): pl.pallas_call(functools.partial(post_kernel, sides), out_shape=jax.Shape...  2.16 us
    pallas_call x1, Pallas kernels, split(): pl.pallas_call(split_kernel, out_shape=[jax.ShapeDtypeStruct((8, chans),...  1.07 us
  transfers between devices with their start and end apart: 5, of which 1 were waited for; matrix products, arithmetic and copies ran while one was open for 1% of the time, Pallas kernels for 16%

profile of v2, /device:TPU:0, one launch (start us, length us, event | category | flops | bytes accessed | tf_op | source)
XLA Modules:
  0.0 14.5 jit_solution(9852926969552049447)
XLA Ops:
  0.0 0.0 copy-start.2
  0.0 0.0 copy-start
  0.0 0.0 copy-start.3
  0.0 0.0 copy-start.1
  0.0 1.1 %shard_map.64 = (bf16[8,384]{1,0:T(8,128)(2,1)S(1)}, bf16[64,384]{1,0:T(8,128)(2,1)S(1)}) custom-call(bf16[2,2,32,384]{3,2,1,0:T(8,128)(2,1)} %own.1), custom_call_target="tpu_custom_call" | custom-call | flops 8000000000 | bytes 100000 | tf_op jit(solution)/shard_map/pallas_call | solution.py:73
  1.1 0.5 %collective-permute-start = (bf16[8,384]{1,0:T(8,128)(2,1)S(1)}, bf16[8,384]{1,0:T(8,128)(2,1)S(1)}, u32[]{:S(2)}, u32[]{:S(2)}) collective-permute-start(bf16[8,384]{1,0:T(8,128)(2,1)S(1)} %get-tuple-element.8), channel_id=1, source_target_pairs={{0,1},{1,0},{2,3},{3,2},{4,5},{5,4},{6,7},{7,6},{8,9},{9,8},{10,11... | collective-permute-start | bytes 18440 | tf_op jit(solution)/shard_map/ppermute | solution.py:277
  1.6 2.6 %collective-permute-start.3 = (bf16[2,2,32,384]{3,2,1,0:T(8,128)(2,1)}, bf16[2,2,32,384]{3,2,1,0:T(8,128)(2,1)S(1)}, u32[]{:S(2)}, u32[]{:S(2)}) collective-permute-start(bf16[2,2,32,384]{3,2,1,0:T(8,128)(2,1)} %own.1), channel_id=1, source_target_pairs={{0,4},{1,5},{2,6},{3,7},{4,8},{5,9},{6,10},{7,11},{8,12},{9,13},{1... | collective-permute-start | bytes 294920 | tf_op jit(solution)/shard_map/ppermute | solution.py:277
  4.2 0.1 pad.2.clone
  4.3 0.0 collective-permute-done.refs_2_
  4.3 0.1 maximum_maximum_fusion
  4.4 2.6 %collective-permute-start.2 = (bf16[72,384]{1,0:T(8,128)(2,1)S(1)}, bf16[72,384]{1,0:T(8,128)(2,1)S(1)}, u32[]{:S(2)}, u32[]{:S(2)}) collective-permute-start(bf16[72,384]{1,0:T(8,128)(2,1)S(1)} %maximum_maximum_fusion), channel_id=1, source_target_pairs={{0,6},{1,7},{2,4},{3,5},{4,10},{5,11},{6,8},{7,9},{8,14},{9,15},{1... | collective-permute-start | bytes 165896 | tf_op jit(solution)/shard_map/ppermute | solution.py:277
  7.0 0.5 %collective-permute-start.1 = (bf16[72,384]{1,0:T(8,128)(2,1)S(1)}, bf16[72,384]{1,0:T(8,128)(2,1)S(1)}, u32[]{:S(2)}, u32[]{:S(2)}) collective-permute-start(bf16[72,384]{1,0:T(8,128)(2,1)S(1)} %maximum_maximum_fusion), channel_id=1, source_target_pairs={{0,2},{1,3},{2,0},{3,1},{4,6},{5,7},{6,4},{7,5},{8,10},{9,11},{10,... | collective-permute-start | bytes 165896 | tf_op jit(solution)/shard_map/ppermute | solution.py:277
  7.5 2.4 %collective-permute-done.3.x.before = bf16[2,2,32,384]{3,2,1,0:T(8,128)(2,1)S(1)} collective-permute-done((bf16[2,2,32,384]{3,2,1,0:T(8,128)(2,1)}, bf16[2,2,32,384]{3,2,1,0:T(8,128)(2,1)S(1)}, u32[]{:S(2)}, u32[]{:S(2)}) %collective-permute-start.3) | collective-permute-done | bytes 98336 | tf_op jit(solution)/shard_map/ppermute | solution.py:277
  9.9 0.1 collective-permute-start.4
  10.0 0.0 copy-done.2
  10.0 0.0 copy-done
  10.0 0.0 copy-done.3
  10.0 0.0 copy-done.1
  10.0 0.0 copy-start.4
  10.0 2.2 %shard_map.66.refs_4_ = f32[3,3,4,2,32,256]{5,4,3,2,1,0:T(8,128)S(1)} custom-call(bf16[2,2,32,384]{3,2,1,0:T(8,128)(2,1)S(1)} %collective-permute-done.3.x.before, bf16[2,2,32,384]{3,2,1,0:T(8,128)(2,1)} %own.1, f32[384]{0:T(512)S(1)} %copy-done.3, bf16[3,384,768]{2,1,0:T(8,128)(2,1)S(1)} %copy-done, f32[768]{0:T(1024)S(1)} %copy-done.2, ...), custom_call_target="tpu_custom_call" | custom-call | flops 600000000 | bytes 6000000 | tf_op jit(solution)/shard_map/pallas_call | solution.py:110
  12.3 0.0 collective-permute-done.2.refs_1_
  12.3 0.0 collective-permute-done.1.refs_0_
  12.3 0.0 collective-permute-done.4.refs_3_
  12.3 0.0 copy-done.4
  12.3 2.2 %shard_map.67 = bf16[4,4,64,192]{3,2,1,0:T(8,128)(2,1)} custom-call(bf16[72,384]{1,0:T(8,128)(2,1)S(1)} %collective-permute-done.1.refs_0_, bf16[72,384]{1,0:T(8,128)(2,1)S(1)} %collective-permute-done.2.refs_1_, bf16[8,384]{1,0:T(8,128)(2,1)S(1)} %collective-permute-done.refs_2_, bf16[8,384]{1,0:T(8,128)(2,1)S(1)} %collective-permute-done.4.refs_3_, ...), custom_call_target="tpu_custom_call" | custom-call | tf_op jit(solution)/shard_map/pallas_call | solution.py:245
  (3 shorter events, 0.0 us)
Async XLA Ops:
  0.0 10.0 %copy-start.2 = (f32[768]{0:T(1024)S(1)}, f32[768]{0:T(1024)}, u32[]{:S(2)}) copy-start(f32[768]{0:T(1024)} %refs_7_.1) | copy-start | bytes 9220
  0.0 10.0 %copy-start = (bf16[3,384,768]{2,1,0:T(8,128)(2,1)S(1)}, bf16[3,384,768]{2,1,0:T(8,128)(2,1)}, u32[]{:S(2)}) copy-start(bf16[3,384,768]{2,1,0:T(8,128)(2,1)} %refs_6_.1) | copy-start | bytes 5308420
  0.0 10.0 %copy-start.3 = (f32[384]{0:T(512)S(1)}, f32[384]{0:T(512)}, u32[]{:S(2)}) copy-start(f32[384]{0:T(512)} %refs_5_.1) | copy-start | bytes 4612
  0.0 10.0 %copy-start.1 = (bf16[3,3,384,192]{2,3,1,0:T(8,128)(2,1)S(1)}, bf16[3,3,384,192]{2,3,1,0:T(8,128)(2,1)}, u32[]{:S(2)}) copy-start(bf16[3,3,384,192]{2,3,1,0:T(8,128)(2,1)} %param.10) | copy-start | bytes 3981316
  1.1 3.3 %collective-permute-start = (bf16[8,384]{1,0:T(8,128)(2,1)S(1)}, bf16[8,384]{1,0:T(8,128)(2,1)S(1)}, u32[]{:S(2)}, u32[]{:S(2)}) collective-permute-start(bf16[8,384]{1,0:T(8,128)(2,1)S(1)} %get-tuple-element.8), channel_id=1, source_target_pairs={{0,1},{1,0},{2,3},{3,2},{4,5},{5,4},{6,7},{7,6},{8,9},{9,8},{10,11... | collective-permute-start | bytes 18440 | tf_op jit(solution)/shard_map/ppermute | solution.py:277
  1.6 8.3 %collective-permute-start.3 = (bf16[2,2,32,384]{3,2,1,0:T(8,128)(2,1)}, bf16[2,2,32,384]{3,2,1,0:T(8,128)(2,1)S(1)}, u32[]{:S(2)}, u32[]{:S(2)}) collective-permute-start(bf16[2,2,32,384]{3,2,1,0:T(8,128)(2,1)} %own.1), channel_id=1, source_target_pairs={{0,4},{1,5},{2,6},{3,7},{4,8},{5,9},{6,10},{7,11},{8,12},{9,13},{1... | collective-permute-start | bytes 294920 | tf_op jit(solution)/shard_map/ppermute | solution.py:277
  4.4 7.9 %collective-permute-start.2 = (bf16[72,384]{1,0:T(8,128)(2,1)S(1)}, bf16[72,384]{1,0:T(8,128)(2,1)S(1)}, u32[]{:S(2)}, u32[]{:S(2)}) collective-permute-start(bf16[72,384]{1,0:T(8,128)(2,1)S(1)} %maximum_maximum_fusion), channel_id=1, source_target_pairs={{0,6},{1,7},{2,4},{3,5},{4,10},{5,11},{6,8},{7,9},{8,14},{9,15},{1... | collective-permute-start | bytes 165896 | tf_op jit(solution)/shard_map/ppermute | solution.py:277
  7.0 5.3 %collective-permute-start.1 = (bf16[72,384]{1,0:T(8,128)(2,1)S(1)}, bf16[72,384]{1,0:T(8,128)(2,1)S(1)}, u32[]{:S(2)}, u32[]{:S(2)}) collective-permute-start(bf16[72,384]{1,0:T(8,128)(2,1)S(1)} %maximum_maximum_fusion), channel_id=1, source_target_pairs={{0,2},{1,3},{2,0},{3,1},{4,6},{5,7},{6,4},{7,5},{8,10},{9,11},{10,... | collective-permute-start | bytes 165896 | tf_op jit(solution)/shard_map/ppermute | solution.py:277
  9.9 2.4 %collective-permute-start.4 = (bf16[8,384]{1,0:T(8,128)(2,1)S(1)}, bf16[8,384]{1,0:T(8,128)(2,1)S(1)}, u32[]{:S(2)}, u32[]{:S(2)}) collective-permute-start(bf16[8,384]{1,0:T(8,128)(2,1)S(1)} %shard_map.65), channel_id=1, source_target_pairs={{0,1},{1,0},{2,3},{3,2},{4,5},{5,4},{6,7},{7,6},{8,9},{9,8},{10,11... | collective-permute-start | bytes 18440 | tf_op jit(solution)/shard_map/ppermute | solution.py:277
  10.0 2.3 %copy-start.4 = (f32[192]{0:T(256)S(1)}, f32[192]{0:T(256)}, u32[]{:S(2)}) copy-start(f32[192]{0:T(256)} %refs_9_.1) | copy-start | bytes 2308

commit v3 on v2

--- a/solution.py
+++ b/solution.py
@@ -32,18 +32,30 @@
     return (summed + tb[...].reshape(1, -1)).astype(jnp.bfloat16)
 
 
-def put_column(x, out):
+def keep_kernel(keep):
+    keep[...] = jnp.full(keep.shape, (lax.axis_index("tm") > 0).astype(jnp.float32))
+
+
+def keep_row(chans):
+    return pl.pallas_call(
+        keep_kernel,
+        out_shape=jax.ShapeDtypeStruct((1, chans), jnp.float32),
+        out_specs=VMEM,
+        compiler_params=SMALL,
+    )()
+
+
+def put_column(x, last, out):
     frames, rows, cols, _ = x.shape
-    col = lax.axis_index("cols")
     for i in range(rows):
         for f in range(frames):
-            first = x[f, i, 0:8].astype(jnp.float32)[0:1]
-            last = x[f, i, cols - 8 :].astype(jnp.float32)[7:8]
-            out[i * frames + f : i * frames + f + 1] = jnp.where(col == 0, last, first)
+            low = x[f, i, 0:8].astype(jnp.float32)[0:1]
+            high = x[f, i, cols - 8 :].astype(jnp.float32)[7:8]
+            out[i * frames + f : i * frames + f + 1] = jnp.where(last, high, low)
 
 
 def column_kernel(x, out, rows_f32):
-    put_column(x, rows_f32)
+    put_column(x, lax.axis_index("cols") == 0, rows_f32)
     out[...] = rows_f32[...].astype(out.dtype)
 
 
@@ -59,42 +71,63 @@
     )(x)
 
 
-def split_kernel(latent, column, near, rows_f32):
-    frames, rows, cols, _ = latent.shape
-    put_column(latent, rows_f32)
-    column[...] = rows_f32[...].astype(column.dtype)
-    row = lax.axis_index("rows")
-    for f in range(frames):
-        near[f * cols : (f + 1) * cols] = jnp.where(row == 0, latent[f, rows - 1], latent[f, 0])
-
-
-def split(latent):
-    frames, _, cols, chans = latent.shape
+def split_kernel(row, beside, edge, near, rows_f32):
+    frames, rows, cols, _ = beside.shape
+    put_column(beside, lax.axis_index("cols") > 0, rows_f32)
+    edge[...] = rows_f32[...].astype(edge.dtype)
+    upper = lax.axis_index("rows") == 0
+    near[: frames * cols] = row[...]
+    corner = rows_f32[...]
+    corner = jnp.where(upper, pltpu.roll(corner, 8 - (rows - 1) * frames, 0), corner)
+    near[frames * cols :] = corner.astype(near.dtype)
+
+
+def split(row, beside):
+    frames, _, cols, chans = beside.shape
     return pl.pallas_call(
         split_kernel,
         out_shape=[
-            jax.ShapeDtypeStruct((8, chans), latent.dtype),
-            jax.ShapeDtypeStruct((frames * cols, chans), latent.dtype),
+            jax.ShapeDtypeStruct((8, chans), row.dtype),
+            jax.ShapeDtypeStruct((frames * cols + 8, chans), row.dtype),
         ],
-        in_specs=[VMEM],
+        in_specs=[VMEM] * 2,
         out_specs=[VMEM] * 2,
         scratch_shapes=[pltpu.VMEM((8, chans), jnp.float32)],
         cost_estimate=pl.CostEstimate(flops=8 * 10**9, bytes_accessed=10**5, transcendentals=0),
         compiler_params=SMALL,
-    )(latent)
-
-
-def mid_kernel(before, own, gain_v, tw, tb, sw, taps, acts, ups):
+    )(row, beside)
+
+
+def pre_kernel(own, gain_v, acts):
+    frames, rows, cols, _ = own.shape
+    g = gain_v[...].reshape(1, -1)
+    for f in range(frames):
+        for i in range(rows):
+            acts[f, i * cols : (i + 1) * cols] = activate(own[f, i], g).astype(jnp.bfloat16)
+
+
+def pre(own, gain):
+    frames, rows, cols, chans = own.shape
+    return pl.pallas_call(
+        pre_kernel,
+        out_shape=jax.ShapeDtypeStruct((frames, rows * cols, chans), jnp.bfloat16),
+        in_specs=[VMEM] * 2,
+        out_specs=VMEM,
+        cost_estimate=pl.CostEstimate(flops=10**6, bytes_accessed=10**5, transcendentals=0),
+        compiler_params=SMALL,
+    )(own, gain)
+
+
+def mid_kernel(before, acts_own, keep, gain_v, tw, tb, sw, taps, acts, ups):
     frames, rows, cols, chans = before.shape
     body = rows * cols
     c_out = sw.shape[2]
-    keep = (lax.axis_index("tm") > 0).astype(jnp.float32)
     g = gain_v[...].reshape(1, -1)
     for f in range(frames):
         for i in range(rows):
             at = slice(i * cols, (i + 1) * cols)
-            acts[f, at] = (activate(before[f, i], g) * keep).astype(jnp.bfloat16)
-            acts[frames + f, at] = activate(own[f, i], g).astype(jnp.bfloat16)
+            acts[f, at] = (activate(before[f, i], g) * keep[...]).astype(jnp.bfloat16)
+    acts[frames:] = acts_own[...]
     stacked = time_conv(acts, tw, tb)
     for t in range(frames):
         for s in range(2):
@@ -105,12 +138,12 @@
             taps[a, b, :, :, :, :c_out] = product.reshape(2 * frames, rows, cols, c_out)
 
 
-def mid(before, own, gain, tw, tb, sw):
+def mid(before, acts_own, keep, gain, tw, tb, sw):
     frames, rows, cols, chans = before.shape
     return pl.pallas_call(
         mid_kernel,
         out_shape=jax.ShapeDtypeStruct((3, 3, 2 * frames, rows, cols, 2 * LANES), jnp.float32),
-        in_specs=[VMEM] * 6,
+        in_specs=[VMEM] * 7,
         out_specs=VMEM,
         scratch_shapes=[
             pltpu.VMEM((2 * frames, rows * cols, chans), jnp.bfloat16),
@@ -118,14 +151,14 @@
         ],
         cost_estimate=pl.CostEstimate(flops=6 * 10**8, bytes_accessed=6 * 10**6, transcendentals=0),
         compiler_params=pltpu.CompilerParams(vmem_limit_bytes=16 * 1024 * 1024),
-    )(before, own, gain, tw, tb, sw)
+    )(before, acts_own, keep, gain, tw, tb, sw)
 
 
 def post_kernel(sides, *refs):
     n = len(sides)
     halo_own, halo_before = refs[:n], refs[n : 2 * n]
-    edge_own, edge_before, taps, gain_v, tw, tb, sw, sb, out = refs[2 * n : 9 + 2 * n]
-    edges, acts, ups, side, reach, rim, shift, wide = refs[9 + 2 * n :]
+    edge_own, edge_before, taps, keep, gain_v, tw, tb, sw, sb, out = refs[2 * n : 10 + 2 * n]
+    edges, acts, ups, side, reach, rim, shift, wide, done, sems = refs[10 + 2 * n :]
     ups_frames, rows, cols = taps.shape[2:5]
     frames = ups_frames // 2
     chans, c_out = sw.shape[3], sw.shape[2]
@@ -135,7 +168,6 @@
     row = lax.axis_index("rows")
     col = lax.axis_index("cols")
     last_row = lax.axis_size("rows") - 1
-    not_first = (lax.axis_index("tm") > 0).astype(jnp.float32)
     has_above = (row > 0).astype(jnp.float32)
     has_below = (row < last_row).astype(jnp.float32)
 
@@ -153,7 +185,7 @@
         for part in parts:
             values = activate(part, gain)
             if f < frames:
-                values = values * not_first
+                values = values * keep[...]
             acts[f, first : first + part.shape[0]] = values.astype(jnp.bfloat16)
             first += part.shape[0]
     stacked = time_conv(acts, tw, tb)
@@ -205,10 +237,11 @@
     below = [h for h, where in enumerate(sides) if where != "above"][0]
 
     place = lax.broadcasted_iota(jnp.int32, (cols, LANES), 0)
-    for half in range(2):
-        lanes = slice(half * LANES, (half + 1) * LANES)
-        bias = shift[:, lanes]
-        for u in range(ups_frames):
+    copies = []
+    for u in range(ups_frames):
+        for half in range(2):
+            lanes = slice(half * LANES, (half + 1) * LANES)
+            bias = shift[:, lanes]
             for i in range(rows):
                 for p in range(2):
                     parts = []
@@ -232,21 +265,25 @@
                     middle = parts[1] + bias
                     wide[half, u, 2 * i + p, pl.ds(0, cols, 2)] = middle + parts[2] + left
                     wide[half, u, 2 * i + p, pl.ds(1, cols, 2)] = middle + parts[0] + right
-    out[:, :, :, :LANES] = wide[0].astype(out.dtype)
-    out[:, :, :, LANES:] = wide[1, :, :, :, : c_out - LANES].astype(out.dtype)
-
-
-def post(sides, halo_own, halo_before, edge_own, edge_before, taps, gain, tw, tb, sw, sb):
+        done[u, :, :, :LANES] = wide[0, u].astype(done.dtype)
+        done[u, :, :, LANES:] = wide[1, u, :, :, : c_out - LANES].astype(done.dtype)
+        copies.append(pltpu.make_async_copy(done.at[u], out.at[u], sems.at[u]))
+        copies[u].start()
+    for copy in copies:
+        copy.wait()
+
+
+def post(sides, halo_own, halo_before, edge_own, edge_before, taps, keep, gain, tw, tb, sw, sb):
     frames = taps.shape[2] // 2
     rows, cols = taps.shape[3:5]
     chans, c_out = sw.shape[3], sw.shape[2]
     n = len(sides)
-    operands = (*halo_own, *halo_before, edge_own, edge_before, taps, gain, tw, tb, sw, sb)
+    operands = (*halo_own, *halo_before, edge_own, edge_before, taps, keep, gain, tw, tb, sw, sb)
     return pl.pallas_call(
         functools.partial(post_kernel, sides),
         out_shape=jax.ShapeDtypeStruct((2 * frames, 2 * rows, 2 * cols, c_out), jnp.bfloat16),
         in_specs=[VMEM] * len(operands),
-        out_specs=VMEM,
+        out_specs=pl.BlockSpec(memory_space=pl.ANY),
         scratch_shapes=[
             pltpu.VMEM((2 * frames, 16, chans), jnp.float32),
             pltpu.VMEM((2 * frames, n * cols + 16, chans), jnp.bfloat16),
@@ -256,6 +293,8 @@
             pltpu.VMEM((2, rows, 8, 2 * LANES), jnp.float32),
             pltpu.VMEM((1, 2 * LANES), jnp.float32),
             pltpu.VMEM((2, 2 * frames, 2 * rows, 2 * cols, LANES), jnp.float32),
+            pltpu.VMEM((2 * frames, 2 * rows, 2 * cols, c_out), jnp.bfloat16),
+            pltpu.SemaphoreType.DMA((2 * frames,)),
         ],
         compiler_params=pltpu.CompilerParams(vmem_limit_bytes=24 * 1024 * 1024),
     )(*operands)
@@ -264,7 +303,6 @@
 def local(latent, norm_gain, time_weight, time_bias, space_weight, space_bias):
     frames, rows, cols, chans = latent.shape
     shards, n_rows, n_cols = (lax.axis_size(a) for a in ("tm", "rows", "cols"))
-    row = lax.axis_index("rows")
     axes = ("tm", "rows", "cols")
 
     def moved(x, route):
@@ -279,24 +317,27 @@
     def later(t):
         return (t + 1) % shards
 
-    def column(x):
+    def across(x):
         return moved(x, lambda t, r, c: (t, r, 1 - c))
 
-    def and_corner(x, column, i):
-        corner = lax.dynamic_slice_in_dim(column, i * frames, frames, 0)
-        return jnp.concatenate([x, corner, jnp.zeros((8 - frames, chans), x.dtype)], axis=0)
-
-    edge, near = split(latent)
-    edge_own = column(edge)
+    keep = keep_row(chans)
+    beside = across(latent)
     before = moved(latent, lambda t, r, c: (later(t), r, c))
-    edge_before = column(column_of(before))
+    after, beside = lax.optimization_barrier((latent, beside))
+    upper = lax.axis_index("rows") == 0
+    row = jnp.where(upper, after[:, rows - 1], after[:, 0]).reshape(frames * cols, chans)
+    edge_own, near = split(row, beside)
+    edge_before = across(column_of(before))
     if n_rows == 2:
         sides = ("either",)
-        near = and_corner(near, edge_own, (rows - 1) * (1 - row))
         halo_before = (moved(near, lambda t, r, c: (later(t), 1 - r, c)),)
         halo_own = (moved(near, lambda t, r, c: (t, 1 - r, c)),)
     else:
         sides = ("above", "below")
+
+        def and_corner(x, edge, i):
+            corner = edge[i * frames : (i + 1) * frames]
+            return jnp.concatenate([x, corner, jnp.zeros((8 - frames, chans), x.dtype)], axis=0)
 
         def both(x, edge):
             last = and_corner(x[:, rows - 1].reshape(frames * cols, chans), edge, rows - 1)
@@ -311,8 +352,9 @@
 
     gain, tw, tb, sb = norm_gain, time_weight, time_bias, space_bias
     sw = jnp.swapaxes(space_weight, 2, 3)
-    taps = mid(before, latent, gain, tw, tb, sw)
-    return post(sides, halo_own, halo_before, edge_own, edge_before, taps, gain, tw, tb, sw, sb)
+    ready, _ = lax.optimization_barrier((latent, edge_own))
+    taps = mid(before, pre(ready, gain), keep, gain, tw, tb, sw)
+    return post(sides, halo_own, halo_before, edge_own, edge_before, taps, keep, gain, tw, tb, sw, sb)
 
 
 def solution(mesh):

time: 14.6 us -> 13.7 us (0.938)
  Pallas kernels: 5.49 us -> 3.73 us
  other arithmetic: 0.08 us -> 0.84 us
  waiting for transfers between devices: 2.37 us -> 2.67 us
    pallas_call x1, Pallas kernels: 1.07 us -> 0.03 us  [split(): pl.pallas_call(split_kernel, out_shape=[jax.ShapeDtypeStruct((8, chans),...]
    pallas_call x1, Pallas kernels: 2.24 us -> 1.36 us  [mid(): pl.pallas_call(mid_kernel, out_shape=jax.ShapeDtypeStruct((3, 3, 2 * fram...]
    select_n x0 -> x1, other arithmetic: none -> 0.84 us  [local(): jnp.where(upper, after[:, rows - 1], after[:, 0])]
    ppermute x5, waiting for transfers between devices: 2.37 us -> 2.67 us  [moved(): return lax.ppermute(x, axes, pairs)]
    pallas_call x0 -> x2, Pallas kernels: none -> 0.17 us  [the longest x1 0.16 us: pre(): pl.pallas_call(pre_kernel, out_shape=jax.ShapeDtypeStruct((frames, rows *...]
  transfers between devices with their start and end apart: 5 -> 5, of which waited for: 1 -> 3; matrix products, arithmetic and copies ran while one was open for 1% -> 6% of each run, Pallas kernels for 16% -> 12%
where the time goes in v3:
time: 13.7 us; the launch traced here: 13.6 us
  starting transfers between devices  6.19 us (45%)
  Pallas kernels  3.73 us (27%)
  waiting for transfers between devices  2.67 us (19%)
  other arithmetic  0.84 us (6%)
    ppermute x5, starting transfers between devices, moved(): return lax.ppermute(x, axes, pairs)  6.19 us
    ppermute x5, waiting for transfers between devices, moved(): return lax.ppermute(x, axes, pairs)  2.67 us
    pallas_call x1, Pallas kernels, post(): pl.pallas_call(functools.partial(post_kernel, sides), out_shape=jax.Shape...  2.15 us
    pallas_call x1, Pallas kernels, mid(): pl.pallas_call(mid_kernel, out_shape=jax.ShapeDtypeStruct((3, 3, 2 * fram...  1.36 us
    select_n x1, other arithmetic, local(): jnp.where(upper, after[:, rows - 1], after[:, 0])  0.84 us
  transfers between devices with their start and end apart: 5, of which 3 were waited for; matrix products, arithmetic and copies ran while one was open for 6% of the time, Pallas kernels for 12%

profile of v3, /device:TPU:0, one launch (start us, length us, event | category | flops | bytes accessed | tf_op | source)
XLA Modules:
  0.0 13.6 jit_solution(16268656743707879047)
XLA Ops:
  0.0 0.5 %collective-permute-start = (bf16[2,2,32,384]{3,2,1,0:T(8,128)(2,1)}, bf16[2,2,32,384]{3,2,1,0:T(8,128)(2,1)S(1)}, u32[]{:S(2)}, u32[]{:S(2)}) collective-permute-start(bf16[2,2,32,384]{3,2,1,0:T(8,128)(2,1)} %own), channel_id=1, source_target_pairs={{0,1},{1,0},{2,3},{3,2},{4,5},{5,4},{6,7},{7,6},{8,9},{9,8},{10,11... | collective-permute-start | bytes 294920 | tf_op jit(solution)/shard_map/ppermute | solution.py:315
  0.5 2.6 %collective-permute-start.3 = (bf16[2,2,32,384]{3,2,1,0:T(8,128)(2,1)}, bf16[2,2,32,384]{3,2,1,0:T(8,128)(2,1)S(1)}, u32[]{:S(2)}, u32[]{:S(2)}) collective-permute-start(bf16[2,2,32,384]{3,2,1,0:T(8,128)(2,1)} %own), channel_id=1, source_target_pairs={{0,4},{1,5},{2,6},{3,7},{4,8},{5,9},{6,10},{7,11},{8,12},{9,13},{1... | collective-permute-start | bytes 294920 | tf_op jit(solution)/shard_map/ppermute | solution.py:315
  3.0 0.0 collective-permute-done.beside
  3.0 0.8 %slice_select_fusion = bf16[2,1,32,384]{3,2,1,0:T(8,128)(2,1)S(1)} fusion(bf16[2,2,32,384]{3,2,1,0:T(8,128)(2,1)} %own, pred[]{:T(512)S(6)} %eq.3), kind=kLoop, calls=%fused_computation | loop fusion | flops 24576 | bytes 147457 | tf_op jit(solution)/shard_map/jit(_where)/select_n | solution.py:328
  3.9 0.0 copy-start.2
  3.9 0.0 copy-start.3
  3.9 0.0 copy-start
  3.9 0.0 copy-start.1
  3.9 0.0 copy-start.4
  4.0 2.6 %collective-permute-start.2 = (bf16[72,384]{1,0:T(8,128)(2,1)S(1)}, bf16[72,384]{1,0:T(8,128)(2,1)S(1)}, u32[]{:S(2)}, u32[]{:S(2)}) collective-permute-start(bf16[72,384]{1,0:T(8,128)(2,1)S(1)} %get-tuple-element.12), channel_id=1, source_target_pairs={{0,6},{1,7},{2,4},{3,5},{4,10},{5,11},{6,8},{7,9},{8,14},{9,15},{1... | collective-permute-start | bytes 165896 | tf_op jit(solution)/shard_map/ppermute | solution.py:315
  6.5 0.5 %collective-permute-start.1 = (bf16[72,384]{1,0:T(8,128)(2,1)S(1)}, bf16[72,384]{1,0:T(8,128)(2,1)S(1)}, u32[]{:S(2)}, u32[]{:S(2)}) collective-permute-start(bf16[72,384]{1,0:T(8,128)(2,1)S(1)} %get-tuple-element.12), channel_id=1, source_target_pairs={{0,2},{1,3},{2,0},{3,1},{4,6},{5,7},{6,4},{7,5},{8,10},{9,11},{10,... | collective-permute-start | bytes 165896 | tf_op jit(solution)/shard_map/ppermute | solution.py:315
  7.1 1.7 %collective-permute-done.3.x.before = bf16[2,2,32,384]{3,2,1,0:T(8,128)(2,1)S(1)} collective-permute-done((bf16[2,2,32,384]{3,2,1,0:T(8,128)(2,1)}, bf16[2,2,32,384]{3,2,1,0:T(8,128)(2,1)S(1)}, u32[]{:S(2)}, u32[]{:S(2)}) %collective-permute-start.3) | collective-permute-done | bytes 98336 | tf_op jit(solution)/shard_map/ppermute | solution.py:315
  8.8 0.1 collective-permute-start.4
  8.8 0.0 copy-done.2
  8.8 0.0 copy-done.3
  8.8 0.2 %shard_map.66.acts_own = bf16[2,64,384]{2,1,0:T(8,128)(2,1)S(1)} custom-call(bf16[2,2,32,384]{3,2,1,0:T(8,128)(2,1)S(1)} %copy-done.2, f32[384]{0:T(512)S(1)} %copy-done.3), custom_call_target="tpu_custom_call" | custom-call | flops 1000000 | bytes 100000 | tf_op jit(solution)/shard_map/pallas_call | solution.py:111
  9.0 0.0 copy-done
  9.0 0.0 copy-done.1
  9.0 0.0 copy-done.4
  9.0 0.0 copy-start.5
  9.1 1.4 %shard_map.68.refs_4_ = f32[3,3,4,2,32,256]{5,4,3,2,1,0:T(8,128)S(1)} custom-call(bf16[2,2,32,384]{3,2,1,0:T(8,128)(2,1)S(1)} %collective-permute-done.3.x.before, bf16[2,64,384]{2,1,0:T(8,128)(2,1)S(1)} %shard_map.66.acts_own, f32[1,384]{1,0:T(1,128)S(1)} %shard_map.67.keep.refs_5_, f32[384]{0:T(512)S(1)} %copy-done.3, bf16[3,384,768]{2,1,0:T(8,128)(2,1)S(1)} %copy-done, ...), custom_call_target="tpu_custom_call" | custom-call | flops 600000000 | bytes 6000000 | tf_op jit(solution)/shard_map/pallas_call | solution.py:143
  10.4 0.0 collective-permute-done.4.refs_3_
  10.4 0.5 %collective-permute-done.2.refs_1_ = bf16[72,384]{1,0:T(8,128)(2,1)S(1)} collective-permute-done((bf16[72,384]{1,0:T(8,128)(2,1)S(1)}, bf16[72,384]{1,0:T(8,128)(2,1)S(1)}, u32[]{:S(2)}, u32[]{:S(2)}) %collective-permute-start.2) | collective-permute-done | bytes 55328 | tf_op jit(solution)/shard_map/ppermute | solution.py:315
  10.9 0.5 %collective-permute-done.1.refs_0_ = bf16[72,384]{1,0:T(8,128)(2,1)S(1)} collective-permute-done((bf16[72,384]{1,0:T(8,128)(2,1)S(1)}, bf16[72,384]{1,0:T(8,128)(2,1)S(1)}, u32[]{:S(2)}, u32[]{:S(2)}) %collective-permute-start.1) | collective-permute-done | bytes 55328 | tf_op jit(solution)/shard_map/ppermute | solution.py:315
  11.4 0.0 copy-done.5
  11.4 2.1 %shard_map.69 = bf16[4,4,64,192]{3,2,1,0:T(8,128)(2,1)} custom-call(bf16[72,384]{1,0:T(8,128)(2,1)S(1)} %collective-permute-done.1.refs_0_, bf16[72,384]{1,0:T(8,128)(2,1)S(1)} %collective-permute-done.2.refs_1_, bf16[8,384]{1,0:T(8,128)(2,1)S(1)} %get-tuple-element.13.refs_2_, bf16[8,384]{1,0:T(8,128)(2,1)S(1)} %collective-permute-done.4.refs_3_, ...), custom_call_target="tpu_custom_call" | custom-call | tf_op jit(solution)/shard_map/pallas_call | solution.py:282
  (3 shorter events, 0.1 us)
Async XLA Ops:
  0.0 3.0 %collective-permute-start = (bf16[2,2,32,384]{3,2,1,0:T(8,128)(2,1)}, bf16[2,2,32,384]{3,2,1,0:T(8,128)(2,1)S(1)}, u32[]{:S(2)}, u32[]{:S(2)}) collective-permute-start(bf16[2,2,32,384]{3,2,1,0:T(8,128)(2,1)} %own), channel_id=1, source_target_pairs={{0,1},{1,0},{2,3},{3,2},{4,5},{5,4},{6,7},{7,6},{8,9},{9,8},{10,11... | collective-permute-start | bytes 294920 | tf_op jit(solution)/shard_map/ppermute | solution.py:315
  0.5 8.3 %collective-permute-start.3 = (bf16[2,2,32,384]{3,2,1,0:T(8,128)(2,1)}, bf16[2,2,32,384]{3,2,1,0:T(8,128)(2,1)S(1)}, u32[]{:S(2)}, u32[]{:S(2)}) collective-permute-start(bf16[2,2,32,384]{3,2,1,0:T(8,128)(2,1)} %own), channel_id=1, source_target_pairs={{0,4},{1,5},{2,6},{3,7},{4,8},{5,9},{6,10},{7,11},{8,12},{9,13},{1... | collective-permute-start | bytes 294920 | tf_op jit(solution)/shard_map/ppermute | solution.py:315
  3.9 5.0 %copy-start.2 = (bf16[2,2,32,384]{3,2,1,0:T(8,128)(2,1)S(1)}, bf16[2,2,32,384]{3,2,1,0:T(8,128)(2,1)}, u32[]{:S(2)}) copy-start(bf16[2,2,32,384]{3,2,1,0:T(8,128)(2,1)} %own) | copy-start | bytes 294916
  3.9 5.0 %copy-start.3 = (f32[384]{0:T(512)S(1)}, f32[384]{0:T(512)}, u32[]{:S(2)}) copy-start(f32[384]{0:T(512)} %refs_6_.1) | copy-start | bytes 4612
  3.9 5.1 %copy-start = (bf16[3,384,768]{2,1,0:T(8,128)(2,1)S(1)}, bf16[3,384,768]{2,1,0:T(8,128)(2,1)}, u32[]{:S(2)}) copy-start(bf16[3,384,768]{2,1,0:T(8,128)(2,1)} %refs_7_.1) | copy-start | bytes 5308420
  3.9 5.1 %copy-start.1 = (bf16[3,3,384,192]{2,3,1,0:T(8,128)(2,1)S(1)}, bf16[3,3,384,192]{2,3,1,0:T(8,128)(2,1)}, u32[]{:S(2)}) copy-start(bf16[3,3,384,192]{2,3,1,0:T(8,128)(2,1)} %param.10) | copy-start | bytes 3981316
  3.9 5.1 %copy-start.4 = (f32[768]{0:T(1024)S(1)}, f32[768]{0:T(1024)}, u32[]{:S(2)}) copy-start(f32[768]{0:T(1024)} %refs_8_.1) | copy-start | bytes 9220
  4.0 7.0 %collective-permute-start.2 = (bf16[72,384]{1,0:T(8,128)(2,1)S(1)}, bf16[72,384]{1,0:T(8,128)(2,1)S(1)}, u32[]{:S(2)}, u32[]{:S(2)}) collective-permute-start(bf16[72,384]{1,0:T(8,128)(2,1)S(1)} %get-tuple-element.12), channel_id=1, source_target_pairs={{0,6},{1,7},{2,4},{3,5},{4,10},{5,11},{6,8},{7,9},{8,14},{9,15},{1... | collective-permute-start | bytes 165896 | tf_op jit(solution)/shard_map/ppermute | solution.py:315
  6.5 4.9 %collective-permute-start.1 = (bf16[72,384]{1,0:T(8,128)(2,1)S(1)}, bf16[72,384]{1,0:T(8,128)(2,1)S(1)}, u32[]{:S(2)}, u32[]{:S(2)}) collective-permute-start(bf16[72,384]{1,0:T(8,128)(2,1)S(1)} %get-tuple-element.12), channel_id=1, source_target_pairs={{0,2},{1,3},{2,0},{3,1},{4,6},{5,7},{6,4},{7,5},{8,10},{9,11},{10,... | collective-permute-start | bytes 165896 | tf_op jit(solution)/shard_map/ppermute | solution.py:315
  8.8 1.7 %collective-permute-start.4 = (bf16[8,384]{1,0:T(8,128)(2,1)S(1)}, bf16[8,384]{1,0:T(8,128)(2,1)S(1)}, u32[]{:S(2)}, u32[]{:S(2)}) collective-permute-start(bf16[8,384]{1,0:T(8,128)(2,1)S(1)} %shard_map.65), channel_id=1, source_target_pairs={{0,1},{1,0},{2,3},{3,2},{4,5},{5,4},{6,7},{7,6},{8,9},{9,8},{10,11... | collective-permute-start | bytes 18440 | tf_op jit(solution)/shard_map/ppermute | solution.py:315
  9.0 2.4 %copy-start.5 = (f32[192]{0:T(256)S(1)}, f32[192]{0:T(256)}, u32[]{:S(2)}) copy-start(f32[192]{0:T(256)} %refs_10_.1) | copy-start | bytes 2308

commit v4 on v3

v4 whole, which is shorter than its diff:
```python
import functools

import jax
import jax.numpy as jnp
from jax import lax
from jax.experimental import pallas as pl
from jax.experimental.pallas import tpu as pltpu
from jax.sharding import PartitionSpec as P

LANES = 128
SMALL = pltpu.CompilerParams(vmem_limit_bytes=4 * 1024 * 1024)
VMEM = pl.BlockSpec(memory_space=pltpu.VMEM)


def activate(values, gain):
    values = values.astype(jnp.float32)
    mean_square = jnp.mean(values * values, axis=-1, keepdims=True)
    scaled = values * lax.rsqrt(mean_square + 1e-06) * gain
    return scaled / (1.0 + jnp.exp(-scaled))


def dot_nt(x, w):
    return lax.dot_general(x, w, (((1,), (1,)), ((), ())), preferred_element_type=jnp.float32)


def time_conv(acts, tw, tb):
    frames, positions, chans = acts.shape[0] - 2, acts.shape[1], acts.shape[2]
    window = jnp.concatenate(
        [acts[k : k + frames].reshape(frames * positions, chans) for k in range(3)], axis=1
    )
    summed = jnp.dot(window, tw[...].reshape(3 * chans, 2 * chans), preferred_element_type=jnp.float32)
    return (summed + tb[...].reshape(1, -1)).astype(jnp.bfloat16)


def keep_kernel(keep):
    keep[...] = jnp.full(keep.shape, (lax.axis_index("tm") > 0).astype(jnp.float32))


def keep_row(chans):
    return pl.pallas_call(
        keep_kernel,
        out_shape=jax.ShapeDtypeStruct((1, chans), jnp.float32),
        out_specs=VMEM,
        compiler_params=SMALL,
    )()


def put_column(x, last, out):
    frames, rows, cols, _ = x.shape
    for i in range(rows):
        for f in range(frames):
            low = x[f, i, 0:8].astype(jnp.float32)[0:1]
            high = x[f, i, cols - 8 :].astype(jnp.float32)[7:8]
            out[i * frames + f : i * frames + f + 1] = jnp.where(last, high, low)


def column_kernel(x, out, rows_f32):
    put_column(x, lax.axis_index("cols") == 0, rows_f32)
    out[...] = rows_f32[...].astype(out.dtype)


def column_of(x):
    shape = (8, x.shape[-1])
    return pl.pallas_call(
        column_kernel,
        out_shape=jax.ShapeDtypeStruct(shape, x.dtype),
        in_specs=[VMEM],
        out_specs=VMEM,
        scratch_shapes=[pltpu.VMEM(shape, jnp.float32)],
        compiler_params=SMALL,
    )(x)


def split_kernel(beside, corner, edge, near, rows_f32):
    frames, rows, cols, _ = beside.shape
    put_column(beside, lax.axis_index("cols") > 0, rows_f32)
    edge[...] = rows_f32[...].astype(edge.dtype)
    outer = jnp.where(lax.axis_index("rows") == 0, rows - 1, 0)
    for f in range(frames):
        near[f * cols : (f + 1) * cols] = beside[f, outer]
    near[frames * cols :] = corner[...]


def split(beside, corner):
    frames, _, cols, chans = beside.shape
    return pl.pallas_call(
        split_kernel,
        out_shape=[
            jax.ShapeDtypeStruct((8, chans), beside.dtype),
            jax.ShapeDtypeStruct((frames * cols + 8, chans), beside.dtype),
        ],
        in_specs=[VMEM] * 2,
        out_specs=[VMEM] * 2,
        scratch_shapes=[pltpu.VMEM((8, chans), jnp.float32)],
        cost_estimate=pl.CostEstimate(flops=8 * 10**9, bytes_accessed=10**5, transcendentals=0),
        compiler_params=SMALL,
    )(beside, corner)


def copy_kernel(x, out):
    out[...] = x[...]


def copied(x):
    return pl.pallas_call(
        copy_kernel,
        out_shape=jax.ShapeDtypeStruct(x.shape, x.dtype),
        in_specs=[VMEM],
        out_specs=VMEM,
        compiler_params=SMALL,
    )(x)


def pre_kernel(own, gain_v, acts):
    frames, rows, cols, _ = own.shape
    g = gain_v[...].reshape(1, -1)
    for f in range(frames):
        for i in range(rows):
            acts[f, i * cols : (i + 1) * cols] = activate(own[f, i], g).astype(jnp.bfloat16)


def pre(own, gain):
    frames, rows, cols, chans = own.shape
    return pl.pallas_call(
        pre_kernel,
        out_shape=jax.ShapeDtypeStruct((frames, rows * cols, chans), jnp.bfloat16),
        in_specs=[VMEM] * 2,
        out_specs=VMEM,
        cost_estimate=pl.CostEstimate(flops=10**6, bytes_accessed=10**5, transcendentals=0),
        compiler_params=SMALL,
    )(own, gain)


def mid_kernel(before, acts_own, keep, gain_v, tw, tb, sw, taps, acts, ups):
    frames, rows, cols, chans = before.shape
    body = rows * cols
    c_out = sw.shape[2]
    g = gain_v[...].reshape(1, -1)
    for f in range(frames):
        for i in range(rows):
            at = slice(i * cols, (i + 1) * cols)
            acts[f, at] = (activate(before[f, i], g) * keep[...]).astype(jnp.bfloat16)
    acts[frames:] = acts_own[...]
    stacked = time_conv(acts, tw, tb)
    for t in range(frames):
        for s in range(2):
            ups[2 * t + s] = stacked[t * body : (t + 1) * body, s * chans : (s + 1) * chans]
    for a in range(3):
        for b in range(3):
            product = dot_nt(ups[...].reshape(2 * frames * body, chans), sw[a, b])
            taps[a, b, :, :, :, :c_out] = product.reshape(2 * frames, rows, cols, c_out)


def mid(before, acts_own, keep, gain, tw, tb, sw):
    frames, rows, cols, chans = before.shape
    return pl.pallas_call(
        mid_kernel,
        out_shape=jax.ShapeDtypeStruct((3, 3, 2 * frames, rows, cols, 2 * LANES), jnp.float32),
        in_specs=[VMEM] * 7,
        out_specs=VMEM,
        scratch_shapes=[
            pltpu.VMEM((2 * frames, rows * cols, chans), jnp.bfloat16),
            pltpu.VMEM((2 * frames, rows * cols, chans), jnp.bfloat16),
        ],
        cost_estimate=pl.CostEstimate(flops=10**6, bytes_accessed=10**5, transcendentals=0),
        compiler_params=pltpu.CompilerParams(vmem_limit_bytes=16 * 1024 * 1024),
    )(before, acts_own, keep, gain, tw, tb, sw)


def sums(near, far, border, at_left, at_right, place):
    cols = place.shape[0]
    parts = [n if f is None else n + f for n, f in zip(near, far, strict=True)]
    left = jnp.where(place == 0, border * at_left, pltpu.roll(parts[0], 1, 0))
    right = jnp.where(place == cols - 1, border * at_right, pltpu.roll(parts[2], cols - 1, 0))
    return parts[1] + parts[2] + left, parts[0] + parts[1] + right


def store_row(done, index, wide, c_out):
    done[(*index, slice(None), slice(0, LANES))] = wide[0].astype(done.dtype)
    done[(*index, slice(None), slice(LANES, c_out))] = wide[1, :, : c_out - LANES].astype(done.dtype)


def column_sides():
    col = lax.axis_index("cols")
    at_left = (col > 0).astype(jnp.float32)
    at_right = (col < lax.axis_size("cols") - 1).astype(jnp.float32)
    return at_left, at_right, jnp.where(col == 0, 2, 0)


def rows_of(sides, rows):
    if sides == ("either",):
        upper = lax.axis_index("rows") == 0
        first = (0, 0)
        last = (rows - 1, 1)
        outer = tuple(jnp.where(upper, x, y) for x, y in zip(first, last, strict=True))
        inner = tuple(jnp.where(upper, y, x) for x, y in zip(first, last, strict=True))
        free, bound = [(*outer, False)], [inner]
    else:
        free, bound = [], [(0, 0), (rows - 1, 1)]
    for i in range(rows):
        for p in range(2):
            if (i, p) not in ((0, 0), (rows - 1, 1)):
                free.append((i, p, True))
    return free, bound


def sum_kernel(sides, edge_own, edge_before, taps, keep, gain_v, tw, tb, sw, sb, free_rows, near, rim, *scratch):
    edges, acts, side, border, shift, wide = scratch
    ups_frames, rows, cols = taps.shape[2:5]
    frames = ups_frames // 2
    chans, c_out = sw.shape[3], sw.shape[2]
    gain = gain_v[...].reshape(1, -1)
    for f in range(2 * frames):
        edge, g = (edge_before, f) if f < frames else (edge_own, f - frames)
        values = edge[...].astype(jnp.float32)
        for i in range(rows):
            edges[f, i : i + 1] = values[i * frames + g : i * frames + g + 1]
        values = activate(edges[f], gain)
        if f < frames:
            values = values * keep[...]
        acts[f] = values.astype(jnp.bfloat16)
    stacked = time_conv(acts, tw, tb)
    for t in range(frames):
        for s in range(2):
            beside = stacked[t * 16 : (t + 1) * 16, s * chans : (s + 1) * chans].astype(jnp.float32)
            for i in range(rows):
                at = 8 * i + 2 * t + s
                side[at : at + 1] = beside[i : i + 1]
    at_left, at_right, tap = column_sides()
    x = side[...].astype(jnp.bfloat16)
    for a in range(3):
        border[a, :, :, :c_out] = dot_nt(x, sw[a, tap]).reshape(rows, 8, c_out)
    shift[:, :c_out] = sb[...].reshape(1, c_out)

    place = lax.broadcasted_iota(jnp.int32, (cols, LANES), 0)
    free, bound = rows_of(sides, rows)
    for k, (i, p, inside) in enumerate(free):
        for u in range(ups_frames):
            for half in range(2):
                lanes = slice(half * LANES, (half + 1) * LANES)
                close = [taps[1 - p, b, u, i, :, lanes] + taps[2 - p, b, u, i, :, lanes] for b in range(3)]
                close[1] = close[1] + shift[:, lanes]
                line = border[1 - p, i, :, lanes] + border[2 - p, i, :, lanes]
                if inside:
                    far = [taps[2 * p, b, u, i + 2 * p - 1, :, lanes] for b in range(3)]
                    line = line + border[2 * p, i + 2 * p - 1, :, lanes]
                else:
                    far = [None] * 3
                even, odd = sums(close, far, line[u : u + 1], at_left, at_right, place)
                wide[half, pl.ds(0, cols, 2)] = even
                wide[half, pl.ds(1, cols, 2)] = odd
            store_row(free_rows, (k, u), wide, c_out)
    for k, (i, p) in enumerate(bound):
        rim[k] = border[1 - p, i] + border[2 - p, i]
        for u in range(ups_frames):
            for b in range(3):
                close = taps[1 - p, b, u, i] + taps[2 - p, b, u, i]
                near[k, b, u] = close + shift[...] if b == 1 else close


def partial_sums(sides, edge_own, edge_before, taps, keep, gain, tw, tb, sw, sb):
    ups_frames, rows, cols = taps.shape[2:5]
    chans, c_out = sw.shape[3], sw.shape[2]
    n_bound = len(sides)
    operands = (edge_own, edge_before, taps, keep, gain, tw, tb, sw, sb)
    return pl.pallas_call(
        functools.partial(sum_kernel, sides),
        out_shape=[
            jax.ShapeDtypeStruct((2 * rows - n_bound, ups_frames, 2 * cols, c_out), jnp.bfloat16),
            jax.ShapeDtypeStruct((n_bound, 3, ups_frames, cols, 2 * LANES), jnp.float32),
            jax.ShapeDtypeStruct((n_bound, 8, 2 * LANES), jnp.float32),
        ],
        in_specs=[VMEM] * len(operands),
        out_specs=[VMEM] * 3,
        scratch_shapes=[
            pltpu.VMEM((ups_frames, 16, chans), jnp.float32),
            pltpu.VMEM((ups_frames, 16, chans), jnp.bfloat16),
            pltpu.VMEM((8 * rows, chans), jnp.float32),
            pltpu.VMEM((3, rows, 8, 2 * LANES), jnp.float32),
            pltpu.VMEM((1, 2 * LANES), jnp.float32),
            pltpu.VMEM((2, 2 * cols, LANES), jnp.float32),
        ],
        cost_estimate=pl.CostEstimate(flops=10**6, bytes_accessed=10**5, transcendentals=0),
        compiler_params=pltpu.CompilerParams(vmem_limit_bytes=16 * 1024 * 1024),
    )(*operands)


def post_kernel(sides, *refs):
    n = len(sides)
    halo_own, halo_before = refs[:n], refs[n : 2 * n]
    free_rows, near, rim, keep, gain_v, tw, tb, sw, out = refs[2 * n : 9 + 2 * n]
    acts, ups, side, reach, corner, wide, bound_rows, free_sems, bound_sems = refs[9 + 2 * n :]
    ups_frames, cols = near.shape[2:4]
    rows = (free_rows.shape[0] + n) // 2
    frames = ups_frames // 2
    chans, c_out = sw.shape[3], sw.shape[2]
    span = n * cols
    padded = span + 16
    free, bound = rows_of(sides, rows)
    copies = []
    for k, (i, p, _) in enumerate(free):
        copies.append(pltpu.make_async_copy(free_rows.at[k], out.at[:, 2 * i + p], free_sems.at[k]))
        copies[-1].start()

    row = lax.axis_index("rows")
    gain = gain_v[...].reshape(1, -1)
    for f in range(2 * frames):
        halo, g = (halo_before, f) if f < frames else (halo_own, f - frames)
        parts = [halo[h][g * cols : (g + 1) * cols] for h in range(n)]
        corners = []
        for h in range(n):
            values = halo[h][frames * cols : frames * cols + 8].astype(jnp.float32)
            corners.append(pltpu.roll(values, 8 - g, 0) if g else values)
        parts.append(jnp.concatenate((corners * 2)[:2], axis=0))
        first = 0
        for part in parts:
            values = activate(part, gain)
            if f < frames:
                values = values * keep[...]
            acts[f, first : first + part.shape[0]] = values.astype(jnp.bfloat16)
            first += part.shape[0]
    stacked = time_conv(acts, tw, tb)
    for t in range(frames):
        for s in range(2):
            u = 2 * t + s
            lanes = slice(s * chans, (s + 1) * chans)
            ups[u] = stacked[t * padded : t * padded + span, lanes]
            beside = stacked[t * padded + span : (t + 1) * padded, lanes].astype(jnp.float32)
            for h in range(n):
                side[8 * h + u : 8 * h + u + 1] = beside[8 * h : 8 * h + 1]

    at_left, at_right, col_tap = column_sides()
    place = lax.broadcasted_iota(jnp.int32, (cols, LANES), 0)
    for h, where in enumerate(sides):
        if where == "either":
            tap, exists = jnp.where(row == 0, 2, 0), 1.0
        elif where == "above":
            tap, exists = 0, (row > 0).astype(jnp.float32)
        else:
            tap, exists = 2, (row < lax.axis_size("rows") - 1).astype(jnp.float32)
        x = ups[:, h * cols : (h + 1) * cols].reshape(ups_frames * cols, chans)
        for b in range(3):
            reach[b, :, :, :c_out] = dot_nt(x, sw[tap, b]).reshape(ups_frames, cols, c_out)
        x = side[8 * h : 8 * h + 8].astype(jnp.bfloat16)
        corner[:, :c_out] = dot_nt(x, sw[tap, col_tap])
        i, p = bound[h]
        for u in range(ups_frames):
            for half in range(2):
                lanes = slice(half * LANES, (half + 1) * LANES)
                close = [near[h, b, u, :, lanes] for b in range(3)]
                far = [reach[b, u, :, lanes] * exists for b in range(3)]
                line = rim[h, u : u + 1, lanes] + corner[u : u + 1, lanes] * exists
                even, odd = sums(close, far, line, at_left, at_right, place)
                wide[half, pl.ds(0, cols, 2)] = even
                wide[half, pl.ds(1, cols, 2)] = odd
            store_row(bound_rows, (h, u), wide, c_out)
            copies.append(
                pltpu.make_async_copy(bound_rows.at[h, u], out.at[u, 2 * i + p], bound_sems.at[h, u])
            )
            copies[-1].start()
    for copy in copies:
        copy.wait()


def post(sides, halo_own, halo_before, free_rows, near, rim, keep, gain, tw, tb, sw):
    n = len(sides)
    n_free, ups_frames, out_cols, c_out = free_rows.shape
    cols, chans = out_cols // 2, sw.shape[3]
    operands = (*halo_own, *halo_before, free_rows, near, rim, keep, gain, tw, tb, sw)
    return pl.pallas_call(
        functools.partial(post_kernel, sides),
        out_shape=jax.ShapeDtypeStruct((ups_frames, n_free + n, out_cols, c_out), jnp.bfloat16),
        in_specs=[VMEM] * len(operands),
        out_specs=pl.BlockSpec(memory_space=pl.ANY),
        scratch_shapes=[
            pltpu.VMEM((ups_frames, n * cols + 16, chans), jnp.bfloat16),
            pltpu.VMEM((ups_frames, n * cols, chans), jnp.bfloat16),
            pltpu.VMEM((8 * n, chans), jnp.float32),
            pltpu.VMEM((3, ups_frames, cols, 2 * LANES), jnp.float32),
            pltpu.VMEM((8, 2 * LANES), jnp.float32),
            pltpu.VMEM((2, out_cols, LANES), jnp.float32),
            pltpu.VMEM((n, ups_frames, out_cols, c_out), jnp.bfloat16),
            pltpu.SemaphoreType.DMA((n_free,)),
            pltpu.SemaphoreType.DMA((n, ups_frames)),
        ],
        compiler_params=pltpu.CompilerParams(vmem_limit_bytes=16 * 1024 * 1024),
    )(*operands)


def local(latent, norm_gain, time_weight, time_bias, space_weight, space_bias):
    frames, rows, cols, chans = latent.shape
    shards, n_rows, n_cols = (lax.axis_size(a) for a in ("tm", "rows", "cols"))
    axes = ("tm", "rows", "cols")

    def moved(x, route):
        pairs = []
        for t in range(shards):
            for r in range(n_rows):
                for c in range(n_cols):
                    t2, r2, c2 = route(t, r, c)
                    pairs.append(((t * n_rows + r) * n_cols + c, (t2 * n_rows + r2) * n_cols + c2))
        return lax.ppermute(x, axes, pairs)

    def onward(t, r, c, to):
        return (t + 1, *to) if t + 1 < shards else (0, r, 1 - c)

    def across(x):
        return moved(x, lambda t, r, c: (t, r, 1 - c))

    keep = keep_row(chans)
    beside = across(latent)
    before = moved(latent, lambda t, r, c: onward(t, r, c, (r, c)))
    after, beside = lax.optimization_barrier((latent, beside))
    tile = lax.dynamic_slice(
        after,
        (0, (rows - 1) * (1 - lax.axis_index("rows")), (cols - 8) * (1 - lax.axis_index("cols")), 0),
        (frames, 1, 8, chans),
    ).reshape(frames, 8, chans)
    corner = jnp.where(lax.axis_index("cols") == 0, tile[:, 7], tile[:, 0])
    edge_own, near = split(beside, jnp.pad(corner, ((0, 8 - frames), (0, 0))))
    if n_rows == 2:
        sides = ("either",)
        halo_before = (moved(near, lambda t, r, c: onward(t, r, c, (1 - r, 1 - c))),)
        halo_own = (moved(copied(near), lambda t, r, c: (t, 1 - r, 1 - c)),)
    else:
        sides = ("above", "below")

        def and_corner(x, edge, i):
            corner = edge[i * frames : (i + 1) * frames]
            return jnp.concatenate([x, corner, jnp.zeros((8 - frames, chans), x.dtype)], axis=0)

        def both(x, edge):
            last = and_corner(x[:, rows - 1].reshape(frames * cols, chans), edge, rows - 1)
            first = and_corner(x[:, 0].reshape(frames * cols, chans), edge, 0)
            return (
                moved(last, lambda t, r, c: (t, (r + 1) % n_rows, c)),
                moved(first, lambda t, r, c: (t, (r - 1) % n_rows, c)),
            )

        halo_own = both(latent, edge_own)
        halo_before = both(before, across(column_of(before)))

    gain, tw, tb, sb = norm_gain, time_weight, time_bias, space_bias
    sw = jnp.swapaxes(space_weight, 2, 3)
    ready, _ = lax.optimization_barrier((latent, edge_own))
    before, acts = lax.optimization_barrier((before, pre(ready, gain)))
    edge_before = across(column_of(before))
    taps = mid(before, acts, keep, gain, tw, tb, sw)
    free_rows, near, rim = partial_sums(sides, edge_own, edge_before, taps, keep, gain, tw, tb, sw, sb)
    return post(sides, halo_own, halo_before, free_rows, near, rim, keep, gain, tw, tb, sw)


def solution(mesh):
    in_specs = (P(("clips", "tm"), "rows", "cols", None), P(), P(), P(), P(), P())
    out_specs = P(("clips", "tm"), "rows", "cols", None)
    return jax.shard_map(local, mesh=mesh, in_specs=in_specs, out_specs=out_specs, check_vma=False)
```

time: 13.7 us -> 13.1 us (0.956)
  waiting for transfers between devices: 2.67 us -> 1.63 us
  other arithmetic: 0.84 us -> 0.01 us
  local copies, waits for them, and re-layouts: 0.04 us -> 0.8 us
  Pallas kernels: 3.73 us -> 4.38 us
  starting transfers between devices: 6.19 us -> 6.03 us
    pallas_call x0 -> x2, Pallas kernels: none -> 1.1 us  [the longest x1 1.09 us: partial_sums(): pl.pallas_call(functools.partial(sum_kernel, sides), out_shape=[jax.Shape...]
    ppermute x5, waiting for transfers between devices: 2.67 us -> 1.63 us  [moved(): return lax.ppermute(x, axes, pairs)]
    select_n x1, other arithmetic: 0.84 us -> 0.01 us  [local(): corner = jnp.where(lax.axis_index('cols') == 0, tile[:, 7], tile[:, 0])]
    dynamic_slice x0 -> x2, local copies, waits for them, and re-layouts: none -> 0.75 us  [local(): lax.dynamic_slice(after, (0, (rows - 1) * (1 - lax.axis_index('rows')), (...]
    pallas_call x1, Pallas kernels: 2.15 us -> 1.69 us  [post(): pl.pallas_call(functools.partial(post_kernel, sides), out_shape=jax.Shape...]
    ppermute x5, starting transfers between devices: 6.19 us -> 6.03 us  [moved(): return lax.ppermute(x, axes, pairs)]
  transfers between devices with their start and end apart: 5 -> 5, of which waited for: 3 -> 1; matrix products, arithmetic and copies ran while one was open for 6% -> 6% of each run, Pallas kernels for 12% -> 21%
where the time goes in v4:
time: 13.1 us; the launch traced here: 13 us
  starting transfers between devices  6.03 us (46%)
  Pallas kernels  4.38 us (33%)
  waiting for transfers between devices  1.63 us (12%)
  local copies, waits for them, and re-layouts  0.8 us (6%)
  between operations  0.14 us (1%)
    ppermute x5, starting transfers between devices, moved(): return lax.ppermute(x, axes, pairs)  6.03 us
    pallas_call x1, Pallas kernels, post(): pl.pallas_call(functools.partial(post_kernel, sides), out_shape=jax.Shape...  1.69 us
    ppermute x5, waiting for transfers between devices, moved(): return lax.ppermute(x, axes, pairs)  1.63 us
    pallas_call x1, Pallas kernels, mid(): pl.pallas_call(mid_kernel, out_shape=jax.ShapeDtypeStruct((3, 3, 2 * fram...  1.38 us
    pallas_call x1, Pallas kernels, partial_sums(): pl.pallas_call(functools.partial(sum_kernel, sides), out_shape=[jax.Shape...  1.09 us
    dynamic_slice x2, local copies, waits for them, and re-layouts, local(): lax.dynamic_slice(after, (0, (rows - 1) * (1 - lax.axis_index('rows')), (...  0.75 us
  transfers between devices with their start and end apart: 5, of which 1 were waited for; matrix products, arithmetic and copies ran while one was open for 6% of the time, Pallas kernels for 21%

profile of v4, /device:TPU:0, one launch (start us, length us, event | category | flops | bytes accessed | tf_op | source)
XLA Modules:
  0.0 13.0 jit_solution(9600170042798737560)
XLA Ops:
  0.0 0.5 %collective-permute-start = (bf16[2,2,32,384]{3,2,1,0:T(8,128)(2,1)}, bf16[2,2,32,384]{3,2,1,0:T(8,128)(2,1)S(1)}, u32[]{:S(2)}, u32[]{:S(2)}) collective-permute-start(bf16[2,2,32,384]{3,2,1,0:T(8,128)(2,1)} %own), channel_id=1, source_target_pairs={{0,1},{1,0},{2,3},{3,2},{4,5},{5,4},{6,7},{7,6},{8,9},{9,8},{10,11... | collective-permute-start | bytes 294920 | tf_op jit(solution)/shard_map/ppermute | solution.py:402
  0.5 2.6 %collective-permute-start.3 = (bf16[2,2,32,384]{3,2,1,0:T(8,128)(2,1)}, bf16[2,2,32,384]{3,2,1,0:T(8,128)(2,1)S(1)}, u32[]{:S(2)}, u32[]{:S(2)}) collective-permute-start(bf16[2,2,32,384]{3,2,1,0:T(8,128)(2,1)} %own), channel_id=1, source_target_pairs={{0,4},{1,5},{2,6},{3,7},{4,8},{5,9},{6,10},{7,11},{8,12},{9,13},{1... | collective-permute-start | bytes 294920 | tf_op jit(solution)/shard_map/ppermute | solution.py:402
  3.0 0.0 collective-permute-done.beside
  3.0 0.7 %constant_dynamic-slice_fusion = bf16[2,1,8,384]{3,2,1,0:T(8,128)(2,1)S(1)} fusion(bf16[2,2,32,384]{3,2,1,0:T(8,128)(2,1)} %own, s32[]{:T(128)S(6)} %select_n.18, s32[]{:T(128)S(6)} %select_n.19), kind=kLoop, calls=%fused_computation.3 | loop fusion | bytes 24584 | tf_op jit(solution)/shard_map/dynamic_slice | solution.py:414
  3.8 0.0 copy-start.2
  3.8 0.0 copy-start.4
  3.8 0.0 copy-start
  3.9 0.0 copy-start.1
  3.9 0.0 copy-start.3
  3.9 1.4 %collective-permute-start.1 = (bf16[72,384]{1,0:T(8,128)(2,1)S(1)}, bf16[72,384]{1,0:T(8,128)(2,1)S(1)}, u32[]{:S(2)}, u32[]{:S(2)}) collective-permute-start(bf16[72,384]{1,0:T(8,128)(2,1)S(1)} %shard_map.65), channel_id=1, source_target_pairs={{0,3},{1,2},{2,1},{3,0},{4,7},{5,6},{6,5},{7,4},{8,11},{9,10},{10,... | collective-permute-start | bytes 165896 | tf_op jit(solution)/shard_map/ppermute | solution.py:402
  5.3 1.4 %collective-permute-start.2 = (bf16[72,384]{1,0:T(8,128)(2,1)S(1)}, bf16[72,384]{1,0:T(8,128)(2,1)S(1)}, u32[]{:S(2)}, u32[]{:S(2)}) collective-permute-start(bf16[72,384]{1,0:T(8,128)(2,1)S(1)} %get-tuple-element.17.x), channel_id=1, source_target_pairs={{0,7},{1,6},{2,5},{3,4},{4,11},{5,10},{6,9},{7,8},{8,15},{9,14},{1... | collective-permute-start | bytes 165896 | tf_op jit(solution)/shard_map/ppermute | solution.py:402
  6.7 0.0 copy-done.2
  6.7 0.0 copy-done.4
  6.8 0.2 %shard_map.66.acts_own = bf16[2,64,384]{2,1,0:T(8,128)(2,1)S(1)} custom-call(bf16[2,2,32,384]{3,2,1,0:T(8,128)(2,1)S(1)} %copy-done.2, f32[384]{0:T(512)S(1)} %copy-done.4), custom_call_target="tpu_custom_call" | custom-call | flops 1000000 | bytes 100000 | tf_op jit(solution)/shard_map/pallas_call | solution.py:124
  6.9 1.6 %collective-permute-done.3.x.before = bf16[2,2,32,384]{3,2,1,0:T(8,128)(2,1)S(1)} collective-permute-done((bf16[2,2,32,384]{3,2,1,0:T(8,128)(2,1)}, bf16[2,2,32,384]{3,2,1,0:T(8,128)(2,1)S(1)}, u32[]{:S(2)}, u32[]{:S(2)}) %collective-permute-start.3) | collective-permute-done | bytes 98336 | tf_op jit(solution)/shard_map/ppermute | solution.py:402
  8.6 0.2 %collective-permute-start.4 = (bf16[8,384]{1,0:T(8,128)(2,1)S(1)}, bf16[8,384]{1,0:T(8,128)(2,1)S(1)}, u32[]{:S(2)}, u32[]{:S(2)}) collective-permute-start(bf16[8,384]{1,0:T(8,128)(2,1)S(1)} %shard_map.67), channel_id=1, source_target_pairs={{0,1},{1,0},{2,3},{3,2},{4,5},{5,4},{6,7},{7,6},{8,9},{9,8},{10,11... | collective-permute-start | bytes 18440 | tf_op jit(solution)/shard_map/ppermute | solution.py:402
  8.7 0.0 copy-done
  8.8 0.0 copy-done.1
  8.8 0.0 copy-done.3
  8.8 0.0 copy-start.5
  8.8 1.4 %shard_map.69.taps = f32[3,3,4,2,32,256]{5,4,3,2,1,0:T(8,128)S(1)} custom-call(bf16[2,2,32,384]{3,2,1,0:T(8,128)(2,1)S(1)} %collective-permute-done.3.x.before, bf16[2,64,384]{2,1,0:T(8,128)(2,1)S(1)} %shard_map.66.acts_own, f32[1,384]{1,0:T(1,128)S(1)} %shard_map.68.keep.refs_5_, f32[384]{0:T(512)S(1)} %copy-done.4, bf16[3,384,768]{2,1,0:T(8,128)(2,1)S(1)} %copy-done, ...), custom_call_target="tpu_custom_call" | custom-call | flops 1000000 | bytes 100000 | tf_op jit(solution)/shard_map/pallas_call | solution.py:156
  10.2 0.0 collective-permute-done.4.edge_before
  10.2 0.0 copy-done.5
  10.2 1.1 %shard_map.70 = (bf16[3,4,64,192]{3,2,1,0:T(8,128)(2,1)S(1)}, f32[1,3,4,32,256]{4,3,2,1,0:T(8,128)S(1)}, f32[1,8,256]{2,1,0:T(8,128)S(1)}) custom-call(bf16[8,384]{1,0:T(8,128)(2,1)S(1)} %get-tuple-element.18.edge_own, bf16[8,384]{1,0:T(8,128)(2,1)S(1)} %collective-permute-done.4.edge_before, f32[3,3,4,2,32,256]{5,4,3,2,1,0:T(8,128)S(1)} %shard_map.69.taps, ...), custom_call_target="tpu_custom_call" | custom-call | flops 1000000 | bytes 100000 | tf_op jit(solution)/shard_map/pallas_call | solution.py:266
  11.3 0.0 collective-permute-done.1.refs_0_
  11.3 0.0 collective-permute-done.2.refs_1_
  11.3 1.7 %shard_map.71 = bf16[4,4,64,192]{3,2,1,0:T(8,128)(2,1)} custom-call(bf16[72,384]{1,0:T(8,128)(2,1)S(1)} %collective-permute-done.1.refs_0_, bf16[72,384]{1,0:T(8,128)(2,1)S(1)} %collective-permute-done.2.refs_1_, bf16[3,4,64,192]{3,2,1,0:T(8,128)(2,1)S(1)} %get-tuple-element.22.refs_2_, f32[1,3,4,32,256]{4,3,2,1,0:T(8,128)S(1)} %get-tuple-element.23.refs_3_, ...), custom_call_target="tpu_custom_call" | custom-call | tf_op jit(solution)/shard_map/pallas_call | solution.py:370
  (7 shorter events, 0.1 us)
Async XLA Ops:
  0.0 3.0 %collective-permute-start = (bf16[2,2,32,384]{3,2,1,0:T(8,128)(2,1)}, bf16[2,2,32,384]{3,2,1,0:T(8,128)(2,1)S(1)}, u32[]{:S(2)}, u32[]{:S(2)}) collective-permute-start(bf16[2,2,32,384]{3,2,1,0:T(8,128)(2,1)} %own), channel_id=1, source_target_pairs={{0,1},{1,0},{2,3},{3,2},{4,5},{5,4},{6,7},{7,6},{8,9},{9,8},{10,11... | collective-permute-start | bytes 294920 | tf_op jit(solution)/shard_map/ppermute | solution.py:402
  0.5 8.1 %collective-permute-start.3 = (bf16[2,2,32,384]{3,2,1,0:T(8,128)(2,1)}, bf16[2,2,32,384]{3,2,1,0:T(8,128)(2,1)S(1)}, u32[]{:S(2)}, u32[]{:S(2)}) collective-permute-start(bf16[2,2,32,384]{3,2,1,0:T(8,128)(2,1)} %own), channel_id=1, source_target_pairs={{0,4},{1,5},{2,6},{3,7},{4,8},{5,9},{6,10},{7,11},{8,12},{9,13},{1... | collective-permute-start | bytes 294920 | tf_op jit(solution)/shard_map/ppermute | solution.py:402
  3.8 2.9 %copy-start.2 = (bf16[2,2,32,384]{3,2,1,0:T(8,128)(2,1)S(1)}, bf16[2,2,32,384]{3,2,1,0:T(8,128)(2,1)}, u32[]{:S(2)}) copy-start(bf16[2,2,32,384]{3,2,1,0:T(8,128)(2,1)} %own) | copy-start | bytes 294916
  3.8 2.9 %copy-start.4 = (f32[384]{0:T(512)S(1)}, f32[384]{0:T(512)}, u32[]{:S(2)}) copy-start(f32[384]{0:T(512)} %refs_6_.1) | copy-start | bytes 4612
  3.8 4.9 %copy-start = (bf16[3,384,768]{2,1,0:T(8,128)(2,1)S(1)}, bf16[3,384,768]{2,1,0:T(8,128)(2,1)}, u32[]{:S(2)}) copy-start(bf16[3,384,768]{2,1,0:T(8,128)(2,1)} %refs_7_.1) | copy-start | bytes 5308420
  3.9 4.9 %copy-start.1 = (bf16[3,3,384,192]{2,3,1,0:T(8,128)(2,1)S(1)}, bf16[3,3,384,192]{2,3,1,0:T(8,128)(2,1)}, u32[]{:S(2)}) copy-start(bf16[3,3,384,192]{2,3,1,0:T(8,128)(2,1)} %param.10) | copy-start | bytes 3981316
  3.9 4.9 %copy-start.3 = (f32[768]{0:T(1024)S(1)}, f32[768]{0:T(1024)}, u32[]{:S(2)}) copy-start(f32[768]{0:T(1024)} %refs_8_.1) | copy-start | bytes 9220
  3.9 7.4 %collective-permute-start.1 = (bf16[72,384]{1,0:T(8,128)(2,1)S(1)}, bf16[72,384]{1,0:T(8,128)(2,1)S(1)}, u32[]{:S(2)}, u32[]{:S(2)}) collective-permute-start(bf16[72,384]{1,0:T(8,128)(2,1)S(1)} %shard_map.65), channel_id=1, source_target_pairs={{0,3},{1,2},{2,1},{3,0},{4,7},{5,6},{6,5},{7,4},{8,11},{9,10},{10,... | collective-permute-start | bytes 165896 | tf_op jit(solution)/shard_map/ppermute | solution.py:402
  5.3 6.0 %collective-permute-start.2 = (bf16[72,384]{1,0:T(8,128)(2,1)S(1)}, bf16[72,384]{1,0:T(8,128)(2,1)S(1)}, u32[]{:S(2)}, u32[]{:S(2)}) collective-permute-start(bf16[72,384]{1,0:T(8,128)(2,1)S(1)} %get-tuple-element.17.x), channel_id=1, source_target_pairs={{0,7},{1,6},{2,5},{3,4},{4,11},{5,10},{6,9},{7,8},{8,15},{9,14},{1... | collective-permute-start | bytes 165896 | tf_op jit(solution)/shard_map/ppermute | solution.py:402
  8.6 1.6 %collective-permute-start.4 = (bf16[8,384]{1,0:T(8,128)(2,1)S(1)}, bf16[8,384]{1,0:T(8,128)(2,1)S(1)}, u32[]{:S(2)}, u32[]{:S(2)}) collective-permute-start(bf16[8,384]{1,0:T(8,128)(2,1)S(1)} %shard_map.67), channel_id=1, source_target_pairs={{0,1},{1,0},{2,3},{3,2},{4,5},{5,4},{6,7},{7,6},{8,9},{9,8},{10,11... | collective-permute-start | bytes 18440 | tf_op jit(solution)/shard_map/ppermute | solution.py:402
  8.8 1.4 %copy-start.5 = (f32[192]{0:T(256)S(1)}, f32[192]{0:T(256)}, u32[]{:S(2)}) copy-start(f32[192]{0:T(256)} %sb.1) | copy-start | bytes 2308

commit v5 on v4

--- a/solution.py
+++ b/solution.py
@@ -30,19 +30,6 @@
     )
     summed = jnp.dot(window, tw[...].reshape(3 * chans, 2 * chans), preferred_element_type=jnp.float32)
     return (summed + tb[...].reshape(1, -1)).astype(jnp.bfloat16)
-
-
-def keep_kernel(keep):
-    keep[...] = jnp.full(keep.shape, (lax.axis_index("tm") > 0).astype(jnp.float32))
-
-
-def keep_row(chans):
-    return pl.pallas_call(
-        keep_kernel,
-        out_shape=jax.ShapeDtypeStruct((1, chans), jnp.float32),
-        out_specs=VMEM,
-        compiler_params=SMALL,
-    )()
 
 
 def put_column(x, last, out):
@@ -111,60 +98,26 @@
     )(x)
 
 
-def pre_kernel(own, gain_v, acts):
-    frames, rows, cols, _ = own.shape
-    g = gain_v[...].reshape(1, -1)
-    for f in range(frames):
-        for i in range(rows):
-            acts[f, i * cols : (i + 1) * cols] = activate(own[f, i], g).astype(jnp.bfloat16)
-
-
-def pre(own, gain):
-    frames, rows, cols, chans = own.shape
-    return pl.pallas_call(
-        pre_kernel,
-        out_shape=jax.ShapeDtypeStruct((frames, rows * cols, chans), jnp.bfloat16),
-        in_specs=[VMEM] * 2,
-        out_specs=VMEM,
-        cost_estimate=pl.CostEstimate(flops=10**6, bytes_accessed=10**5, transcendentals=0),
-        compiler_params=SMALL,
-    )(own, gain)
-
-
-def mid_kernel(before, acts_own, keep, gain_v, tw, tb, sw, taps, acts, ups):
-    frames, rows, cols, chans = before.shape
+def on_first_shard():
+    return lax.axis_index("tm") == 0
+
+
+def own_taps(acts, tw, tb, sw, ups, taps):
+    ups_frames, rows, cols = taps.shape[2:5]
     body = rows * cols
-    c_out = sw.shape[2]
-    g = gain_v[...].reshape(1, -1)
-    for f in range(frames):
-        for i in range(rows):
-            at = slice(i * cols, (i + 1) * cols)
-            acts[f, at] = (activate(before[f, i], g) * keep[...]).astype(jnp.bfloat16)
-    acts[frames:] = acts_own[...]
+    chans, c_out = sw.shape[3], sw.shape[2]
     stacked = time_conv(acts, tw, tb)
-    for t in range(frames):
+    for t in range(ups_frames // 2):
         for s in range(2):
             ups[2 * t + s] = stacked[t * body : (t + 1) * body, s * chans : (s + 1) * chans]
     for a in range(3):
         for b in range(3):
-            product = dot_nt(ups[...].reshape(2 * frames * body, chans), sw[a, b])
-            taps[a, b, :, :, :, :c_out] = product.reshape(2 * frames, rows, cols, c_out)
-
-
-def mid(before, acts_own, keep, gain, tw, tb, sw):
-    frames, rows, cols, chans = before.shape
-    return pl.pallas_call(
-        mid_kernel,
-        out_shape=jax.ShapeDtypeStruct((3, 3, 2 * frames, rows, cols, 2 * LANES), jnp.float32),
-        in_specs=[VMEM] * 7,
-        out_specs=VMEM,
-        scratch_shapes=[
-            pltpu.VMEM((2 * frames, rows * cols, chans), jnp.bfloat16),
-            pltpu.VMEM((2 * frames, rows * cols, chans), jnp.bfloat16),
-        ],
-        cost_estimate=pl.CostEstimate(flops=10**6, bytes_accessed=10**5, transcendentals=0),
-        compiler_params=pltpu.CompilerParams(vmem_limit_bytes=16 * 1024 * 1024),
-    )(before, acts_own, keep, gain, tw, tb, sw)
+            product = dot_nt(ups[...].reshape(ups_frames * body, chans), sw[a, b])
+            taps[a, b, :, :, :, :c_out] = product.reshape(ups_frames, rows, cols, c_out)
+
+
+def taps_shape(frames, rows, cols):
+    return (3, 3, 2 * frames, rows, cols, 2 * LANES)
 
 
 def sums(near, far, border, at_left, at_right, place):
@@ -204,21 +157,17 @@
     return free, bound
 
 
-def sum_kernel(sides, edge_own, edge_before, taps, keep, gain_v, tw, tb, sw, sb, free_rows, near, rim, *scratch):
-    edges, acts, side, border, shift, wide = scratch
+def put_edge(edges, acts, f, edge, g, rows, frames, gain):
+    values = edge[...].astype(jnp.float32)
+    for i in range(rows):
+        edges[f, i : i + 1] = values[i * frames + g : i * frames + g + 1]
+    acts[f] = activate(edges[f], gain).astype(jnp.bfloat16)
+
+
+def row_sums(sides, acts, taps, tw, tb, sw, sb, free_rows, near, rim, side, border, shift, wide):
     ups_frames, rows, cols = taps.shape[2:5]
     frames = ups_frames // 2
     chans, c_out = sw.shape[3], sw.shape[2]
-    gain = gain_v[...].reshape(1, -1)
-    for f in range(2 * frames):
-        edge, g = (edge_before, f) if f < frames else (edge_own, f - frames)
-        values = edge[...].astype(jnp.float32)
-        for i in range(rows):
-            edges[f, i : i + 1] = values[i * frames + g : i * frames + g + 1]
-        values = activate(edges[f], gain)
-        if f < frames:
-            values = values * keep[...]
-        acts[f] = values.astype(jnp.bfloat16)
     stacked = time_conv(acts, tw, tb)
     for t in range(frames):
         for s in range(2):
@@ -258,38 +207,138 @@
                 near[k, b, u] = close + shift[...] if b == 1 else close
 
 
-def partial_sums(sides, edge_own, edge_before, taps, keep, gain, tw, tb, sw, sb):
+def sums_shapes(sides, frames, rows, cols, c_out):
+    n = len(sides)
+    return [
+        jax.ShapeDtypeStruct((2 * rows - n, 2 * frames, 2 * cols, c_out), jnp.bfloat16),
+        jax.ShapeDtypeStruct((n, 3, 2 * frames, cols, 2 * LANES), jnp.float32),
+        jax.ShapeDtypeStruct((n, 8, 2 * LANES), jnp.float32),
+    ]
+
+
+def sums_scratch(frames, rows, cols, chans):
+    return [
+        pltpu.VMEM((2 * frames, 16, chans), jnp.float32),
+        pltpu.VMEM((2 * frames, 16, chans), jnp.bfloat16),
+        pltpu.VMEM((8 * rows, chans), jnp.float32),
+        pltpu.VMEM((3, rows, 8, 2 * LANES), jnp.float32),
+        pltpu.VMEM((1, 2 * LANES), jnp.float32),
+        pltpu.VMEM((2, 2 * cols, LANES), jnp.float32),
+    ]
+
+
+def sum_kernel(sides, edge_own, edge_before, taps, gain_v, tw, tb, sw, sb, free_rows, near, rim, edges, acts, *scratch):
+    ups_frames, rows, _ = taps.shape[2:5]
+    frames = ups_frames // 2
+
+    @pl.when(jnp.logical_not(on_first_shard()))
+    def _():
+        gain = gain_v[...].reshape(1, -1)
+        for f in range(frames):
+            put_edge(edges, acts, f, edge_before, f, rows, frames, gain)
+            put_edge(edges, acts, frames + f, edge_own, f, rows, frames, gain)
+        row_sums(sides, acts, taps, tw, tb, sw, sb, free_rows, near, rim, *scratch)
+
+
+def partial_sums(sides, edge_own, edge_before, taps, gain, tw, tb, sw, sb):
     ups_frames, rows, cols = taps.shape[2:5]
+    frames = ups_frames // 2
     chans, c_out = sw.shape[3], sw.shape[2]
-    n_bound = len(sides)
-    operands = (edge_own, edge_before, taps, keep, gain, tw, tb, sw, sb)
+    operands = (edge_own, edge_before, taps, gain, tw, tb, sw, sb)
     return pl.pallas_call(
         functools.partial(sum_kernel, sides),
+        out_shape=sums_shapes(sides, frames, rows, cols, c_out),
+        in_specs=[VMEM] * len(operands),
+        out_specs=[VMEM] * 3,
+        scratch_shapes=sums_scratch(frames, rows, cols, chans),
+        cost_estimate=pl.CostEstimate(flops=10**6, bytes_accessed=10**5, transcendentals=0),
+        compiler_params=pltpu.CompilerParams(vmem_limit_bytes=16 * 1024 * 1024),
+    )(*operands)
+
+
+def early_kernel(own, gain_v, tw, tb, sw, acts_own, taps, acts, ups):
+    frames, rows, cols, _ = own.shape
+    gain = gain_v[...].reshape(1, -1)
+    for f in range(frames):
+        for i in range(rows):
+            acts_own[f, i * cols : (i + 1) * cols] = activate(own[f, i], gain).astype(jnp.bfloat16)
+
+    @pl.when(on_first_shard())
+    def _():
+        acts[:frames] = jnp.zeros((frames, *acts.shape[1:]), acts.dtype)
+        acts[frames:] = acts_own[...]
+        own_taps(acts, tw, tb, sw, ups, taps)
+
+
+def early(own, gain, tw, tb, sw):
+    frames, rows, cols, chans = own.shape
+    operands = (own, gain, tw, tb, sw)
+    return pl.pallas_call(
+        early_kernel,
         out_shape=[
-            jax.ShapeDtypeStruct((2 * rows - n_bound, ups_frames, 2 * cols, c_out), jnp.bfloat16),
-            jax.ShapeDtypeStruct((n_bound, 3, ups_frames, cols, 2 * LANES), jnp.float32),
-            jax.ShapeDtypeStruct((n_bound, 8, 2 * LANES), jnp.float32),
+            jax.ShapeDtypeStruct((frames, rows * cols, chans), jnp.bfloat16),
+            jax.ShapeDtypeStruct(taps_shape(frames, rows, cols), jnp.float32),
         ],
         in_specs=[VMEM] * len(operands),
-        out_specs=[VMEM] * 3,
+        out_specs=[VMEM] * 2,
         scratch_shapes=[
-            pltpu.VMEM((ups_frames, 16, chans), jnp.float32),
-            pltpu.VMEM((ups_frames, 16, chans), jnp.bfloat16),
-            pltpu.VMEM((8 * rows, chans), jnp.float32),
-            pltpu.VMEM((3, rows, 8, 2 * LANES), jnp.float32),
-            pltpu.VMEM((1, 2 * LANES), jnp.float32),
-            pltpu.VMEM((2, 2 * cols, LANES), jnp.float32),
+            pltpu.VMEM((2 * frames, rows * cols, chans), jnp.bfloat16),
+            pltpu.VMEM((2 * frames, rows * cols, chans), jnp.bfloat16),
         ],
         cost_estimate=pl.CostEstimate(flops=10**6, bytes_accessed=10**5, transcendentals=0),
         compiler_params=pltpu.CompilerParams(vmem_limit_bytes=16 * 1024 * 1024),
     )(*operands)
 
 
+def mid_kernel(
+    sides, before, acts_own, taps_first, edge_own, gain_v, tw, tb, sw, sb, taps, free_rows, near, rim, acts, ups, *scratch
+):
+    frames, rows, cols, _ = before.shape
+    gain = gain_v[...].reshape(1, -1)
+
+    @pl.when(on_first_shard())
+    def _():
+        edges, edge_acts, *others = scratch
+        edge_acts[:frames] = jnp.zeros((frames, *edge_acts.shape[1:]), edge_acts.dtype)
+        for f in range(frames):
+            put_edge(edges, edge_acts, frames + f, edge_own, f, rows, frames, gain)
+        row_sums(sides, edge_acts, taps_first, tw, tb, sw, sb, free_rows, near, rim, *others)
+
+    @pl.when(jnp.logical_not(on_first_shard()))
+    def _():
+        for f in range(frames):
+            for i in range(rows):
+                acts[f, i * cols : (i + 1) * cols] = activate(before[f, i], gain).astype(jnp.bfloat16)
+        acts[frames:] = acts_own[...]
+        own_taps(acts, tw, tb, sw, ups, taps)
+
+
+def mid(sides, before, acts_own, taps_first, edge_own, gain, tw, tb, sw, sb):
+    frames, rows, cols, chans = before.shape
+    operands = (before, acts_own, taps_first, edge_own, gain, tw, tb, sw, sb)
+    return pl.pallas_call(
+        functools.partial(mid_kernel, sides),
+        out_shape=[
+            jax.ShapeDtypeStruct(taps_shape(frames, rows, cols), jnp.float32),
+            *sums_shapes(sides, frames, rows, cols, sb.shape[0]),
+        ],
+        in_specs=[VMEM] * len(operands),
+        out_specs=[VMEM] * 4,
+        scratch_shapes=[
+            pltpu.VMEM((2 * frames, rows * cols, chans), jnp.bfloat16),
+            pltpu.VMEM((2 * frames, rows * cols, chans), jnp.bfloat16),
+            *sums_scratch(frames, rows, cols, chans),
+        ],
+        cost_estimate=pl.CostEstimate(flops=10**6, bytes_accessed=10**5, transcendentals=0),
+        compiler_params=pltpu.CompilerParams(vmem_limit_bytes=16 * 1024 * 1024),
+    )(*operands)
+
+
 def post_kernel(sides, *refs):
     n = len(sides)
     halo_own, halo_before = refs[:n], refs[n : 2 * n]
-    free_rows, near, rim, keep, gain_v, tw, tb, sw, out = refs[2 * n : 9 + 2 * n]
-    acts, ups, side, reach, corner, wide, bound_rows, free_sems, bound_sems = refs[9 + 2 * n :]
+    free_first, near_first, rim_first, free_rows, near, rim, gain_v, tw, tb, sw, out = refs[2 * n : 11 + 2 * n]
+    acts, ups, side, reach, corner, wide, bound_rows, free_sems, bound_sems = refs[11 + 2 * n :]
     ups_frames, cols = near.shape[2:4]
     rows = (free_rows.shape[0] + n) // 2
     frames = ups_frames // 2
@@ -297,10 +346,14 @@
     span = n * cols
     padded = span + 16
     free, bound = rows_of(sides, rows)
+    first_shard = on_first_shard()
+    not_first = jnp.logical_not(first_shard).astype(jnp.float32)
     copies = []
     for k, (i, p, _) in enumerate(free):
-        copies.append(pltpu.make_async_copy(free_rows.at[k], out.at[:, 2 * i + p], free_sems.at[k]))
-        copies[-1].start()
+        target = out.at[:, 2 * i + p]
+        copies.append(pltpu.make_async_copy(free_rows.at[k], target, free_sems.at[k]))
+        pl.when(jnp.logical_not(first_shard))(copies[-1].start)
+        pl.when(first_shard)(pltpu.make_async_copy(free_first.at[k], target, free_sems.at[k]).start)
 
     row = lax.axis_index("rows")
     gain = gain_v[...].reshape(1, -1)
@@ -316,7 +369,7 @@
         for part in parts:
             values = activate(part, gain)
             if f < frames:
-                values = values * keep[...]
+                values = values * not_first
             acts[f, first : first + part.shape[0]] = values.astype(jnp.bfloat16)
             first += part.shape[0]
     stacked = time_conv(acts, tw, tb)
@@ -347,9 +400,10 @@
         for u in range(ups_frames):
             for half in range(2):
                 lanes = slice(half * LANES, (half + 1) * LANES)
-                close = [near[h, b, u, :, lanes] for b in range(3)]
+                close = [jnp.where(first_shard, near_first[h, b, u, :, lanes], near[h, b, u, :, lanes]) for b in range(3)]
                 far = [reach[b, u, :, lanes] * exists for b in range(3)]
-                line = rim[h, u : u + 1, lanes] + corner[u : u + 1, lanes] * exists
+                line = jnp.where(first_shard, rim_first[h, u : u + 1, lanes], rim[h, u : u + 1, lanes])
+                line = line + corner[u : u + 1, lanes] * exists
                 even, odd = sums(close, far, line, at_left, at_right, place)
                 wide[half, pl.ds(0, cols, 2)] = even
                 wide[half, pl.ds(1, cols, 2)] = odd
@@ -362,11 +416,11 @@
         copy.wait()
 
 
-def post(sides, halo_own, halo_before, free_rows, near, rim, keep, gain, tw, tb, sw):
+def post(sides, halo_own, halo_before, first, rest, gain, tw, tb, sw):
     n = len(sides)
-    n_free, ups_frames, out_cols, c_out = free_rows.shape
+    n_free, ups_frames, out_cols, c_out = rest[0].shape
     cols, chans = out_cols // 2, sw.shape[3]
-    operands = (*halo_own, *halo_before, free_rows, near, rim, keep, gain, tw, tb, sw)
+    operands = (*halo_own, *halo_before, *first, *rest, gain, tw, tb, sw)
     return pl.pallas_call(
         functools.partial(post_kernel, sides),
         out_shape=jax.ShapeDtypeStruct((ups_frames, n_free + n, out_cols, c_out), jnp.bfloat16),
@@ -407,7 +461,6 @@
     def across(x):
         return moved(x, lambda t, r, c: (t, r, 1 - c))
 
-    keep = keep_row(chans)
     beside = across(latent)
     before = moved(latent, lambda t, r, c: onward(t, r, c, (r, c)))
     after, beside = lax.optimization_barrier((latent, beside))
@@ -420,8 +473,8 @@
     edge_own, near = split(beside, jnp.pad(corner, ((0, 8 - frames), (0, 0))))
     if n_rows == 2:
         sides = ("either",)
-        halo_before = (moved(near, lambda t, r, c: onward(t, r, c, (1 - r, 1 - c))),)
-        halo_own = (moved(copied(near), lambda t, r, c: (t, 1 - r, 1 - c)),)
+        halo_before = (moved(copied(near), lambda t, r, c: onward(t, r, c, (1 - r, 1 - c))),)
+        halo_own = (moved(near, lambda t, r, c: (t, 1 - r, 1 - c)),)
     else:
         sides = ("above", "below")
 
@@ -443,11 +496,12 @@
     gain, tw, tb, sb = norm_gain, time_weight, time_bias, space_bias
     sw = jnp.swapaxes(space_weight, 2, 3)
     ready, _ = lax.optimization_barrier((latent, edge_own))
-    before, acts = lax.optimization_barrier((before, pre(ready, gain)))
+    acts, taps = early(ready, gain, tw, tb, sw)
+    before, acts = lax.optimization_barrier((before, acts))
     edge_before = across(column_of(before))
-    taps = mid(before, acts, keep, gain, tw, tb, sw)
-    free_rows, near, rim = partial_sums(sides, edge_own, edge_before, taps, keep, gain, tw, tb, sw, sb)
-    return post(sides, halo_own, halo_before, free_rows, near, rim, keep, gain, tw, tb, sw)
+    taps, *first = mid(sides, before, acts, taps, edge_own, gain, tw, tb, sw, sb)
+    rest = partial_sums(sides, edge_own, edge_before, taps, gain, tw, tb, sw, sb)
+    return post(sides, halo_own, halo_before, first, rest, gain, tw, tb, sw)
 
 
 def solution(mesh):

time: 13.1 us -> 12 us (0.916)
  waiting for transfers between devices: 1.63 us -> 0.64 us
  Pallas kernels: 4.38 us -> 4.22 us
    ppermute x5, waiting for transfers between devices: 1.63 us -> 0.64 us  [moved(): return lax.ppermute(x, axes, pairs)]
    pallas_call x4 -> x3, Pallas kernels: 2.64 us -> 2.46 us  [the longest x1 1.41 us: early(): pl.pallas_call(early_kernel, out_shape=[jax.ShapeDtypeStruct((frames, row...]
  transfers between devices with their start and end apart: 5 -> 5, of which waited for: 1 -> 2; matrix products, arithmetic and copies ran while one was open for 6% -> 7% of each run, Pallas kernels for 21% -> 21%
where the time goes in v5:
time: 12 us; the launch traced here: 11.8 us
  starting transfers between devices  6.02 us (50%)
  Pallas kernels  4.22 us (35%)
  local copies, waits for them, and re-layouts  0.8 us (7%)
  waiting for transfers between devices  0.64 us (5%)
  between operations  0.13 us (1%)
    ppermute x5, starting transfers between devices, moved(): return lax.ppermute(x, axes, pairs)  6.02 us
    pallas_call x1, Pallas kernels, post(): pl.pallas_call(functools.partial(post_kernel, sides), out_shape=jax.Shape...  1.7 us
    pallas_call x1, Pallas kernels, early(): pl.pallas_call(early_kernel, out_shape=[jax.ShapeDtypeStruct((frames, row...  1.41 us
    pallas_call x1, Pallas kernels, mid(): pl.pallas_call(functools.partial(mid_kernel, sides), out_shape=[jax.Shape...  1.04 us
    dynamic_slice x2, local copies, waits for them, and re-layouts, local(): lax.dynamic_slice(after, (0, (rows - 1) * (1 - lax.axis_index('rows')), (...  0.75 us
    ppermute x5, waiting for transfers between devices, moved(): return lax.ppermute(x, axes, pairs)  0.64 us
  transfers between devices with their start and end apart: 5, of which 2 were waited for; matrix products, arithmetic and copies ran while one was open for 7% of the time, Pallas kernels for 21%

profile of v5, /device:TPU:0, one launch (start us, length us, event | category | flops | bytes accessed | tf_op | source)
XLA Modules:
  0.0 11.8 jit_solution(6652290411657962493)
XLA Ops:
  0.0 0.5 %collective-permute-start = (bf16[2,2,32,384]{3,2,1,0:T(8,128)(2,1)}, bf16[2,2,32,384]{3,2,1,0:T(8,128)(2,1)S(1)}, u32[]{:S(2)}, u32[]{:S(2)}) collective-permute-start(bf16[2,2,32,384]{3,2,1,0:T(8,128)(2,1)} %own), channel_id=1, source_target_pairs={{0,1},{1,0},{2,3},{3,2},{4,5},{5,4},{6,7},{7,6},{8,9},{9,8},{10,11... | collective-permute-start | bytes 294920 | tf_op jit(solution)/shard_map/ppermute | solution.py:456
  0.5 2.6 %collective-permute-start.3 = (bf16[2,2,32,384]{3,2,1,0:T(8,128)(2,1)}, bf16[2,2,32,384]{3,2,1,0:T(8,128)(2,1)S(1)}, u32[]{:S(2)}, u32[]{:S(2)}) collective-permute-start(bf16[2,2,32,384]{3,2,1,0:T(8,128)(2,1)} %own), channel_id=1, source_target_pairs={{0,4},{1,5},{2,6},{3,7},{4,8},{5,9},{6,10},{7,11},{8,12},{9,13},{1... | collective-permute-start | bytes 294920 | tf_op jit(solution)/shard_map/ppermute | solution.py:456
  3.0 0.0 collective-permute-done.beside
  3.0 0.7 %constant_dynamic-slice_fusion = bf16[2,1,8,384]{3,2,1,0:T(8,128)(2,1)S(1)} fusion(bf16[2,2,32,384]{3,2,1,0:T(8,128)(2,1)} %own, s32[]{:T(128)S(6)} %select_n.18, s32[]{:T(128)S(6)} %select_n.19), kind=kLoop, calls=%fused_computation.3 | loop fusion | bytes 24584 | tf_op jit(solution)/shard_map/dynamic_slice | solution.py:467
  3.8 0.0 copy-start
  3.8 0.0 copy-start.1
  3.8 0.0 copy-start.2
  3.9 0.0 copy-start.3
  3.9 0.0 copy-start.4
  3.9 0.0 copy-start.5
  3.9 2.4 %collective-permute-start.2 = (bf16[72,384]{1,0:T(8,128)(2,1)S(1)}, bf16[72,384]{1,0:T(8,128)(2,1)S(1)}, u32[]{:S(2)}, u32[]{:S(2)}) collective-permute-start(bf16[72,384]{1,0:T(8,128)(2,1)S(1)} %shard_map.65), channel_id=1, source_target_pairs={{0,7},{1,6},{2,5},{3,4},{4,11},{5,10},{6,9},{7,8},{8,15},{9,14},{1... | collective-permute-start | bytes 165896 | tf_op jit(solution)/shard_map/ppermute | solution.py:456
  6.3 0.4 %collective-permute-start.1 = (bf16[72,384]{1,0:T(8,128)(2,1)S(1)}, bf16[72,384]{1,0:T(8,128)(2,1)S(1)}, u32[]{:S(2)}, u32[]{:S(2)}) collective-permute-start(bf16[72,384]{1,0:T(8,128)(2,1)S(1)} %get-tuple-element.23.x), channel_id=1, source_target_pairs={{0,3},{1,2},{2,1},{3,0},{4,7},{5,6},{6,5},{7,4},{8,11},{9,10},{10,... | collective-permute-start | bytes 165896 | tf_op jit(solution)/shard_map/ppermute | solution.py:456
  6.7 0.0 copy-done
  6.7 0.0 copy-done.1
  6.8 0.0 copy-done.2
  6.8 0.0 copy-done.3
  6.8 0.0 copy-done.4
  6.8 1.4 %shard_map.66 = (bf16[2,64,384]{2,1,0:T(8,128)(2,1)S(1)}, f32[3,3,4,2,32,256]{5,4,3,2,1,0:T(8,128)S(1)}) custom-call(bf16[2,2,32,384]{3,2,1,0:T(8,128)(2,1)S(1)} %copy-done.2, f32[384]{0:T(512)S(1)} %copy-done.4, bf16[3,384,768]{2,1,0:T(8,128)(2,1)S(1)} %copy-done, f32[768]{0:T(1024)S(1)} %copy-done.3, bf16[3,3,192,384]{3,2,1,0:T(8,128)(2,1)S(1)} %bitcast.6), custom_call_target="tpu_custom_call" | custom-call | flops 1000000 | bytes 100000 | tf_op jit(solution)/shard_map/pallas_call | solution.py:276
  8.2 0.4 %collective-permute-done.3.before.x = bf16[2,2,32,384]{3,2,1,0:T(8,128)(2,1)S(1)} collective-permute-done((bf16[2,2,32,384]{3,2,1,0:T(8,128)(2,1)}, bf16[2,2,32,384]{3,2,1,0:T(8,128)(2,1)S(1)}, u32[]{:S(2)}, u32[]{:S(2)}) %collective-permute-start.3) | collective-permute-done | bytes 98336 | tf_op jit(solution)/shard_map/ppermute | solution.py:456
  8.6 0.2 %collective-permute-start.4 = (bf16[8,384]{1,0:T(8,128)(2,1)S(1)}, bf16[8,384]{1,0:T(8,128)(2,1)S(1)}, u32[]{:S(2)}, u32[]{:S(2)}) collective-permute-start(bf16[8,384]{1,0:T(8,128)(2,1)S(1)} %shard_map.68), channel_id=1, source_target_pairs={{0,1},{1,0},{2,3},{3,2},{4,5},{5,4},{6,7},{7,6},{8,9},{9,8},{10,11... | collective-permute-start | bytes 18440 | tf_op jit(solution)/shard_map/ppermute | solution.py:456
  8.7 0.0 copy-done.5
  8.7 1.0 %shard_map.67 = (f32[3,3,4,2,32,256]{5,4,3,2,1,0:T(8,128)S(1)}, bf16[3,4,64,192]{3,2,1,0:T(8,128)(2,1)S(1)}, f32[1,3,4,32,256]{4,3,2,1,0:T(8,128)S(1)}, f32[1,8,256]{2,1,0:T(8,128)S(1)}) custom-call(bf16[2,2,32,384]{3,2,1,0:T(8,128)(2,1)S(1)} %collective-permute-done.3.before.x, bf16[2,64,384]{2,1,0:T(8,128)(2,1)S(1)} %get-tuple-element.28.acts_own, ...), custom_call_target="tpu_custom_call" | custom-call | flops 1000000 | bytes 100000 | tf_op jit(solution)/shard_map/pallas_call | solution.py:319
  9.8 0.0 collective-permute-done.4.edge_before
  9.8 0.0 collective-permute-done.2.refs_1_
  9.8 0.3 %collective-permute-done.1.refs_0_ = bf16[72,384]{1,0:T(8,128)(2,1)S(1)} collective-permute-done((bf16[72,384]{1,0:T(8,128)(2,1)S(1)}, bf16[72,384]{1,0:T(8,128)(2,1)S(1)}, u32[]{:S(2)}, u32[]{:S(2)}) %collective-permute-start.1) | collective-permute-done | bytes 55328 | tf_op jit(solution)/shard_map/ppermute | solution.py:456
  10.1 1.7 %shard_map.70 = bf16[4,4,64,192]{3,2,1,0:T(8,128)(2,1)} custom-call(bf16[72,384]{1,0:T(8,128)(2,1)S(1)} %collective-permute-done.1.refs_0_, bf16[72,384]{1,0:T(8,128)(2,1)S(1)} %collective-permute-done.2.refs_1_, bf16[3,4,64,192]{3,2,1,0:T(8,128)(2,1)S(1)} %get-tuple-element.30.refs_2_, f32[1,3,4,32,256]{4,3,2,1,0:T(8,128)S(1)} %get-tuple-element.31.refs_3_, ...), custom_call_target="tpu_custom_call" | custom-call | tf_op jit(solution)/shard_map/pallas_call | solution.py:424
  (7 shorter events, 0.1 us)
Async XLA Ops:
  0.0 3.0 %collective-permute-start = (bf16[2,2,32,384]{3,2,1,0:T(8,128)(2,1)}, bf16[2,2,32,384]{3,2,1,0:T(8,128)(2,1)S(1)}, u32[]{:S(2)}, u32[]{:S(2)}) collective-permute-start(bf16[2,2,32,384]{3,2,1,0:T(8,128)(2,1)} %own), channel_id=1, source_target_pairs={{0,1},{1,0},{2,3},{3,2},{4,5},{5,4},{6,7},{7,6},{8,9},{9,8},{10,11... | collective-permute-start | bytes 294920 | tf_op jit(solution)/shard_map/ppermute | solution.py:456
  0.5 8.1 %collective-permute-start.3 = (bf16[2,2,32,384]{3,2,1,0:T(8,128)(2,1)}, bf16[2,2,32,384]{3,2,1,0:T(8,128)(2,1)S(1)}, u32[]{:S(2)}, u32[]{:S(2)}) collective-permute-start(bf16[2,2,32,384]{3,2,1,0:T(8,128)(2,1)} %own), channel_id=1, source_target_pairs={{0,4},{1,5},{2,6},{3,7},{4,8},{5,9},{6,10},{7,11},{8,12},{9,13},{1... | collective-permute-start | bytes 294920 | tf_op jit(solution)/shard_map/ppermute | solution.py:456
  3.8 2.9 %copy-start = (bf16[3,384,768]{2,1,0:T(8,128)(2,1)S(1)}, bf16[3,384,768]{2,1,0:T(8,128)(2,1)}, u32[]{:S(2)}) copy-start(bf16[3,384,768]{2,1,0:T(8,128)(2,1)} %refs_9_.1) | copy-start | bytes 5308420
  3.8 2.9 %copy-start.1 = (bf16[3,3,384,192]{2,3,1,0:T(8,128)(2,1)S(1)}, bf16[3,3,384,192]{2,3,1,0:T(8,128)(2,1)}, u32[]{:S(2)}) copy-start(bf16[3,3,384,192]{2,3,1,0:T(8,128)(2,1)} %param.10) | copy-start | bytes 3981316
  3.8 2.9 %copy-start.2 = (bf16[2,2,32,384]{3,2,1,0:T(8,128)(2,1)S(1)}, bf16[2,2,32,384]{3,2,1,0:T(8,128)(2,1)}, u32[]{:S(2)}) copy-start(bf16[2,2,32,384]{3,2,1,0:T(8,128)(2,1)} %own) | copy-start | bytes 294916
  3.9 2.9 %copy-start.3 = (f32[768]{0:T(1024)S(1)}, f32[768]{0:T(1024)}, u32[]{:S(2)}) copy-start(f32[768]{0:T(1024)} %refs_10_.1) | copy-start | bytes 9220
  3.9 2.9 %copy-start.4 = (f32[384]{0:T(512)S(1)}, f32[384]{0:T(512)}, u32[]{:S(2)}) copy-start(f32[384]{0:T(512)} %refs_8_.1) | copy-start | bytes 4612
  3.9 4.8 %copy-start.5 = (f32[192]{0:T(256)S(1)}, f32[192]{0:T(256)}, u32[]{:S(2)}) copy-start(f32[192]{0:T(256)} %sb.3) | copy-start | bytes 2308
  3.9 5.9 %collective-permute-start.2 = (bf16[72,384]{1,0:T(8,128)(2,1)S(1)}, bf16[72,384]{1,0:T(8,128)(2,1)S(1)}, u32[]{:S(2)}, u32[]{:S(2)}) collective-permute-start(bf16[72,384]{1,0:T(8,128)(2,1)S(1)} %shard_map.65), channel_id=1, source_target_pairs={{0,7},{1,6},{2,5},{3,4},{4,11},{5,10},{6,9},{7,8},{8,15},{9,14},{1... | collective-permute-start | bytes 165896 | tf_op jit(solution)/shard_map/ppermute | solution.py:456
  6.3 3.8 %collective-permute-start.1 = (bf16[72,384]{1,0:T(8,128)(2,1)S(1)}, bf16[72,384]{1,0:T(8,128)(2,1)S(1)}, u32[]{:S(2)}, u32[]{:S(2)}) collective-permute-start(bf16[72,384]{1,0:T(8,128)(2,1)S(1)} %get-tuple-element.23.x), channel_id=1, source_target_pairs={{0,3},{1,2},{2,1},{3,0},{4,7},{5,6},{6,5},{7,4},{8,11},{9,10},{10,... | collective-permute-start | bytes 165896 | tf_op jit(solution)/shard_map/ppermute | solution.py:456
  8.6 1.2 %collective-permute-start.4 = (bf16[8,384]{1,0:T(8,128)(2,1)S(1)}, bf16[8,384]{1,0:T(8,128)(2,1)S(1)}, u32[]{:S(2)}, u32[]{:S(2)}) collective-permute-start(bf16[8,384]{1,0:T(8,128)(2,1)S(1)} %shard_map.68), channel_id=1, source_target_pairs={{0,1},{1,0},{2,3},{3,2},{4,5},{5,4},{6,7},{7,6},{8,9},{9,8},{10,11... | collective-permute-start | bytes 18440 | tf_op jit(solution)/shard_map/ppermute | solution.py:456

commit v6 on v4

v6 whole, which is shorter than its diff:
```python
import functools

import jax
import jax.numpy as jnp
from jax import lax
from jax.experimental import pallas as pl
from jax.experimental.pallas import tpu as pltpu
from jax.sharding import PartitionSpec as P

LANES = 128
VMEM = pl.BlockSpec(memory_space=pltpu.VMEM)
ANY = pl.BlockSpec(memory_space=pl.ANY)
SMALL = pltpu.CompilerParams(vmem_limit_bytes=4 * 1024 * 1024)
LARGE = pltpu.CompilerParams(vmem_limit_bytes=16 * 1024 * 1024)
SHORT = pl.CostEstimate(flops=10**6, bytes_accessed=10**5, transcendentals=0)


def activate(values, gain):
    values = values.astype(jnp.float32)
    mean_square = jnp.mean(values * values, axis=-1, keepdims=True)
    scaled = values * lax.rsqrt(mean_square + 1e-06) * gain
    return scaled / (1.0 + jnp.exp(-scaled))


def dot_nt(x, w):
    return lax.dot_general(x, w, (((1,), (1,)), ((), ())), preferred_element_type=jnp.float32)


def time_conv(parts, tw, tb):
    chans = tw.shape[1]
    n = len(parts)
    window = parts[0] if n == 1 else jnp.concatenate(parts, axis=1)
    summed = jnp.dot(window, tw[3 - n :].reshape(n * chans, 2 * chans), preferred_element_type=jnp.float32)
    return (summed + tb[...].reshape(1, -1)).astype(jnp.bfloat16)


def on_first_shard():
    return lax.axis_index("tm") == 0


def odd_rows(shape):
    return lax.broadcasted_iota(jnp.int32, shape, 0) % 2 == 1


def shifted(early, late):
    before = 0.0 if early is None else pltpu.roll(early, early.shape[0] - 1, 0)
    return jnp.where(odd_rows(late.shape), pltpu.roll(late, 1, 0), before)


def put_column(x, last, out):
    frames, rows, cols, _ = x.shape
    for i in range(rows):
        for f in range(frames):
            low = x[f, i, 0:8].astype(jnp.float32)[0:1]
            high = x[f, i, cols - 8 :].astype(jnp.float32)[7:8]
            out[8 * i + f : 8 * i + f + 1] = jnp.where(last, high, low)


def column_kernel(x, out, rows_f32):
    rows_f32[...] = jnp.zeros_like(rows_f32)
    put_column(x, lax.axis_index("cols") == 0, rows_f32)
    out[...] = rows_f32[...].astype(out.dtype)


def column_of(x):
    shape = (8 * x.shape[1], x.shape[-1])
    return pl.pallas_call(
        column_kernel,
        out_shape=jax.ShapeDtypeStruct(shape, x.dtype),
        in_specs=[VMEM],
        out_specs=VMEM,
        scratch_shapes=[pltpu.VMEM(shape, jnp.float32)],
        compiler_params=SMALL,
    )(x)


def split_kernel(beside, corner, edge, near, rows_f32):
    frames, rows, cols, _ = beside.shape
    rows_f32[...] = jnp.zeros_like(rows_f32)
    put_column(beside, lax.axis_index("cols") > 0, rows_f32)
    edge[...] = rows_f32[...].astype(edge.dtype)
    outer = jnp.where(lax.axis_index("rows") == 0, rows - 1, 0)
    for f in range(frames):
        near[f * cols : (f + 1) * cols] = beside[f, outer]
    near[frames * cols :] = corner[...]


def split(beside, corner):
    frames, rows, cols, chans = beside.shape
    return pl.pallas_call(
        split_kernel,
        out_shape=[
            jax.ShapeDtypeStruct((8 * rows, chans), beside.dtype),
            jax.ShapeDtypeStruct((frames * cols + 8, chans), beside.dtype),
        ],
        in_specs=[VMEM] * 2,
        out_specs=[VMEM] * 2,
        scratch_shapes=[pltpu.VMEM((8 * rows, chans), jnp.float32)],
        cost_estimate=pl.CostEstimate(flops=8 * 10**9, bytes_accessed=10**5, transcendentals=0),
        compiler_params=SMALL,
    )(beside, corner)


def put_taps(ups, sw, taps):
    ups_frames, rows, cols = taps.shape[2:5]
    chans, c_out = sw.shape[3], sw.shape[2]
    for a in range(3):
        for b in range(3):
            product = dot_nt(ups[...].reshape(ups_frames * rows * cols, chans), sw[a, b])
            taps[a, b, :, :, :, :c_out] = product.reshape(ups_frames, rows, cols, c_out)


def put_ups(ups, stacked, body):
    chans = ups.shape[2]
    for t in range(ups.shape[0] // 2):
        for s in range(2):
            ups[2 * t + s] = stacked[t * body : (t + 1) * body, s * chans : (s + 1) * chans]


def taps_shape(frames, rows, cols):
    return (3, 3, 2 * frames, rows, cols, 2 * LANES)


def column_sides():
    col = lax.axis_index("cols")
    at_left = (col > 0).astype(jnp.float32)
    at_right = (col < lax.axis_size("cols") - 1).astype(jnp.float32)
    return at_left, at_right, jnp.where(col == 0, 2, 0)


def sums(near, far, border, at_left, at_right, place):
    cols = place.shape[0]
    parts = [n if f is None else n + f for n, f in zip(near, far, strict=True)]
    left = jnp.where(place == 0, border * at_left, pltpu.roll(parts[0], 1, 0))
    right = jnp.where(place == cols - 1, border * at_right, pltpu.roll(parts[2], cols - 1, 0))
    return parts[1] + parts[2] + left, parts[0] + parts[1] + right


def store_row(done, index, wide, c_out):
    done[(*index, slice(None), slice(0, LANES))] = wide[0].astype(done.dtype)
    done[(*index, slice(None), slice(LANES, c_out))] = wide[1, :, : c_out - LANES].astype(done.dtype)


def rows_of(sides, rows):
    if sides == ("either",):
        upper = lax.axis_index("rows") == 0
        first = (0, 0)
        last = (rows - 1, 1)
        outer = tuple(jnp.where(upper, x, y) for x, y in zip(first, last, strict=True))
        inner = tuple(jnp.where(upper, y, x) for x, y in zip(first, last, strict=True))
        free, bound = [(*outer, False)], [inner]
    else:
        free, bound = [], [(0, 0), (rows - 1, 1)]
    for i in range(rows):
        for p in range(2):
            if (i, p) not in ((0, 0), (rows - 1, 1)):
                free.append((i, p, True))
    return free, bound


def row_sums(sides, beside, taps, sw, sb, free_rows, near, rim, border, shift, wide):
    ups_frames, rows, cols = taps.shape[2:5]
    chans, c_out = sw.shape[3], sw.shape[2]
    at_left, at_right, tap = column_sides()
    x = jnp.concatenate([beside[:, :chans], beside[:, chans:]], axis=0)
    for a in range(3):
        border[a, :, :, :, :c_out] = dot_nt(x, sw[a, tap]).reshape(2, rows, 8, c_out)
    shift[:, :c_out] = sb[...].reshape(1, c_out)

    place = lax.broadcasted_iota(jnp.int32, (cols, LANES), 0)
    free, bound = rows_of(sides, rows)
    for k, (i, p, inside) in enumerate(free):
        for u in range(ups_frames):
            t, s = u // 2, u % 2
            for half in range(2):
                lanes = slice(half * LANES, (half + 1) * LANES)
                close = [taps[1 - p, b, u, i, :, lanes] + taps[2 - p, b, u, i, :, lanes] for b in range(3)]
                close[1] = close[1] + shift[:, lanes]
                line = border[1 - p, s, i, :, lanes] + border[2 - p, s, i, :, lanes]
                if inside:
                    far = [taps[2 * p, b, u, i + 2 * p - 1, :, lanes] for b in range(3)]
                    line = line + border[2 * p, s, i + 2 * p - 1, :, lanes]
                else:
                    far = [None] * 3
                even, odd = sums(close, far, line[t : t + 1], at_left, at_right, place)
                wide[half, pl.ds(0, cols, 2)] = even
                wide[half, pl.ds(1, cols, 2)] = odd
            store_row(free_rows, (k, u), wide, c_out)
    for k, (i, p) in enumerate(bound):
        rim[k] = border[1 - p, :, i] + border[2 - p, :, i]
        for u in range(ups_frames):
            for b in range(3):
                close = taps[1 - p, b, u, i] + taps[2 - p, b, u, i]
                near[k, b, u] = close + shift[...] if b == 1 else close


def sums_shapes(sides, frames, rows, cols, c_out):
    n = len(sides)
    return [
        jax.ShapeDtypeStruct((2 * rows - n, 2 * frames, 2 * cols, c_out), jnp.bfloat16),
        jax.ShapeDtypeStruct((n, 3, 2 * frames, cols, 2 * LANES), jnp.float32),
        jax.ShapeDtypeStruct((n, 2, 8, 2 * LANES), jnp.float32),
    ]


def sums_scratch(rows, cols):
    return [
        pltpu.VMEM((3, 2, rows, 8, 2 * LANES), jnp.float32),
        pltpu.VMEM((1, 2 * LANES), jnp.float32),
        pltpu.VMEM((2, 2 * cols, LANES), jnp.float32),
    ]


def early_kernel(sides, own, edge_own, gain_v, tw, tb, sw, sb, acts, free_rows, near, rim, soon, late, ups, taps, *scratch):
    frames, rows, cols, _ = own.shape
    body = rows * cols
    gain = gain_v[...].reshape(1, -1)
    for f in range(frames):
        for i in range(rows):
            acts[f, i * cols : (i + 1) * cols] = activate(own[f, i], gain).astype(acts.dtype)

    @pl.when(on_first_shard())
    def _():
        edge = activate(edge_own[...], gain)
        soon[:body] = jnp.zeros_like(acts[0])
        for f in range(frames):
            if f:
                soon[f * body : (f + 1) * body] = acts[f - 1]
            late[f * body : (f + 1) * body] = acts[f]
        soon[frames * body :] = shifted(None, edge).astype(soon.dtype)
        late[frames * body :] = edge.astype(late.dtype)
        stacked = time_conv([soon[...], late[...]], tw, tb)
        put_ups(ups, stacked, body)
        put_taps(ups, sw, taps)
        row_sums(sides, stacked[frames * body :], taps, sw, sb, free_rows, near, rim, *scratch)


def early(sides, own, edge_own, gain, tw, tb, sw, sb):
    frames, rows, cols, chans = own.shape
    body = rows * cols
    operands = (own, edge_own, gain, tw, tb, sw, sb)
    return pl.pallas_call(
        functools.partial(early_kernel, sides),
        out_shape=[
            jax.ShapeDtypeStruct((frames, body, chans), jnp.bfloat16),
            *sums_shapes(sides, frames, rows, cols, sb.shape[0]),
        ],
        in_specs=[VMEM] * len(operands),
        out_specs=[VMEM] * 4,
        scratch_shapes=[
            pltpu.VMEM((frames * body + 8 * rows, chans), jnp.bfloat16),
            pltpu.VMEM((frames * body + 8 * rows, chans), jnp.bfloat16),
            pltpu.VMEM((2 * frames, body, chans), jnp.bfloat16),
            pltpu.VMEM(taps_shape(frames, rows, cols), jnp.float32),
            *sums_scratch(rows, cols),
        ],
        cost_estimate=SHORT,
        compiler_params=LARGE,
    )(*operands)


def mid_kernel(before, acts_own, gain_v, tw, tb, sw, taps, acts, ups):
    frames, rows, cols, chans = before.shape
    body = rows * cols

    @pl.when(jnp.logical_not(on_first_shard()))
    def _():
        gain = gain_v[...].reshape(1, -1)
        for f in range(frames):
            for i in range(rows):
                acts[f, i * cols : (i + 1) * cols] = activate(before[f, i], gain).astype(acts.dtype)
        acts[frames:] = acts_own[...]
        parts = [acts[k : k + frames].reshape(frames * body, chans) for k in range(3)]
        put_ups(ups, time_conv(parts, tw, tb), body)
        put_taps(ups, sw, taps)


def mid(before, acts_own, gain, tw, tb, sw):
    frames, rows, cols, chans = before.shape
    operands = (before, acts_own, gain, tw, tb, sw)
    return pl.pallas_call(
        mid_kernel,
        out_shape=jax.ShapeDtypeStruct(taps_shape(frames, rows, cols), jnp.float32),
        in_specs=[VMEM] * len(operands),
        out_specs=VMEM,
        scratch_shapes=[
            pltpu.VMEM((2 * frames, rows * cols, chans), jnp.bfloat16),
            pltpu.VMEM((2 * frames, rows * cols, chans), jnp.bfloat16),
        ],
        cost_estimate=SHORT,
        compiler_params=LARGE,
    )(*operands)


def sum_kernel(sides, edge_own, edge_before, taps, gain_v, tw, tb, sw, sb, free_rows, near, rim, *scratch):
    @pl.when(jnp.logical_not(on_first_shard()))
    def _():
        gain = gain_v[...].reshape(1, -1)
        soon = activate(edge_before[...], gain)
        late = activate(edge_own[...], gain)
        parts = [x.astype(jnp.bfloat16) for x in (soon, shifted(soon, late), late)]
        row_sums(sides, time_conv(parts, tw, tb), taps, sw, sb, free_rows, near, rim, *scratch)


def partial_sums(sides, edge_own, edge_before, taps, gain, tw, tb, sw, sb):
    ups_frames, rows, cols = taps.shape[2:5]
    operands = (edge_own, edge_before, taps, gain, tw, tb, sw, sb)
    return pl.pallas_call(
        functools.partial(sum_kernel, sides),
        out_shape=sums_shapes(sides, ups_frames // 2, rows, cols, sb.shape[0]),
        in_specs=[VMEM] * len(operands),
        out_specs=[VMEM] * 3,
        scratch_shapes=sums_scratch(rows, cols),
        cost_estimate=SHORT,
        compiler_params=LARGE,
    )(*operands)


def finish(
    sides, halo_own, halo_before, free_rows, near, rim, gain_v, tw, tb, sw, out,
    acts, ups, reach, corner, wide, bound_rows, free_sems, bound_sems,
):
    ups_frames, cols = near.shape[2:4]
    rows = (free_rows.shape[0] + len(sides)) // 2
    frames = ups_frames // 2
    chans, c_out = sw.shape[3], sw.shape[2]
    span = frames * cols
    free, bound = rows_of(sides, rows)
    copies = []
    for k, (i, p, _) in enumerate(free):
        copies.append(pltpu.make_async_copy(free_rows.at[k], out.at[:, 2 * i + p], free_sems.at[k]))
        copies[-1].start()

    row = lax.axis_index("rows")
    gain = gain_v[...].reshape(1, -1)
    at_left, at_right, col_tap = column_sides()
    place = lax.broadcasted_iota(jnp.int32, (cols, LANES), 0)

    def put(f, values):
        for k in range(3):
            t = f - k
            if 0 <= t < frames:
                acts[k, t * cols : (t + 1) * cols] = values.astype(acts.dtype)

    def put_corners(k, values):
        acts[k, span:] = jnp.concatenate([values, jnp.zeros_like(values)], axis=0).astype(acts.dtype)

    for h, where in enumerate(sides):
        if where == "either":
            tap, exists = jnp.where(row == 0, 2, 0), 1.0
        elif where == "above":
            tap, exists = 0, (row > 0).astype(jnp.float32)
        else:
            tap, exists = 2, (row < lax.axis_size("rows") - 1).astype(jnp.float32)
        for f in range(frames):
            put(frames + f, activate(halo_own[h][f * cols : (f + 1) * cols], gain))
        late = activate(halo_own[h][span : span + 8], gain)
        put_corners(2, late)
        if halo_before is None:
            put(frames - 1, jnp.zeros((cols, chans), acts.dtype))
            put_corners(1, shifted(None, late))
            stacked = time_conv([acts[1], acts[2]], tw, tb)
        else:
            for f in range(frames):
                put(f, activate(halo_before[h][f * cols : (f + 1) * cols], gain))
            soon = activate(halo_before[h][span : span + 8], gain)
            put_corners(0, soon)
            put_corners(1, shifted(soon, late))
            stacked = time_conv([acts[0], acts[1], acts[2]], tw, tb)
        put_ups(ups, stacked, cols)
        x = ups[...].reshape(ups_frames * cols, chans)
        for b in range(3):
            reach[b, :, :, :c_out] = dot_nt(x, sw[tap, b]).reshape(ups_frames, cols, c_out)
        x = jnp.concatenate([stacked[span:, :chans], stacked[span:, chans:]], axis=0)
        corner[:, :c_out] = dot_nt(x, sw[tap, col_tap])
        i, p = bound[h]
        for u in range(ups_frames):
            t, s = u // 2, u % 2
            for half in range(2):
                lanes = slice(half * LANES, (half + 1) * LANES)
                close = [near[h, b, u, :, lanes] for b in range(3)]
                far = [reach[b, u, :, lanes] * exists for b in range(3)]
                line = rim[h, s, t : t + 1, lanes] + corner[16 * s + t : 16 * s + t + 1, lanes] * exists
                even, odd = sums(close, far, line, at_left, at_right, place)
                wide[half, pl.ds(0, cols, 2)] = even
                wide[half, pl.ds(1, cols, 2)] = odd
            store_row(bound_rows, (h, u), wide, c_out)
            copies.append(
                pltpu.make_async_copy(bound_rows.at[h, u], out.at[u, 2 * i + p], bound_sems.at[h, u])
            )
            copies[-1].start()
    for copy in copies:
        copy.wait()


def finish_scratch(n, n_free, ups_frames, cols, chans, c_out):
    span = ups_frames // 2 * cols + 16
    return [
        pltpu.VMEM((3, span, chans), jnp.bfloat16),
        pltpu.VMEM((ups_frames, cols, chans), jnp.bfloat16),
        pltpu.VMEM((3, ups_frames, cols, 2 * LANES), jnp.float32),
        pltpu.VMEM((32, 2 * LANES), jnp.float32),
        pltpu.VMEM((2, 2 * cols, LANES), jnp.float32),
        pltpu.VMEM((n, ups_frames, 2 * cols, c_out), jnp.bfloat16),
        pltpu.SemaphoreType.DMA((n_free,)),
        pltpu.SemaphoreType.DMA((n, ups_frames)),
    ]


def first_kernel(sides, *refs):
    n = len(sides)

    @pl.when(on_first_shard())
    def _():
        finish(sides, refs[:n], None, *refs[n:])


def rest_kernel(sides, *refs):
    n = len(sides)

    @pl.when(jnp.logical_not(on_first_shard()))
    def _():
        finish(sides, refs[:n], refs[n : 2 * n], *refs[2 * n : 2 * n + 7], *refs[2 * n + 8 :])


def finished(kernel, sides, halos, partial, gain, tw, tb, sw, so_far=()):
    n = len(sides)
    n_free, ups_frames, out_cols, c_out = partial[0].shape
    cols, chans = out_cols // 2, sw.shape[3]
    operands = (*halos, *partial, gain, tw, tb, sw)
    return pl.pallas_call(
        functools.partial(kernel, sides),
        out_shape=jax.ShapeDtypeStruct((ups_frames, n_free + n, out_cols, c_out), jnp.bfloat16),
        in_specs=[VMEM] * len(operands) + [ANY] * len(so_far),
        out_specs=ANY,
        scratch_shapes=finish_scratch(n, n_free, ups_frames, cols, chans, c_out),
        input_output_aliases={len(operands): 0} if so_far else {},
        cost_estimate=SHORT,
        compiler_params=LARGE,
    )(*operands, *so_far)


def local(latent, norm_gain, time_weight, time_bias, space_weight, space_bias):
    frames, rows, cols, chans = latent.shape
    shards, n_rows, n_cols = (lax.axis_size(a) for a in ("tm", "rows", "cols"))
    axes = ("tm", "rows", "cols")

    def moved(x, route):
        pairs = []
        for t in range(shards):
            for r in range(n_rows):
                for c in range(n_cols):
                    t2, r2, c2 = route(t, r, c)
                    pairs.append(((t * n_rows + r) * n_cols + c, (t2 * n_rows + r2) * n_cols + c2))
        return lax.ppermute(x, axes, pairs)

    def onward(t, r, c, to):
        return (t + 1, *to) if t + 1 < shards else (0, r, 1 - c)

    def across(x):
        return moved(x, lambda t, r, c: (t, r, 1 - c))

    beside = across(latent)
    before = moved(latent, lambda t, r, c: onward(t, r, c, (r, c)))
    tile = lax.dynamic_slice(
        latent,
        (0, (rows - 1) * (1 - lax.axis_index("rows")), (cols - 8) * (1 - lax.axis_index("cols")), 0),
        (frames, 1, 8, chans),
    ).reshape(frames, 8, chans)
    corner = jnp.where(lax.axis_index("cols") == 0, tile[:, 7], tile[:, 0])
    edge_own, near = split(beside, jnp.pad(corner, ((0, 8 - frames), (0, 0))))
    if n_rows == 2:
        sides = ("either",)
        halo_own = (moved(near, lambda t, r, c: (t, 1 - r, 1 - c)),)
        halo_before = (moved(near, lambda t, r, c: onward(t, r, c, (1 - r, 1 - c))),)
    else:
        sides = ("above", "below")

        def and_corner(x, edge, i):
            row = x[:, i].reshape(frames * cols, chans)
            return jnp.concatenate([row, edge[8 * i : 8 * i + frames], jnp.zeros((8 - frames, chans), x.dtype)], axis=0)

        def both(x, edge):
            return (
                moved(and_corner(x, edge, rows - 1), lambda t, r, c: (t, (r + 1) % n_rows, c)),
                moved(and_corner(x, edge, 0), lambda t, r, c: (t, (r - 1) % n_rows, c)),
            )

        halo_own = both(latent, edge_own)
        halo_before = both(before, across(column_of(before)))

    sw = jnp.swapaxes(space_weight, 2, 3)
    weights = (norm_gain, time_weight, time_bias, sw)
    ready, _ = lax.optimization_barrier((latent, edge_own))
    acts, *first = early(sides, ready, edge_own, *weights, space_bias)
    before, acts = lax.optimization_barrier((before, acts))
    edge_before = across(column_of(before))
    taps = mid(before, acts, *weights)
    taps, *halo_own = lax.optimization_barrier((taps, *halo_own))
    result = finished(first_kernel, sides, halo_own, first, *weights)
    edge_before, result = lax.optimization_barrier((edge_before, result))
    rest = partial_sums(sides, edge_own, edge_before, taps, *weights, space_bias)
    return finished(rest_kernel, sides, (*halo_own, *halo_before), rest, *weights, so_far=(result,))


def solution(mesh):
    in_specs = (P(("clips", "tm"), "rows", "cols", None), P(), P(), P(), P(), P())
    out_specs = P(("clips", "tm"), "rows", "cols", None)
    return jax.shard_map(local, mesh=mesh, in_specs=in_specs, out_specs=out_specs, check_vma=False)
```

time: 13.1 us -> 11.1 us (0.85)
  waiting for transfers between devices: 1.63 us -> 0.4 us
  Pallas kernels: 4.38 us -> 3.47 us
    ppermute x5, waiting for transfers between devices: 1.63 us -> 0.4 us  [moved(): return lax.ppermute(x, axes, pairs)]
    pallas_call x7 -> x6, Pallas kernels: 4.36 us -> 3.44 us  [the longest x1 1.85 us: early(): pl.pallas_call(functools.partial(early_kernel, sides), out_shape=[jax.Sha...]
  transfers between devices with their start and end apart: 5 -> 5, of which waited for: 1 -> 1; matrix products, arithmetic and copies ran while one was open for 6% -> 7% of each run, Pallas kernels for 21% -> 31%
where the time goes in v6:
time: 11.1 us; the launch traced here: 11 us
  starting transfers between devices  6.15 us (55%)
  Pallas kernels  3.47 us (31%)
  local copies, waits for them, and re-layouts  0.8 us (7%)
  waiting for transfers between devices  0.4 us (4%)
  between operations  0.14 us (1%)
    ppermute x5, starting transfers between devices, moved(): return lax.ppermute(x, axes, pairs)  6.15 us
    pallas_call x1, Pallas kernels, early(): pl.pallas_call(functools.partial(early_kernel, sides), out_shape=[jax.Sha...  1.85 us
    pallas_call x2, Pallas kernels, finished(): pl.pallas_call(functools.partial(kernel, sides), out_shape=jax.ShapeDtype...  1.54 us
    dynamic_slice x2, local copies, waits for them, and re-layouts, local(): lax.dynamic_slice(latent, (0, (rows - 1) * (1 - lax.axis_index('rows')),...  0.75 us
    ppermute x5, waiting for transfers between devices, moved(): return lax.ppermute(x, axes, pairs)  0.4 us
  transfers between devices with their start and end apart: 5, of which 1 were waited for; matrix products, arithmetic and copies ran while one was open for 7% of the time, Pallas kernels for 31%

profile of v6, /device:TPU:0, one launch (start us, length us, event | category | flops | bytes accessed | tf_op | source)
XLA Modules:
  0.0 11.0 jit_solution(3301597835642265933)
XLA Ops:
  0.0 0.5 %collective-permute-start.1 = (bf16[2,2,32,384]{3,2,1,0:T(8,128)(2,1)}, bf16[2,2,32,384]{3,2,1,0:T(8,128)(2,1)S(1)}, u32[]{:S(2)}, u32[]{:S(2)}) collective-permute-start(bf16[2,2,32,384]{3,2,1,0:T(8,128)(2,1)} %own), channel_id=1, source_target_pairs={{0,1},{1,0},{2,3},{3,2},{4,5},{5,4},{6,7},{7,6},{8,9},{9,8},{10,11... | collective-permute-start | bytes 294920 | tf_op jit(solution)/shard_map/ppermute | solution.py:455
  0.5 2.6 %collective-permute-start = (bf16[2,2,32,384]{3,2,1,0:T(8,128)(2,1)}, bf16[2,2,32,384]{3,2,1,0:T(8,128)(2,1)S(1)}, u32[]{:S(2)}, u32[]{:S(2)}) collective-permute-start(bf16[2,2,32,384]{3,2,1,0:T(8,128)(2,1)} %own), channel_id=1, source_target_pairs={{0,4},{1,5},{2,6},{3,7},{4,8},{5,9},{6,10},{7,11},{8,12},{9,13},{1... | collective-permute-start | bytes 294920 | tf_op jit(solution)/shard_map/ppermute | solution.py:455
  3.0 0.7 %constant_dynamic-slice_fusion = bf16[2,1,8,384]{3,2,1,0:T(8,128)(2,1)S(1)} fusion(bf16[2,2,32,384]{3,2,1,0:T(8,128)(2,1)} %own, s32[]{:T(128)S(6)} %select_n.18, s32[]{:T(128)S(6)} %select_n.19), kind=kLoop, calls=%fused_computation.3 | loop fusion | bytes 24584 | tf_op jit(solution)/shard_map/dynamic_slice | solution.py:465
  3.8 0.0 copy-start
  3.8 0.0 copy-start.1
  3.8 0.0 copy-start.2
  3.9 0.0 copy-start.3
  3.9 0.0 copy-start.4
  3.9 0.0 copy-start.5
  3.9 0.0 collective-permute-done.1.beside
  3.9 1.4 %collective-permute-start.2 = (bf16[72,384]{1,0:T(8,128)(2,1)S(1)}, bf16[72,384]{1,0:T(8,128)(2,1)S(1)}, u32[]{:S(2)}, u32[]{:S(2)}) collective-permute-start(bf16[72,384]{1,0:T(8,128)(2,1)S(1)} %get-tuple-element.26), channel_id=1, source_target_pairs={{0,3},{1,2},{2,1},{3,0},{4,7},{5,6},{6,5},{7,4},{8,11},{9,10},{10,... | collective-permute-start | bytes 165896 | tf_op jit(solution)/shard_map/ppermute | solution.py:455
  5.3 1.4 %collective-permute-start.3 = (bf16[72,384]{1,0:T(8,128)(2,1)S(1)}, bf16[72,384]{1,0:T(8,128)(2,1)S(1)}, u32[]{:S(2)}, u32[]{:S(2)}) collective-permute-start(bf16[72,384]{1,0:T(8,128)(2,1)S(1)} %get-tuple-element.26), channel_id=1, source_target_pairs={{0,7},{1,6},{2,5},{3,4},{4,11},{5,10},{6,9},{7,8},{8,15},{9,14},{1... | collective-permute-start | bytes 165896 | tf_op jit(solution)/shard_map/ppermute | solution.py:455
  6.8 0.0 copy-done
  6.8 0.0 copy-done.1
  6.8 0.0 copy-done.2
  6.8 0.0 copy-done.3
  6.8 0.0 copy-done.4
  6.8 0.0 copy-done.5
  6.8 1.9 %shard_map.65 = (bf16[2,64,384]{2,1,0:T(8,128)(2,1)S(1)}, bf16[3,4,64,192]{3,2,1,0:T(8,128)(2,1)S(1)}, f32[1,3,4,32,256]{4,3,2,1,0:T(8,128)S(1)}, f32[1,2,8,256]{3,2,1,0:T(8,128)S(1)}) custom-call(bf16[2,2,32,384]{3,2,1,0:T(8,128)(2,1)S(1)} %copy-done.2, bf16[16,384]{1,0:T(8,128)(2,1)S(1)} %get-tuple-element.21.edge_own, f32[384]{0:T(512)S(1)} %copy-done.4, ...), custom_call_target="tpu_custom_call" | custom-call | flops 1000000 | bytes 100000 | tf_op jit(solution)/shard_map/pallas_call | solution.py:242
  8.7 0.0 collective-permute-done.before.x
  8.7 0.3 %collective-permute-start.4 = (bf16[16,384]{1,0:T(8,128)(2,1)S(1)}, bf16[16,384]{1,0:T(8,128)(2,1)S(1)}, u32[]{:S(2)}, u32[]{:S(2)}) collective-permute-start(bf16[16,384]{1,0:T(8,128)(2,1)S(1)} %shard_map.67), channel_id=1, source_target_pairs={{0,1},{1,0},{2,3},{3,2},{4,5},{5,4},{6,7},{7,6},{8,9},{9,8},{10,11... | collective-permute-start | bytes 36872 | tf_op jit(solution)/shard_map/ppermute | solution.py:455
  9.0 0.0 collective-permute-done.2.refs_0_
  9.0 1.5 %shard_map.68.refs_9_ = bf16[4,4,64,192]{3,2,1,0:T(8,128)(2,1)} custom-call(bf16[72,384]{1,0:T(8,128)(2,1)S(1)} %collective-permute-done.2.refs_0_, bf16[3,4,64,192]{3,2,1,0:T(8,128)(2,1)S(1)} %get-tuple-element.28.refs_1_, f32[1,3,4,32,256]{4,3,2,1,0:T(8,128)S(1)} %get-tuple-element.29.refs_2_, f32[1,2,8,256]{3,2,1,0:T(8,128)S(1)} %get-tuple-element.30.refs_3_, ...), custom_call_target="tpu_custom_call" | custom-call | flops 1000000 | bytes 100000 | tf_op jit(solution)/shard_map/pallas_call | solution.py:431
  10.5 0.0 collective-permute-done.4.edge_before
  10.5 0.4 %collective-permute-done.3.refs_1_ = bf16[72,384]{1,0:T(8,128)(2,1)S(1)} collective-permute-done((bf16[72,384]{1,0:T(8,128)(2,1)S(1)}, bf16[72,384]{1,0:T(8,128)(2,1)S(1)}, u32[]{:S(2)}, u32[]{:S(2)}) %collective-permute-start.3) | collective-permute-done | bytes 55328 | tf_op jit(solution)/shard_map/ppermute | solution.py:455
  10.9 0.1 shard_map.70
  (7 shorter events, 0.1 us)
Async XLA Ops:
  0.0 3.9 %collective-permute-start.1 = (bf16[2,2,32,384]{3,2,1,0:T(8,128)(2,1)}, bf16[2,2,32,384]{3,2,1,0:T(8,128)(2,1)S(1)}, u32[]{:S(2)}, u32[]{:S(2)}) collective-permute-start(bf16[2,2,32,384]{3,2,1,0:T(8,128)(2,1)} %own), channel_id=1, source_target_pairs={{0,1},{1,0},{2,3},{3,2},{4,5},{5,4},{6,7},{7,6},{8,9},{9,8},{10,11... | collective-permute-start | bytes 294920 | tf_op jit(solution)/shard_map/ppermute | solution.py:455
  0.5 8.2 %collective-permute-start = (bf16[2,2,32,384]{3,2,1,0:T(8,128)(2,1)}, bf16[2,2,32,384]{3,2,1,0:T(8,128)(2,1)S(1)}, u32[]{:S(2)}, u32[]{:S(2)}) collective-permute-start(bf16[2,2,32,384]{3,2,1,0:T(8,128)(2,1)} %own), channel_id=1, source_target_pairs={{0,4},{1,5},{2,6},{3,7},{4,8},{5,9},{6,10},{7,11},{8,12},{9,13},{1... | collective-permute-start | bytes 294920 | tf_op jit(solution)/shard_map/ppermute | solution.py:455
  3.8 2.9 %copy-start = (bf16[3,384,768]{2,1,0:T(8,128)(2,1)S(1)}, bf16[3,384,768]{2,1,0:T(8,128)(2,1)}, u32[]{:S(2)}) copy-start(bf16[3,384,768]{2,1,0:T(8,128)(2,1)} %refs_6_.3) | copy-start | bytes 5308420
  3.8 2.9 %copy-start.1 = (bf16[3,3,384,192]{2,3,1,0:T(8,128)(2,1)S(1)}, bf16[3,3,384,192]{2,3,1,0:T(8,128)(2,1)}, u32[]{:S(2)}) copy-start(bf16[3,3,384,192]{2,3,1,0:T(8,128)(2,1)} %param.10) | copy-start | bytes 3981316
  3.8 2.9 %copy-start.2 = (bf16[2,2,32,384]{3,2,1,0:T(8,128)(2,1)S(1)}, bf16[2,2,32,384]{3,2,1,0:T(8,128)(2,1)}, u32[]{:S(2)}) copy-start(bf16[2,2,32,384]{3,2,1,0:T(8,128)(2,1)} %own) | copy-start | bytes 294916
  3.9 2.9 %copy-start.3 = (f32[768]{0:T(1024)S(1)}, f32[768]{0:T(1024)}, u32[]{:S(2)}) copy-start(f32[768]{0:T(1024)} %refs_7_.1) | copy-start | bytes 9220
  3.9 2.9 %copy-start.4 = (f32[384]{0:T(512)S(1)}, f32[384]{0:T(512)}, u32[]{:S(2)}) copy-start(f32[384]{0:T(512)} %refs_5_.3) | copy-start | bytes 4612
  3.9 2.9 %copy-start.5 = (f32[192]{0:T(256)S(1)}, f32[192]{0:T(256)}, u32[]{:S(2)}) copy-start(f32[192]{0:T(256)} %sb.3) | copy-start | bytes 2308
  3.9 5.1 %collective-permute-start.2 = (bf16[72,384]{1,0:T(8,128)(2,1)S(1)}, bf16[72,384]{1,0:T(8,128)(2,1)S(1)}, u32[]{:S(2)}, u32[]{:S(2)}) collective-permute-start(bf16[72,384]{1,0:T(8,128)(2,1)S(1)} %get-tuple-element.26), channel_id=1, source_target_pairs={{0,3},{1,2},{2,1},{3,0},{4,7},{5,6},{6,5},{7,4},{8,11},{9,10},{10,... | collective-permute-start | bytes 165896 | tf_op jit(solution)/shard_map/ppermute | solution.py:455
  5.3 5.6 %collective-permute-start.3 = (bf16[72,384]{1,0:T(8,128)(2,1)S(1)}, bf16[72,384]{1,0:T(8,128)(2,1)S(1)}, u32[]{:S(2)}, u32[]{:S(2)}) collective-permute-start(bf16[72,384]{1,0:T(8,128)(2,1)S(1)} %get-tuple-element.26), channel_id=1, source_target_pairs={{0,7},{1,6},{2,5},{3,4},{4,11},{5,10},{6,9},{7,8},{8,15},{9,14},{1... | collective-permute-start | bytes 165896 | tf_op jit(solution)/shard_map/ppermute | solution.py:455
  8.7 1.8 %collective-permute-start.4 = (bf16[16,384]{1,0:T(8,128)(2,1)S(1)}, bf16[16,384]{1,0:T(8,128)(2,1)S(1)}, u32[]{:S(2)}, u32[]{:S(2)}) collective-permute-start(bf16[16,384]{1,0:T(8,128)(2,1)S(1)} %shard_map.67), channel_id=1, source_target_pairs={{0,1},{1,0},{2,3},{3,2},{4,5},{5,4},{6,7},{7,6},{8,9},{9,8},{10,11... | collective-permute-start | bytes 36872 | tf_op jit(solution)/shard_map/ppermute | solution.py:455
